TPU v7x, 32 devices: a whole 2x2x4 slice. The times are simulated.
32 devices in a mesh: dp: 8 (over z, x), seq: 4 (over y, core).
Axes of the slice: x: 2, y: 2, z: 4, core: 2. Of those that a mesh axis runs over, the one named last changes fastest.
Arguments:
- text_embed: bfloat16 [24, 512, 768], P('dp', 'seq'), may hold values from -6 to 6
- region_feature: bfloat16 [24, 512, 768], P('dp', 'seq')
- token_mask: int32 [24, 512], P('dp', 'seq'), may hold values from 0 to 1, as said below
- segment_mask: int32 [24, 512], P('dp', 'seq'), may hold values from 0 to 1, as said below
- mask_vector: float32 [768], replicated, may hold values from -6 to 6
- batch_gain: float32 [768], replicated, may hold values from 0.5 to 1.5
- batch_shift: float32 [768], replicated, may hold values from -3 to 3
- query_weight: bfloat16 [768, 768], P('seq'), may hold values from -0.21875 to 0.21875
- query_bias: float32 [768], replicated, may hold values from -3 to 3
- key_weight: bfloat16 [768, 768], P('seq'), may hold values from -0.21875 to 0.21875
- value_weight: bfloat16 [768, 768], P('seq'), may hold values from -0.21875 to 0.21875
- value_bias: float32 [768], replicated, may hold values from -3 to 3
- output_weight: bfloat16 [768, 768], P('seq'), may hold values from -0.875 to 0.875
- output_bias: float32 [768], replicated, may hold values from -3 to 3
- first_gain: float32 [768], replicated, may hold values from 0.5 to 1.5
- first_shift: float32 [768], replicated, may hold values from -3 to 3
- up_weight: bfloat16 [768, 3072], P('seq'), may hold values from -0.21875 to 0.21875
- up_bias: float32 [3072], replicated, may hold values from -3 to 3
- down_weight: bfloat16 [3072, 768], P('seq'), may hold values from -0.109375 to 0.109375
- down_bias: float32 [768], replicated, may hold values from -3 to 3
- second_gain: float32 [768], replicated, may hold values from 0.5 to 1.5
- second_shift: float32 [768], replicated, may hold values from -3 to 3
- cotangent: bfloat16 [24, 512, 768], P('dp', 'seq'), may hold values from -6 to 6
Outputs:
- layer_output: bfloat16 [24, 512, 768], P('dp', 'seq')
- text_gradient: bfloat16 [24, 512, 768], P('dp', 'seq')
- region_gradient: bfloat16 [24, 512, 768], P('dp', 'seq')
- mask_vector_gradient: float32 [768], replicated
- batch_gain_gradient: float32 [768], replicated
- batch_shift_gradient: float32 [768], replicated
- query_weight_gradient: float32 [768, 768], P('seq')
- query_bias_gradient: float32 [768], replicated
- key_weight_gradient: float32 [768, 768], P('seq')
- value_weight_gradient: float32 [768, 768], P('seq')
- value_bias_gradient: float32 [768], replicated
- output_weight_gradient: float32 [768, 768], P('seq')
- output_bias_gradient: float32 [768], replicated
- first_gain_gradient: float32 [768], replicated
- first_shift_gradient: float32 [768], replicated
- up_weight_gradient: float32 [768, 3072], P('seq')
- up_bias_gradient: float32 [3072], replicated
- down_weight_gradient: float32 [3072, 768], P('seq')
- down_bias_gradient: float32 [768], replicated
- second_gain_gradient: float32 [768], replicated
- second_shift_gradient: float32 [768], replicated
Inputs may be any that keep to these rules, and one draw needn't show every extreme that they name: `token_mask`: 1 marks a masked token position; the share differs from document to document. `segment_mask`: 1 marks a position whose segment box is replaced; the share differs from document to document.
All inputs are finite; a program needn't handle non-finite values.
Results may differ from a plain program's by a relative error of at most 0.024.
The roundings to bfloat16 on the way count: a program that leaves them out, or rounds other values in their place, can miss the bound.
Values may be sent and summed in bfloat16 or wider, within the bound.
No kernel may reach another device: no remote copies, remote signals or barrier semaphores. Data moves between devices by JAX's collectives and lax.ppermute only.
A program may use at most 192 MiB of HBM per device.

v0:
```python
import functools
import math

import jax
import jax.numpy as jnp
from jax import lax
from jax.experimental import pallas as pl
from jax.experimental.pallas import tpu as pltpu
from jax.sharding import PartitionSpec as P

HEAD_DIM = 64
EPS_NORM = 1e-12
EPS_BATCH = 1e-05
F32 = jnp.float32
BF16 = jnp.bfloat16
GELU_IN = math.sqrt(2.0 / math.pi)
GELU_CUBE = 0.044715
PIECES = 8
DOWN_ORDER = (1, 2, 4)
UP_ORDER = (2, 1, 4)
HEAD_ORDER = (1, 2, 4)


def swap(x, axis, by):
    return lax.ppermute(x, axis, [(i, i ^ by) for i in range(lax.axis_size(axis))])


def bits(axis):
    found, by = [], 1
    while by < lax.axis_size(axis):
        found.append(by)
        by *= 2
    return found


def sum_all(x):
    for axis in ("seq", "dp"):
        for by in bits(axis):
            x = x + swap(x, axis, by)
    return x


def nn(a, b):
    return jnp.dot(a, b, preferred_element_type=F32)


def tn(a, b):
    return lax.dot_general(a, b, (((0,), (0,)), ((), ())), preferred_element_type=F32)


def nt(a, b):
    return lax.dot_general(a, b, (((1,), (1,)), ((), ())), preferred_element_type=F32)


def norm_parts(x):
    centred = x - jnp.mean(x, axis=-1, keepdims=True)
    scale = lax.rsqrt(jnp.mean(centred * centred, axis=-1, keepdims=True) + EPS_NORM)
    return centred * scale, scale


def norm_back(grad, unit, scale, gain):
    g = grad * gain
    return scale * (
        g
        - jnp.mean(g, axis=-1, keepdims=True)
        - unit * jnp.mean(g * unit, axis=-1, keepdims=True)
    )


def gather_rows(x):
    two = swap(x, "seq", 2)
    one, three = swap(x, "seq", 1), swap(two, "seq", 1)
    return [x, one, two, three]


def gather_weight(halves, dp):
    near = swap(lax.dynamic_index_in_dim(halves, dp % 2, 0, keepdims=False), "seq", 2)
    far = swap(near, "dp", 1)
    return [halves, near, far, swap(halves, "seq", 1), swap(near, "seq", 1), swap(far, "seq", 1)]


def scatter_pairs(keep, give):
    got = swap(give, "seq", 1)
    pass_on = (keep[1].astype(F32) + got[1].astype(F32)).astype(BF16)
    own = keep[0].astype(F32) + got[0].astype(F32)
    return own + swap(pass_on, "seq", 2).astype(F32)


def exchange_blocks(blocks):
    return [blocks[0]] + [swap(blocks[r], "seq", r) for r in (1, 2, 3)]


VMEM_BYTES = 56 * 1024 * 1024


def params(*semantics):
    return pltpu.CompilerParams(vmem_limit_bytes=VMEM_BYTES)


def whole_spec():
    return pl.BlockSpec(memory_space=pltpu.VMEM)


def attend_kernel(seq_ref, *refs):
    x_refs, w_refs, bias_ref = refs[:4], refs[4:8], refs[8]
    q_ref, k_ref, v_ref, wc_ref, out_refs = refs[9], refs[10], refs[11], refs[12], refs[13:17]
    part = w_refs[0].shape[1]
    span = x_refs[0].shape[1]

    @pl.when(pl.program_id(0) == 0)
    def _():
        for r in range(4):
            at = pl.multiple_of((seq_ref[0] ^ r) * part, part)
            wc_ref[:, pl.ds(at, part), :] = w_refs[r][...]

    x = jnp.concatenate([ref[0] for ref in x_refs], axis=0)
    for i, ref in enumerate((q_ref, k_ref, v_ref)):
        ref[0] = (nn(x, wc_ref[i]) + bias_ref[i]).astype(BF16)
    q, k, v = q_ref[0], k_ref[0], v_ref[0]
    lane = lax.broadcasted_iota(jnp.int32, (1, part), 1) // HEAD_DIM
    for h in range(part // HEAD_DIM):
        pick = jnp.where(lane == h, 1.0 / math.sqrt(HEAD_DIM), 0.0).astype(BF16)
        scores = nt(k, q * pick)
        raised = jnp.exp(scores - jnp.max(scores, axis=0, keepdims=True))
        chances = (raised * (1.0 / jnp.sum(raised, axis=0, keepdims=True))).astype(BF16)
        attended = tn(v, chances)[h * HEAD_DIM : (h + 1) * HEAD_DIM].astype(BF16)
        for r in range(4):
            out_refs[r][h * HEAD_DIM : (h + 1) * HEAD_DIM, :] = attended[:, r * span : (r + 1) * span]


def attend(seq, x_blocks, w_blocks, bias):
    documents, span, features = x_blocks[0].shape
    part = w_blocks[0].shape[1]
    length = 4 * span
    flops = documents * (2 * length * features * 3 * part + 4 * length * length * part)
    per_doc = pl.BlockSpec((1, length, part), lambda d: (d, 0, 0))
    return pl.pallas_call(
        attend_kernel,
        grid=(documents,),
        in_specs=[pl.BlockSpec(memory_space=pltpu.SMEM)]
        + [pl.BlockSpec((1, span, features), lambda d: (d, 0, 0))] * 4
        + [pl.BlockSpec((3, part, part), lambda d: (0, 0, 0))] * 4
        + [pl.BlockSpec((3, 1, part), lambda d: (0, 0, 0))],
        out_specs=[per_doc] * 3
        + [pl.BlockSpec((3, features, part), lambda d: (0, 0, 0))]
        + [pl.BlockSpec((part, span), lambda d: (0, d))] * 4,
        out_shape=[jax.ShapeDtypeStruct((documents, length, part), BF16)] * 3
        + [jax.ShapeDtypeStruct((3, features, part), BF16)]
        + [jax.ShapeDtypeStruct((part, documents * span), BF16)] * 4,
        compiler_params=params(),
        cost_estimate=pl.CostEstimate(
            flops=flops, bytes_accessed=8 * 1024 * 1024, transcendentals=documents * length * length * 3
        ),
        name="attend",
    )(seq, *x_blocks, *w_blocks, bias)


def attend_back_kernel(place_ref, *refs):
    g_refs, x_refs = refs[:4], refs[4:8]
    q_ref, k_ref, v_ref, wc_ref = refs[8:12]
    keep_ref, give_ref, dw_ref, sums_ref, acc_ref = refs[12:]
    part = q_ref.shape[2]
    span = x_refs[0].shape[1]
    first = pl.program_id(0) == 0
    q, k, v = q_ref[0], k_ref[0], v_ref[0]
    g = jnp.concatenate([ref[...] for ref in g_refs], axis=1)
    lane = lax.broadcasted_iota(jnp.int32, (1, part), 1) // HEAD_DIM
    scale = 1.0 / math.sqrt(HEAD_DIM)
    dq = dk = dv = None
    for h in range(part // HEAD_DIM):
        on = lane == h
        pick = jnp.where(on, scale, 0.0).astype(BF16)
        mask = jnp.where(on, 1.0, 0.0)
        scores = nt(k, q * pick)
        raised = jnp.exp(scores - jnp.max(scores, axis=0, keepdims=True))
        chances = raised * (1.0 / jnp.sum(raised, axis=0, keepdims=True))
        grad = nn(v * mask.astype(BF16), g)
        both = chances * grad
        grad = (both - chances * jnp.sum(both, axis=0, keepdims=True)).astype(BF16)
        part_v = nt(chances.astype(BF16), g) * mask
        part_k = nn(grad, q) * (mask * scale)
        part_q = tn(grad, k) * (mask * scale)
        dq = part_q if dq is None else dq + part_q
        dk = part_k if dk is None else dk + part_k
        dv = part_v if dv is None else dv + part_v
    low = [t.astype(BF16) for t in (dq, dk, dv)]
    sums = jnp.concatenate(
        [jnp.sum(low[i].astype(F32), axis=0, keepdims=True) for i in (0, 2)], axis=0
    )
    x = jnp.concatenate([ref[0] for ref in x_refs], axis=0)
    x_t = x.T
    inner = nt(low[0], wc_ref[0]) + nt(low[1], wc_ref[1]) + nt(low[2], wc_ref[2])
    inner = inner.astype(BF16)
    for r in range(4):
        (give_ref if r % 2 else keep_ref)[r // 2, 0] = inner[r * span : (r + 1) * span]

    @pl.when(first)
    def _():
        sums_ref[...] = sums
        for i in range(3):
            acc_ref[i] = nn(x_t, low[i])

    @pl.when(jnp.logical_not(first))
    def _():
        sums_ref[...] += sums
        for i in range(3):
            acc_ref[i] += nn(x_t, low[i])

    @pl.when(pl.program_id(0) == pl.num_programs(0) - 1)
    def _():
        tall = part // PIECES
        for p in range(PIECES):
            spot = place(p ^ (place_ref[1] % PIECES), HEAD_ORDER)
            for block in range(4):
                at = block * part + p * tall
                for i in range(3):
                    dw_ref[spot, place_ref[0] ^ block, :, i * part : (i + 1) * part] = acc_ref[
                        i, at : at + tall, :
                    ].astype(BF16)


def attend_back(place_word, g_blocks, x_blocks, q, k, v, wc):
    documents, span, features = x_blocks[0].shape
    part = q.shape[2]
    length = 4 * span
    flops = documents * (4 * length * features * 3 * part + 10 * length * length * part)
    per_doc = pl.BlockSpec((1, length, part), lambda d: (d, 0, 0))
    pair = pl.BlockSpec((2, 1, span, features), lambda d: (0, d, 0, 0))
    return pl.pallas_call(
        attend_back_kernel,
        grid=(documents,),
        in_specs=[pl.BlockSpec(memory_space=pltpu.SMEM)]
        + [pl.BlockSpec((part, span), lambda d: (0, d))] * 4
        + [pl.BlockSpec((1, span, features), lambda d: (d, 0, 0))] * 4
        + [per_doc] * 3
        + [pl.BlockSpec((3, features, part), lambda d: (0, 0, 0))],
        out_specs=[
            pair,
            pair,
            pl.BlockSpec((PIECES, 4, part // PIECES, 3 * part), lambda d: (0, 0, 0, 0)),
            pl.BlockSpec((2, part), lambda d: (0, 0)),
        ],
        out_shape=[jax.ShapeDtypeStruct((2, documents, span, features), BF16)] * 2
        + [
            jax.ShapeDtypeStruct((PIECES, 4, part // PIECES, 3 * part), BF16),
            jax.ShapeDtypeStruct((2, part), F32),
        ],
        scratch_shapes=[pltpu.VMEM((3, features, part), F32)],
        compiler_params=params(),
        cost_estimate=pl.CostEstimate(
            flops=flops, bytes_accessed=12 * 1024 * 1024, transcendentals=documents * length * length * 3
        ),
        name="attend_back",
    )(place_word, *g_blocks, *x_blocks, q, k, v, wc)


def place(index, order):
    at = 0
    for by in order:
        at = 2 * at + (index // by) % 2
    return at


def gelu_parts(x):
    bend = jnp.tanh(GELU_IN * x * (1.0 + GELU_CUBE * x * x))
    return 0.5 * (1.0 + bend), bend


def middle_kernel(place_ref, *refs):
    (a_refs, in_ref, cot_ref, vec_ref, upb_ref), refs = (refs[:4], *refs[4:8]), refs[8:]
    pieces, refs = refs[:12], refs[12:]
    out_ref, res_ref, g_refs, sums_ref, upsum_ref = refs[0], refs[1], refs[2:6], refs[6], refs[7]
    down_out, up_out = refs[8:11], refs[11:14]
    wo, up, down, low, low_t, act, pre, acc, tmp, sems = refs[14:]
    seq, dp = place_ref[0], place_ref[1]
    bit = dp % 2
    part, features = wo.shape[1], wo.shape[2]
    half = part // 2
    count = PIECES

    copies = []

    def bring(source, target):
        copies.append(pltpu.make_async_copy(source, target, sems.at[len(copies)]))

    for group, first in ((0, True), (6, False)):
        own, near, far, one, near_one, far_one = pieces[group : group + 6]
        parts = [(own.at[h], 0, h) for h in range(2)] + [(one.at[h], 1, h) for h in range(2)]
        parts += [(near, 2, bit), (far, 2, 1 - bit), (near_one, 3, bit), (far_one, 3, 1 - bit)]
        for source, r, h in parts:
            if first:
                bring(source.at[pl.ds(0, half)], wo.at[r, pl.ds(pl.multiple_of(h * half, half), half)])
                at = pl.multiple_of((seq ^ r) * part + h * half, half)
                for j in range(4):
                    bring(source.at[pl.ds(half * (j + 1), half)], up.at[j, pl.ds(at, half)])
            else:
                size = 2 * part
                bring(source, down.at[seq ^ r, pl.ds(pl.multiple_of(h * size, size), size)])
    for copy in copies:
        copy.start()
    out_bias, gain1, shift1, down_bias, gain2, shift2 = (vec_ref[i : i + 1, :] for i in range(6))
    for copy in copies[:-8]:
        copy.wait()

    residual = in_ref[...] + out_bias
    for r in range(4):
        residual += tn(a_refs[r][...], wo[r])
    unit1, scale1 = norm_parts(residual)
    first_out = unit1 * gain1 + shift1
    low[...] = first_out.astype(BF16)
    low_t[...] = first_out.T.astype(BF16)
    acc[...] = first_out + down_bias
    for copy in copies[-8:]:
        copy.wait()

    def forward(j, carry):
        x = nn(low[...], up[j]) + upb_ref[pl.ds(j, 1), :]
        pre[j] = x
        gate, _ = gelu_parts(x)
        a = (x * gate).astype(BF16)
        act[j] = a
        acc[...] += nn(a, down[j])
        return carry

    lax.fori_loop(0, 4, forward, 0)
    unit2, scale2 = norm_parts(acc[...])
    out_ref[...] = (unit2 * gain2 + shift2).astype(BF16)
    incoming = cot_ref[...].astype(F32)
    grad_second = norm_back(incoming, unit2, scale2, gain2)
    grad_down = grad_second.astype(BF16)
    sums_ref[0:1, :] = jnp.sum(incoming * unit2, axis=0, keepdims=True)
    sums_ref[1:2, :] = jnp.sum(incoming, axis=0, keepdims=True)
    sums_ref[2:3, :] = jnp.sum(grad_down.astype(F32), axis=0, keepdims=True)
    acc[...] = grad_second

    def give(outs, r, store):
        for i in range(4):

            @pl.when(r == i)
            def _(i=i):
                store(outs[2], (i // 2,)) if i % 2 else store(outs[i // 2], ())

    size = features // count

    def backward(j, carry):
        a = act[j]
        tmp[...] = tn(a, grad_down).astype(BF16)

        def store_down(ref, lead):
            for p in range(count):
                ref[(*lead, place(p ^ (dp % count), DOWN_ORDER))] = tmp[p * size : (p + 1) * size, :]

        give(down_out, seq ^ j, store_down)
        x = pre[j]
        gate, bend = gelu_parts(x)
        slope = gate + 0.5 * x * (1.0 - bend * bend) * (GELU_IN * (1.0 + 3.0 * GELU_CUBE * x * x))
        grad_act = nt(grad_down, down[j]).astype(BF16).astype(F32)
        grad_up = (grad_act * slope).astype(BF16)
        upsum_ref[pl.ds(j, 1), :] = jnp.sum(grad_up.astype(F32), axis=0, keepdims=True)
        acc[...] += nt(grad_up, up[j])
        tmp[...] = nn(low_t[...], grad_up).astype(BF16)
        for r in range(4):
            for h in range(2):
                at = pl.multiple_of((seq ^ r) * part + h * half, half)
                ref, lead = (up_out[2], (r // 2,)) if r % 2 else (up_out[r // 2], ())
                spot = place((2 * j + h) ^ (dp % count), UP_ORDER)
                ref[(*lead, spot, pl.ds(0, half))] = tmp[pl.ds(at, half), :]
        return carry

    lax.fori_loop(0, 4, backward, 0)
    grad_first = acc[...]
    grad_residual = norm_back(grad_first, unit1, scale1, gain1)
    res_ref[...] = grad_residual
    grad_out = grad_residual.astype(BF16)
    sums_ref[3:4, :] = jnp.sum(grad_first * unit1, axis=0, keepdims=True)
    sums_ref[4:5, :] = jnp.sum(grad_first, axis=0, keepdims=True)
    sums_ref[5:6, :] = jnp.sum(grad_out.astype(F32), axis=0, keepdims=True)
    for r in range(4):
        g_refs[r][...] = nt(wo[r], grad_out).astype(BF16)
        tall = part // count
        value = nn(a_refs[r][...], grad_out)
        ref, lead = (up_out[2], (r // 2,)) if r % 2 else (up_out[r // 2], ())
        for p in range(count):
            spot = place(p ^ (dp % count), UP_ORDER)
            ref[(*lead, spot, pl.ds(half, tall))] = value[p * tall : (p + 1) * tall].astype(BF16)


def middle(place_word, attended, embedded, cotangent, vectors, up_bias, pieces):
    rows, features = embedded.shape
    part = attended[0].shape[0]
    size = features // PIECES
    tall = size + part // PIECES
    kept = jax.ShapeDtypeStruct((PIECES, size, features), BF16)
    given = jax.ShapeDtypeStruct((2, PIECES, size, features), BF16)
    kept_up = jax.ShapeDtypeStruct((PIECES, tall, features), BF16)
    given_up = jax.ShapeDtypeStruct((2, PIECES, tall, features), BF16)
    hidden = 4 * features
    return pl.pallas_call(
        middle_kernel,
        in_specs=[pl.BlockSpec(memory_space=pltpu.SMEM)]
        + [whole_spec()] * 8
        + [pl.BlockSpec(memory_space=pl.ANY)] * 12,
        out_specs=[whole_spec()] * 14,
        out_shape=[
            jax.ShapeDtypeStruct((rows, features), BF16),
            jax.ShapeDtypeStruct((rows, features), F32),
        ]
        + [jax.ShapeDtypeStruct((part, rows), BF16)] * 4
        + [jax.ShapeDtypeStruct((6, features), F32), jax.ShapeDtypeStruct((4, features), F32)]
        + [kept, kept, given, kept_up, kept_up, given_up],
        scratch_shapes=[
            pltpu.VMEM((4, part, features), BF16),
            pltpu.VMEM((4, features, features), BF16),
            pltpu.VMEM((4, features, features), BF16),
            pltpu.VMEM((rows, features), BF16),
            pltpu.VMEM((features, rows), BF16),
            pltpu.VMEM((4, rows, features), BF16),
            pltpu.VMEM((4, rows, features), F32),
            pltpu.VMEM((rows, features), F32),
            pltpu.VMEM((features, features), BF16),
            pltpu.SemaphoreType.DMA((48,)),
        ],
        compiler_params=params(),
        cost_estimate=pl.CostEstimate(
            flops=12 * rows * features * hidden,
            bytes_accessed=30 * 1024 * 1024,
            transcendentals=2 * rows * hidden,
        ),
        name="middle",
    )(place_word, *attended, embedded, cotangent, vectors, up_bias, *pieces)


def settle_kernel(place_ref, *refs, order, store):
    held, outs = refs[:2], refs[2:]
    seq, dp = place_ref[0], place_ref[1] % PIECES
    half = PIECES // 2
    for index in range(PIECES):
        spot = place(index, order)
        store(outs, held[spot // half].at[spot % half], index ^ dp, seq)


def store_down(outs, piece, p, seq):
    size = piece.shape[0]
    outs[0][pl.ds(pl.multiple_of(p * size, size), size), :] = piece[...].astype(F32)


def store_up(outs, piece, p, seq):
    size = outs[0].shape[0] // 2
    wide = piece.shape[1]
    tall = piece.shape[0] - size
    row, column = pl.multiple_of((p % 2) * size, size), pl.multiple_of((p // 2) * wide, wide)
    outs[0][pl.ds(row, size), pl.ds(column, wide)] = piece[:size].astype(F32)
    outs[1][pl.ds(pl.multiple_of(p * tall, 8), tall), :] = piece[size:].astype(F32)


def store_heads(outs, piece, p, seq):
    tall, part = piece.shape[1], piece.shape[2] // 3
    for c in range(4):
        block = piece[seq ^ c].astype(F32)
        for i in range(3):
            outs[i][pl.ds(pl.multiple_of(p * tall, 8), tall), c * part : (c + 1) * part] = block[
                :, i * part : (i + 1) * part
            ]


def settle(place_word, held, order, store, shapes):
    return pl.pallas_call(
        functools.partial(settle_kernel, order=order, store=store),
        in_specs=[pl.BlockSpec(memory_space=pltpu.SMEM)] + [whole_spec()] * 2,
        out_specs=[whole_spec()] * len(shapes),
        out_shape=[jax.ShapeDtypeStruct(shape, F32) for shape in shapes],
        compiler_params=params(),
        cost_estimate=pl.CostEstimate(flops=0, bytes_accessed=4 * 1024 * 1024, transcendentals=0),
        name="settle",
    )(place_word, *held)


def reduce_dp(x, orders):
    for by in orders:
        half = x.shape[0] // 2
        x = x[:half].astype(F32) + swap(x[half:].astype(BF16), "dp", by).astype(F32)
    return x


def reduce_rest(x):
    for by in bits("dp")[3:]:
        x = x.astype(F32) + swap(x.astype(BF16), "dp", by).astype(F32)
    return x.astype(BF16)


def spread_dp(x, order):
    for by in reversed(order[1:]):
        x = jnp.concatenate([x, swap(x, "dp", by)])
    return x, swap(x, "dp", order[0])


def body(
    text_embed,
    region_feature,
    token_mask,
    segment_mask,
    mask_vector,
    batch_gain,
    batch_shift,
    query_weight,
    query_bias,
    key_weight,
    value_weight,
    value_bias,
    output_weight,
    output_bias,
    first_gain,
    first_shift,
    up_weight,
    up_bias,
    down_weight,
    down_bias,
    second_gain,
    second_shift,
    cotangent,
):
    documents, span, features = text_embed.shape
    rows = documents * span
    seq, dp = lax.axis_index("seq"), lax.axis_index("dp")
    group = lax.axis_size("seq")
    population = rows * lax.axis_size("dp") * group
    score_scale = 1.0 / math.sqrt(HEAD_DIM)
    part = features // group
    heads = part // HEAD_DIM

    region = region_feature.astype(F32).reshape(rows, features)
    sums = sum_all(jnp.stack([jnp.sum(region, axis=0), jnp.sum(region * region, axis=0)]))
    average = sums[0] / population
    inverse = lax.rsqrt(sums[1] / population - average * average + EPS_BATCH)

    cut = (
        jnp.stack([query_weight, key_weight, value_weight])
        .reshape(3, part, group, part)
        .transpose(2, 0, 1, 3)
    )
    head_blocks = exchange_blocks(
        [lax.dynamic_index_in_dim(cut, seq ^ r, 0, keepdims=False) for r in range(group)]
    )
    bias3 = jnp.stack([query_bias, jnp.zeros_like(query_bias), value_bias]).reshape(3, group, part)
    head_bias = lax.dynamic_slice_in_dim(bias3, seq, 1, 1)

    half = part // 2
    early = jnp.concatenate(
        [
            output_weight.reshape(2, half, features),
            up_weight.reshape(2, half, group, features).transpose(0, 2, 1, 3).reshape(2, group * half, features),
        ],
        axis=1,
    )
    pieces = gather_weight(early, dp) + gather_weight(down_weight.reshape(2, -1, features), dp)

    standard = (region - average) * inverse
    token_hit = token_mask.astype(F32).reshape(rows, 1)
    segment_keep = 1.0 - segment_mask.astype(F32).reshape(rows, 1)
    embedded = (
        text_embed.astype(F32).reshape(rows, features) * (1.0 - token_hit)
        + token_hit * mask_vector
        + segment_keep * (standard * batch_gain + batch_shift)
    )
    low_in = embedded.astype(BF16).reshape(documents, span, features)

    place_word = jnp.stack([seq, dp]).astype(jnp.int32)
    x_blocks = gather_rows(low_in)
    q, k, v, head_weight, *attended = attend(place_word, x_blocks, head_blocks, head_bias)
    attn_blocks = exchange_blocks(attended)

    vectors = jnp.stack([output_bias, first_gain, first_shift, down_bias, second_gain, second_shift])
    layer_output, grad_residual, *rest = middle(
        place_word,
        attn_blocks,
        embedded,
        cotangent.reshape(rows, features),
        vectors,
        up_bias.reshape(group, features),
        pieces,
    )
    grad_attn, (middle_sums, up_sums) = rest[:4], rest[4:6]
    down_keep, down_far, down_give, up_keep, up_far, up_give = rest[6:]

    got = swap(down_give, "seq", 1)
    pass_on = (down_far.astype(F32) + got[1].astype(F32)).astype(BF16)
    own = down_keep.astype(F32) + got[0].astype(F32) + swap(pass_on, "seq", 2).astype(F32)
    own = reduce_rest(reduce_dp(own, DOWN_ORDER))
    (total_down,) = settle(
        place_word, spread_dp(own, DOWN_ORDER), DOWN_ORDER, store_down, [down_weight.shape]
    )

    got = swap(up_give, "seq", 1)
    both = jnp.stack(
        [up_keep.astype(F32) + got[0].astype(F32), up_far.astype(F32) + got[1].astype(F32)], axis=1
    )
    both = reduce_dp(both, UP_ORDER[:1])
    own = both[:, 0] + swap(both[:, 1].astype(BF16), "seq", 2).astype(F32)
    own = reduce_rest(reduce_dp(own, UP_ORDER[1:]))
    total_up, total_out = settle(
        place_word, spread_dp(own, UP_ORDER), UP_ORDER, store_up, [up_weight.shape, output_weight.shape]
    )

    g_blocks = exchange_blocks(grad_attn)
    keep, give, term_heads, head_sums = attend_back(place_word, g_blocks, x_blocks, q, k, v, head_weight)
    query_sums, value_sums = head_sums[0], head_sums[1]
    inner = scatter_pairs(keep, give).reshape(rows, features)
    own = reduce_rest(reduce_dp(term_heads, HEAD_ORDER))
    own = jnp.stack(exchange_blocks([own[:, r] for r in range(group)]), axis=1)
    total_query, total_key, total_value = settle(
        place_word, spread_dp(own, HEAD_ORDER), HEAD_ORDER, store_heads, [query_weight.shape] * 3
    )

    grad_embedded = grad_residual + inner
    text_gradient = (grad_embedded * (1.0 - token_hit)).astype(BF16)
    grad_normed = grad_embedded * segment_keep

    def widen(x):
        return lax.dynamic_update_slice_in_dim(jnp.zeros((features,), F32), x, seq * part, 0)

    sums = sum_all(
        jnp.concatenate(
            [
                jnp.stack(
                    [
                        jnp.sum(grad_normed * standard, axis=0),
                        jnp.sum(grad_normed, axis=0),
                        jnp.sum(grad_embedded * token_hit, axis=0),
                        widen(query_sums),
                        widen(value_sums),
                    ]
                ),
                middle_sums,
                up_sums,
            ]
        )
    )
    (
        sum_gain,
        sum_shift,
        sum_mask,
        sum_query_bias,
        sum_value_bias,
        sum_second_gain,
        sum_second_shift,
        sum_down_bias,
        sum_first_gain,
        sum_first_shift,
        sum_output_bias,
    ) = sums[:11]
    sum_up_bias = sums[11:].reshape(-1)

    region_gradient = (
        batch_gain
        * inverse
        * (grad_normed - sum_shift / population - standard * (sum_gain / population))
    ).astype(BF16)
    shape = (documents, span, features)
    return (
        layer_output.reshape(shape),
        text_gradient.reshape(shape),
        region_gradient.reshape(shape),
        sum_mask,
        sum_gain,
        sum_shift,
        total_query,
        sum_query_bias,
        total_key,
        total_value,
        sum_value_bias,
        total_out,
        sum_output_bias,
        sum_first_gain,
        sum_first_shift,
        total_up,
        sum_up_bias,
        total_down,
        sum_down_bias,
        sum_second_gain,
        sum_second_shift,
    )


def solution(mesh):
    rows, weight, copied = P("dp", "seq", None), P("seq", None), P()
    mask = P("dp", "seq")
    in_specs = (
        (rows, rows, mask, mask, copied, copied, copied)
        + (weight, copied, weight, weight, copied, weight, copied, copied, copied)
        + (weight, copied, weight, copied, copied, copied, rows)
    )
    out_specs = (
        (rows, rows, rows, copied, copied, copied)
        + (weight, copied, weight, weight, copied, weight, copied, copied, copied)
        + (weight, copied, weight, copied, copied, copied)
    )
    return jax.shard_map(body, mesh=mesh, in_specs=in_specs, out_specs=out_specs, check_vma=False)
```

profile of v0, /device:TPU:0, one launch (start us, length us, event | category | flops | bytes accessed | tf_op | source)
XLA Modules:
  0.0 349.5 jit_solution(9468224207673808765)
XLA Ops:
  5.7 2.6 collective-permute-start.10
  14.3 18.0 %collective-permute-done.1 = f32[2,768]{1,0:T(2,128)S(1)} collective-permute-done((f32[2,768]{1,0:T(2,128)S(1)}, f32[2,768]{1,0:T(2,128)S(1)}, u32[]{:S(2)}, u32[]{:S(2)}) %collective-permute-start.1) | collective-permute-done | bytes 6176 | tf_op jit(solution)/shard_map/ppermute | solution.py:25
  32.3 2.1 collective-permute-start.2
  36.0 2.1 collective-permute-start.3
  39.7 3.0 collective-permute-start.4
  48.9 14.7 %collective-permute-done.9.refs_6_ = bf16[3,192,192]{2,1,0:T(8,128)(2,1)S(1)} collective-permute-done((bf16[3,192,192]{2,1,0:T(8,128)(2,1)S(1)}, bf16[3,192,192]{2,1,0:T(8,128)(2,1)S(1)}, u32[]{:S(2)}, u32[]{:S(2)}) %collective-permute-start.9) | collective-permute-done | bytes 221216 | tf_op jit(solution)/shard_map/ppermute | solution.py:25
  71.7 11.2 %collective-permute-done.15.refs_10_ = bf16[480,768]{1,0:T(8,128)(2,1)} collective-permute-done((bf16[480,768]{1,0:T(8,128)(2,1)}, bf16[480,768]{1,0:T(8,128)(2,1)}, u32[]{:S(2)}, u32[]{:S(2)}) %collective-permute-start.15) | collective-permute-done | bytes 737312 | tf_op jit(solution)/shard_map/ppermute | solution.py:25
  83.0 10.6 %attend.1 = (bf16[3,512,192]{2,1,0:T(8,128)(2,1)}, bf16[3,512,192]{2,1,0:T(8,128)(2,1)}, bf16[3,512,192]{2,1,0:T(8,128)(2,1)}, bf16[3,768,192]{2,1,0:T(8,128)(2,...) custom-call(s32[2]{0:T(128)} %pad_add_fusion.seq_ref.place_ref, ...), custom_call_target="tpu_custom_call" | custom-call | flops 1962934272 | bytes 8388608 | tf_op jit(solution)/shard_map/attend/pallas_call | solution.py:137
  97.3 4.7 %collective-permute-done.12.refs_2_ = bf16[192,384]{1,0:T(8,128)(2,1)S(1)} collective-permute-done((bf16[192,384]{1,0:T(8,128)(2,1)}, bf16[192,384]{1,0:T(8,128)(2,1)S(1)}, u32[]{:S(2)}, u32[]{:S(2)}) %collective-permute-start.12) | collective-permute-done | bytes 147488 | tf_op jit(solution)/shard_map/ppermute | solution.py:25
  104.4 3.8 %collective-permute-done.13.refs_3_ = bf16[192,384]{1,0:T(8,128)(2,1)S(1)} collective-permute-done((bf16[192,384]{1,0:T(8,128)(2,1)}, bf16[192,384]{1,0:T(8,128)(2,1)S(1)}, u32[]{:S(2)}, u32[]{:S(2)}) %collective-permute-start.13) | collective-permute-done | bytes 147488 | tf_op jit(solution)/shard_map/ppermute | solution.py:25
  109.6 32.4 %middle.1 = (bf16[384,768]{1,0:T(8,128)(2,1)}, f32[384,768]{1,0:T(8,128)}, bf16[192,384]{1,0:T(8,128)(2,1)}, bf16[192,384]{1,0:T(8,128)(2,1)}, bf16[192,384]{1,0...) custom-call(s32[2]{0:T(128)} %pad_add_fusion.seq_ref.place_ref, ...), custom_call_target="tpu_custom_call" | custom-call | flops 10871635968 | bytes 31457280 | tf_op jit(solution)/shard_map/middle/pallas_call | solution.py:398
  144.5 6.8 %collective-permute-done.24.refs_1_ = bf16[192,384]{1,0:T(8,128)(2,1)S(1)} collective-permute-done((bf16[192,384]{1,0:T(8,128)(2,1)}, bf16[192,384]{1,0:T(8,128)(2,1)S(1)}, u32[]{:S(2)}, u32[]{:S(2)}) %collective-permute-start.24) | collective-permute-done | bytes 147488 | tf_op jit(solution)/shard_map/ppermute | solution.py:25
  152.5 17.5 %attend_back.1 = (bf16[2,3,128,768]{3,2,1,0:T(8,128)(2,1)}, bf16[2,3,128,768]{3,2,1,0:T(8,128)(2,1)}, bf16[8,4,24,576]{3,2,1,0:T(8,128)(2,1)}, f32[2,192]{1,0:T(2,128)}) custom-call(s32[2]{0:T(128)} %pad_add_fusion.seq_ref.place_ref, bf16[192,384]{1,0:T(8,128)(2,1)} %get-tuple-element.58.refs_0_, bf16[192,384]{1,0:T(8,128)(2,1)} %copy-done.51, ...), custom_call_target="tpu_custom_call" | custom-call | flops 4227858432 | bytes 12582912 | tf_op jit(solution)/shard_map/attend_back/pallas_call | solution.py:229
  172.9 11.7 %collective-permute-done.34 = bf16[4,4,24,576]{3,2,1,0:T(8,128)(2,1)S(1)} collective-permute-done((bf16[4,4,24,576]{3,2,1,0:T(8,128)(2,1)S(1)}, bf16[4,4,24,576]{3,2,1,0:T(8,128)(2,1)S(1)}, u32[]{:S(2)}, u32[]{:S(2)}) %collective-permute-start.34) | collective-permute-done | bytes 442400 | tf_op jit(solution)/shard_map/ppermute | solution.py:25
  193.2 2.7 collective-permute-start.36
  195.9 30.8 %collective-permute-done.36 = bf16[1,4,24,576]{3,2,1,0:T(8,128)(2,1)S(1)} collective-permute-done((bf16[1,4,24,576]{3,2,1,0:T(8,128)(2,1)S(1)}, bf16[1,4,24,576]{3,2,1,0:T(8,128)(2,1)S(1)}, u32[]{:S(2)}, u32[]{:S(2)}) %collective-permute-start.36) | collective-permute-done | bytes 110624 | tf_op jit(solution)/shard_map/ppermute | solution.py:25
  229.5 2.1 collective-permute-done.38
  233.3 3.4 collective-permute-start.40
  236.7 2.5 fusion.6
  249.7 5.5 %collective-permute-done.41 = bf16[2,4,24,576]{3,2,1,0:T(8,128)(2,1)S(1)} collective-permute-done((bf16[2,4,24,576]{3,2,1,0:T(8,128)(2,1)S(1)}, bf16[2,4,24,576]{3,2,1,0:T(8,128)(2,1)S(1)}, u32[]{:S(2)}, u32[]{:S(2)}) %collective-permute-start.41) | collective-permute-done | bytes 221216 | tf_op jit(solution)/shard_map/ppermute | solution.py:25
  260.7 3.6 %collective-permute-done.45 = bf16[4,120,768]{2,1,0:T(8,128)(2,1)} collective-permute-done((bf16[4,120,768]{2,1,0:T(8,128)(2,1)}, bf16[4,120,768]{2,1,0:T(8,128)(2,1)}, u32[]{:S(2)}, u32[]{:S(2)}) %collective-permute-start.45) | collective-permute-done | bytes 737312 | tf_op jit(solution)/shard_map/ppermute | solution.py:25
  269.5 7.2 %collective-permute-done.46 = bf16[2,120,768]{2,1,0:T(8,128)(2,1)S(1)} collective-permute-done((bf16[2,120,768]{2,1,0:T(8,128)(2,1)S(1)}, bf16[2,120,768]{2,1,0:T(8,128)(2,1)S(1)}, u32[]{:S(2)}, u32[]{:S(2)}) %collective-permute-start.46) | collective-permute-done | bytes 368672 | tf_op jit(solution)/shard_map/ppermute | solution.py:25
  276.8 2.8 collective-permute-start.47
  279.9 11.5 %collective-permute-done.47 = bf16[1,120,768]{2,1,0:T(8,128)(2,1)S(1)} collective-permute-done((bf16[1,120,768]{2,1,0:T(8,128)(2,1)S(1)}, bf16[1,120,768]{2,1,0:T(8,128)(2,1)S(1)}, u32[]{:S(2)}, u32[]{:S(2)}) %collective-permute-start.47) | collective-permute-done | bytes 184352 | tf_op jit(solution)/shard_map/ppermute | solution.py:25
  292.8 8.2 %collective-permute-done.48 = bf16[1,120,768]{2,1,0:T(8,128)(2,1)S(1)} collective-permute-done((bf16[1,120,768]{2,1,0:T(8,128)(2,1)S(1)}, bf16[1,120,768]{2,1,0:T(8,128)(2,1)S(1)}, u32[]{:S(2)}, u32[]{:S(2)}) %collective-permute-start.48) | collective-permute-done | bytes 184352 | tf_op jit(solution)/shard_map/ppermute | solution.py:25
  304.5 6.5 %collective-permute-done.49 = bf16[2,120,768]{2,1,0:T(8,128)(2,1)} collective-permute-done((bf16[2,120,768]{2,1,0:T(8,128)(2,1)S(1)}, bf16[2,120,768]{2,1,0:T(8,128)(2,1)}, u32[]{:S(2)}, u32[]{:S(2)}) %collective-permute-start.49) | collective-permute-done | bytes 368672 | tf_op jit(solution)/shard_map/ppermute | solution.py:25
  318.8 11.7 %collective-permute-done.31 = f32[15,768]{1,0:T(8,128)S(1)} collective-permute-done((f32[15,768]{1,0:T(8,128)S(1)}, f32[15,768]{1,0:T(8,128)S(1)}, u32[]{:S(2)}, u32[]{:S(2)}) %collective-permute-start.31) | collective-permute-done | bytes 46112 | tf_op jit(solution)/shard_map/ppermute | solution.py:25
  330.8 3.8 %collective-permute-done.32 = f32[15,768]{1,0:T(8,128)S(1)} collective-permute-done((f32[15,768]{1,0:T(8,128)S(1)}, f32[15,768]{1,0:T(8,128)S(1)}, u32[]{:S(2)}, u32[]{:S(2)}) %collective-permute-start.32) | collective-permute-done | bytes 46112 | tf_op jit(solution)/shard_map/ppermute | solution.py:25
  334.6 3.4 collective-permute-start.33
  338.0 2.6 settle.3
  343.4 2.8 settle.5
  346.3 3.2 settle.4
  (294 shorter events, 92.2 us)
Async XLA Ops:
  5.7 41.1 %collective-permute-start.10 = (bf16[3,192,192]{2,1,0:T(8,128)(2,1)}, bf16[3,192,192]{2,1,0:T(8,128)(2,1)}, u32[]{:S(2)}, u32[]{:S(2)}) collective-permute-start(bf16[3,192,192]{2,1,0:T(8,128)(2,1)} %get-tuple-element.108), channel_id=1, source_target_pairs={{0,3},{1,2},{2,1},{3,0},{4,7},{5,6},{6,5},{7,4},{8,11},{9,10},{10,... | collective-permute-start | bytes 663560 | tf_op jit(solution)/shard_map/ppermute | solution.py:25
  8.4 38.5 %collective-permute-start.8 = (bf16[3,192,192]{2,1,0:T(8,128)(2,1)}, bf16[3,192,192]{2,1,0:T(8,128)(2,1)}, u32[]{:S(2)}, u32[]{:S(2)}) collective-permute-start(bf16[3,192,192]{2,1,0:T(8,128)(2,1)} %get-tuple-element.110), channel_id=1, source_target_pairs={{0,1},{1,0},{2,3},{3,2},{4,5},{5,4},{6,7},{7,6},{8,9},{9,8},{10,11... | collective-permute-start | bytes 663560 | tf_op jit(solution)/shard_map/ppermute | solution.py:25
  10.4 53.3 %collective-permute-start.14 = (bf16[480,768]{1,0:T(8,128)(2,1)S(1)}, bf16[480,768]{1,0:T(8,128)(2,1)}, u32[]{:S(2)}, u32[]{:S(2)}) collective-permute-start(bf16[480,768]{1,0:T(8,128)(2,1)S(1)} %fusion.12), channel_id=1, source_target_pairs={{0,2},{1,3},{2,0},{3,1},{4,6},{5,7},{6,4},{7,5},{8,10},{9,11},{10,... | collective-permute-start | bytes 2211848 | tf_op jit(solution)/shard_map/ppermute | solution.py:25
  11.0 21.3 %collective-permute-start.1 = (f32[2,768]{1,0:T(2,128)S(1)}, f32[2,768]{1,0:T(2,128)S(1)}, u32[]{:S(2)}, u32[]{:S(2)}) collective-permute-start(f32[2,768]{1,0:T(2,128)S(1)} %fusion.23), channel_id=1, source_target_pairs={{0,2},{1,3},{2,0},{3,1},{4,6},{5,7},{6,4},{7,5},{8,10},{9,11},{10,... | collective-permute-start | bytes 18440 | tf_op jit(solution)/shard_map/ppermute | solution.py:25
  13.7 33.4 %collective-permute-start.19 = (bf16[384,768]{1,0:T(8,128)(2,1)S(1)}, bf16[384,768]{1,0:T(8,128)(2,1)}, u32[]{:S(2)}, u32[]{:S(2)}) collective-permute-start(bf16[384,768]{1,0:T(8,128)(2,1)S(1)} %dynamic-slice_bitcast_fusion), channel_id=1, source_target_pairs={{0,2},{1,3},{2,0},{3,1},{4,6},{5,7},{6,4},{7,5},{8,10},{9,11},{10,... | collective-permute-start | bytes 1769480 | tf_op jit(solution)/shard_map/ppermute | solution.py:25
  44.9 22.3 %collective-permute-start.6 = (bf16[3,128,768]{2,1,0:T(8,128)(2,1)S(1)}, bf16[3,128,768]{2,1,0:T(8,128)(2,1)}, u32[]{:S(2)}, u32[]{:S(2)}) collective-permute-start(bf16[3,128,768]{2,1,0:T(8,128)(2,1)S(1)} %add_convert_fusion.1.refs_0_.refs_4_), channel_id=1, source_target_pairs={{0,2},{1,3},{2,0},{3,1},{4,6},{5,7},{6,4},{7,5},{8,10},{9,11},{10,... | collective-permute-start | bytes 1769480 | tf_op jit(solution)/shard_map/ppermute | solution.py:25
  46.9 20.4 %collective-permute-start.5 = (bf16[3,128,768]{2,1,0:T(8,128)(2,1)S(1)}, bf16[3,128,768]{2,1,0:T(8,128)(2,1)S(1)}, u32[]{:S(2)}, u32[]{:S(2)}) collective-permute-start(bf16[3,128,768]{2,1,0:T(8,128)(2,1)S(1)} %add_convert_fusion.1.refs_0_.refs_4_), channel_id=1, source_target_pairs={{0,1},{1,0},{2,3},{3,2},{4,5},{5,4},{6,7},{7,6},{8,9},{9,8},{10,11... | collective-permute-start | bytes 1769480 | tf_op jit(solution)/shard_map/ppermute | solution.py:25
  46.9 16.8 %collective-permute-start.9 = (bf16[3,192,192]{2,1,0:T(8,128)(2,1)S(1)}, bf16[3,192,192]{2,1,0:T(8,128)(2,1)S(1)}, u32[]{:S(2)}, u32[]{:S(2)}) collective-permute-start(bf16[3,192,192]{2,1,0:T(8,128)(2,1)S(1)} %get-tuple-element.109), channel_id=1, source_target_pairs={{0,2},{1,3},{2,0},{3,1},{4,6},{5,7},{6,4},{7,5},{8,10},{9,11},{10,... | collective-permute-start | bytes 663560 | tf_op jit(solution)/shard_map/ppermute | solution.py:25
  47.1 20.6 %collective-permute-start.20 = (bf16[384,768]{1,0:T(8,128)(2,1)}, bf16[384,768]{1,0:T(8,128)(2,1)}, u32[]{:S(2)}, u32[]{:S(2)}) collective-permute-start(bf16[384,768]{1,0:T(8,128)(2,1)} %collective-permute-done.19.refs_15_), channel_id=1, source_target_pairs={{0,4},{4,0},{8,12},{12,8},{16,20},{20,16},{24,28},{28,24},{1,5},{5... | collective-permute-start | bytes 1769480 | tf_op jit(solution)/shard_map/ppermute | solution.py:25
  63.7 30.5 %collective-permute-start.21 = (bf16[2,384,768]{2,1,0:T(8,128)(2,1)}, bf16[2,384,768]{2,1,0:T(8,128)(2,1)}, u32[]{:S(2)}, u32[]{:S(2)}) collective-permute-start(bf16[2,384,768]{2,1,0:T(8,128)(2,1)} %bitcast.15.refs_14_), channel_id=1, source_target_pairs={{0,1},{1,0},{2,3},{3,2},{4,5},{5,4},{6,7},{7,6},{8,9},{9,8},{10,11... | collective-permute-start | bytes 3538952 | tf_op jit(solution)/shard_map/ppermute | solution.py:25
  64.4 18.5 %collective-permute-start.15 = (bf16[480,768]{1,0:T(8,128)(2,1)}, bf16[480,768]{1,0:T(8,128)(2,1)}, u32[]{:S(2)}, u32[]{:S(2)}) collective-permute-start(bf16[480,768]{1,0:T(8,128)(2,1)} %collective-permute-done.14.refs_9_), channel_id=1, source_target_pairs={{0,4},{4,0},{8,12},{12,8},{16,20},{20,16},{24,28},{28,24},{1,5},{5... | collective-permute-start | bytes 2211848 | tf_op jit(solution)/shard_map/ppermute | solution.py:25
  67.2 41.0 %collective-permute-start.16 = (bf16[2,480,768]{2,1,0:T(8,128)(2,1)}, bf16[2,480,768]{2,1,0:T(8,128)(2,1)S(1)}, u32[]{:S(2)}, u32[]{:S(2)}) collective-permute-start(bf16[2,480,768]{2,1,0:T(8,128)(2,1)} %pad_maximum_fusion.1.refs_8_), channel_id=1, source_target_pairs={{0,1},{1,0},{2,3},{3,2},{4,5},{5,4},{6,7},{7,6},{8,9},{9,8},{10,11... | collective-permute-start | bytes 4423688 | tf_op jit(solution)/shard_map/ppermute | solution.py:25
  68.1 25.5 %collective-permute-start.22 = (bf16[384,768]{1,0:T(8,128)(2,1)}, bf16[384,768]{1,0:T(8,128)(2,1)}, u32[]{:S(2)}, u32[]{:S(2)}) collective-permute-start(bf16[384,768]{1,0:T(8,128)(2,1)} %collective-permute-done.19.refs_15_), channel_id=1, source_target_pairs={{0,1},{1,0},{2,3},{3,2},{4,5},{5,4},{6,7},{7,6},{8,9},{9,8},{10,11... | collective-permute-start | bytes 1769480 | tf_op jit(solution)/shard_map/ppermute | solution.py:25
  71.5 36.7 %collective-permute-start.17 = (bf16[480,768]{1,0:T(8,128)(2,1)}, bf16[480,768]{1,0:T(8,128)(2,1)S(1)}, u32[]{:S(2)}, u32[]{:S(2)}) collective-permute-start(bf16[480,768]{1,0:T(8,128)(2,1)} %collective-permute-done.14.refs_9_), channel_id=1, source_target_pairs={{0,1},{1,0},{2,3},{3,2},{4,5},{5,4},{6,7},{7,6},{8,9},{9,8},{10,11... | collective-permute-start | bytes 2211848 | tf_op jit(solution)/shard_map/ppermute | solution.py:25
  82.9 25.3 %collective-permute-start.18 = (bf16[480,768]{1,0:T(8,128)(2,1)}, bf16[480,768]{1,0:T(8,128)(2,1)}, u32[]{:S(2)}, u32[]{:S(2)}) collective-permute-start(bf16[480,768]{1,0:T(8,128)(2,1)} %collective-permute-done.15.refs_10_), channel_id=1, source_target_pairs={{0,1},{1,0},{2,3},{3,2},{4,5},{5,4},{6,7},{7,6},{8,9},{9,8},{10,11... | collective-permute-start | bytes 2211848 | tf_op jit(solution)/shard_map/ppermute | solution.py:25
  94.2 14.0 %collective-permute-start.23 = (bf16[384,768]{1,0:T(8,128)(2,1)}, bf16[384,768]{1,0:T(8,128)(2,1)}, u32[]{:S(2)}, u32[]{:S(2)}) collective-permute-start(bf16[384,768]{1,0:T(8,128)(2,1)} %collective-permute-done.20.refs_16_), channel_id=1, source_target_pairs={{0,1},{1,0},{2,3},{3,2},{4,5},{5,4},{6,7},{7,6},{8,9},{9,8},{10,11... | collective-permute-start | bytes 1769480 | tf_op jit(solution)/shard_map/ppermute | solution.py:25
  142.1 47.9 %collective-permute-start.43 = (bf16[2,8,120,768]{3,2,1,0:T(8,128)(2,1)}, bf16[2,8,120,768]{3,2,1,0:T(8,128)(2,1)S(1)}, u32[]{:S(2)}, u32[]{:S(2)}) collective-permute-start(bf16[2,8,120,768]{3,2,1,0:T(8,128)(2,1)} %get-tuple-element.76), channel_id=1, source_target_pairs={{0,1},{1,0},{2,3},{3,2},{4,5},{5,4},{6,7},{7,6},{8,9},{9,8},{10,11... | collective-permute-start | bytes 8847368 | tf_op jit(solution)/shard_map/ppermute | solution.py:25
  142.3 44.5 %collective-permute-start.51 = (bf16[2,8,96,768]{3,2,1,0:T(8,128)(2,1)}, bf16[2,8,96,768]{3,2,1,0:T(8,128)(2,1)S(1)}, u32[]{:S(2)}, u32[]{:S(2)}) collective-permute-start(bf16[2,8,96,768]{3,2,1,0:T(8,128)(2,1)} %get-tuple-element.81), channel_id=1, source_target_pairs={{0,1},{1,0},{2,3},{3,2},{4,5},{5,4},{6,7},{7,6},{8,9},{9,8},{10,11... | collective-permute-start | bytes 7077896 | tf_op jit(solution)/shard_map/ppermute | solution.py:25
  171.2 13.5 %collective-permute-start.34 = (bf16[4,4,24,576]{3,2,1,0:T(8,128)(2,1)S(1)}, bf16[4,4,24,576]{3,2,1,0:T(8,128)(2,1)S(1)}, u32[]{:S(2)}, u32[]{:S(2)}) collective-permute-start(bf16[4,4,24,576]{3,2,1,0:T(8,128)(2,1)S(1)} %slice.141), channel_id=1, source_target_pairs={{0,4},{4,0},{8,12},{12,8},{16,20},{20,16},{24,28},{28,24},{1,5},{5... | collective-permute-start | bytes 1327112 | tf_op jit(solution)/shard_map/ppermute | solution.py:25
  188.5 48.2 %collective-permute-start.52 = (bf16[8,96,768]{2,1,0:T(8,128)(2,1)}, bf16[8,96,768]{2,1,0:T(8,128)(2,1)}, u32[]{:S(2)}, u32[]{:S(2)}) collective-permute-start(bf16[8,96,768]{2,1,0:T(8,128)(2,1)} %fusion.5), channel_id=1, source_target_pairs={{0,2},{1,3},{2,0},{3,1},{4,6},{5,7},{6,4},{7,5},{8,10},{9,11},{10,... | collective-permute-start | bytes 3538952 | tf_op jit(solution)/shard_map/ppermute | solution.py:25
  192.7 49.1 %collective-permute-start.44 = (bf16[4,2,120,768]{3,2,0,1:T(8,128)(2,1)}, bf16[4,2,120,768]{3,2,0,1:T(8,128)(2,1)}, u32[]{:S(2)}, u32[]{:S(2)}) collective-permute-start(bf16[4,2,120,768]{3,2,0,1:T(8,128)(2,1)} %fusion.2), channel_id=1, source_target_pairs={{0,8},{4,12},{8,0},{12,4},{16,24},{20,28},{24,16},{28,20},{1,9},{5... | collective-permute-start | bytes 4423688 | tf_op jit(solution)/shard_map/ppermute | solution.py:25
  193.2 33.5 %collective-permute-start.36 = (bf16[1,4,24,576]{3,2,1,0:T(8,128)(2,1)S(1)}, bf16[1,4,24,576]{3,2,1,0:T(8,128)(2,1)S(1)}, u32[]{:S(2)}, u32[]{:S(2)}) collective-permute-start(bf16[1,4,24,576]{3,2,1,0:T(8,128)(2,1)S(1)} %slice.270), channel_id=1, source_target_pairs={{0,16},{4,20},{8,24},{12,28},{16,0},{20,4},{24,8},{28,12},{1,17},{... | collective-permute-start | bytes 331784 | tf_op jit(solution)/shard_map/ppermute | solution.py:25
  229.2 37.5 %collective-permute-start.27 = (bf16[2,3,128,768]{3,2,1,0:T(8,128)(2,1)}, bf16[2,3,128,768]{3,2,1,0:T(8,128)(2,1)}, u32[]{:S(2)}, u32[]{:S(2)}) collective-permute-start(bf16[2,3,128,768]{3,2,1,0:T(8,128)(2,1)} %get-tuple-element.67), channel_id=1, source_target_pairs={{0,1},{1,0},{2,3},{3,2},{4,5},{5,4},{6,7},{7,6},{8,9},{9,8},{10,11... | collective-permute-start | bytes 3538952 | tf_op jit(solution)/shard_map/ppermute | solution.py:25
  233.3 13.7 %collective-permute-start.40 = (bf16[1,4,24,576]{3,2,1,0:T(8,128)(2,1)S(1)}, bf16[1,4,24,576]{3,2,1,0:T(8,128)(2,1)}, u32[]{:S(2)}, u32[]{:S(2)}) collective-permute-start(bf16[1,4,24,576]{3,2,1,0:T(8,128)(2,1)S(1)} %pad_maximum_fusion.8), channel_id=1, source_target_pairs={{0,16},{4,20},{8,24},{12,28},{16,0},{20,4},{24,8},{28,12},{1,17},{... | collective-permute-start | bytes 331784 | tf_op jit(solution)/shard_map/ppermute | solution.py:25
  240.2 17.7 %collective-permute-start.53 = (bf16[4,96,768]{2,1,0:T(8,128)(2,1)}, bf16[4,96,768]{2,1,0:T(8,128)(2,1)}, u32[]{:S(2)}, u32[]{:S(2)}) collective-permute-start(bf16[4,96,768]{2,1,0:T(8,128)(2,1)} %slice.264), channel_id=1, source_target_pairs={{0,4},{4,0},{8,12},{12,8},{16,20},{20,16},{24,28},{28,24},{1,5},{5... | collective-permute-start | bytes 1769480 | tf_op jit(solution)/shard_map/ppermute | solution.py:25
  246.0 18.4 %collective-permute-start.45 = (bf16[4,120,768]{2,1,0:T(8,128)(2,1)}, bf16[4,120,768]{2,1,0:T(8,128)(2,1)}, u32[]{:S(2)}, u32[]{:S(2)}) collective-permute-start(bf16[4,120,768]{2,1,0:T(8,128)(2,1)} %fusion.13), channel_id=1, source_target_pairs={{0,2},{1,3},{2,0},{3,1},{4,6},{5,7},{6,4},{7,5},{8,10},{9,11},{10,... | collective-permute-start | bytes 2211848 | tf_op jit(solution)/shard_map/ppermute | solution.py:25
  257.0 81.1 %collective-permute-start.42 = (bf16[4,4,24,576]{3,2,1,0:T(8,128)(2,1)}, bf16[4,4,24,576]{3,2,1,0:T(8,128)(2,1)}, u32[]{:S(2)}, u32[]{:S(2)}) collective-permute-start(bf16[4,4,24,576]{3,2,1,0:T(8,128)(2,1)} %pad_maximum_fusion.4.refs_0_), channel_id=1, source_target_pairs={{0,4},{4,0},{8,12},{12,8},{16,20},{20,16},{24,28},{28,24},{1,5},{5... | collective-permute-start | bytes 1327112 | tf_op jit(solution)/shard_map/ppermute | solution.py:25
  267.9 23.6 %collective-permute-start.28 = (bf16[3,128,768]{2,1,0:T(8,128)(2,1)S(1)}, bf16[3,128,768]{2,1,0:T(8,128)(2,1)S(1)}, u32[]{:S(2)}, u32[]{:S(2)}) collective-permute-start(bf16[3,128,768]{2,1,0:T(8,128)(2,1)S(1)} %fusion.14), channel_id=1, source_target_pairs={{0,2},{1,3},{2,0},{3,1},{4,6},{5,7},{6,4},{7,5},{8,10},{9,11},{10,... | collective-permute-start | bytes 1769480 | tf_op jit(solution)/shard_map/ppermute | solution.py:25
  276.8 14.6 %collective-permute-start.47 = (bf16[1,120,768]{2,1,0:T(8,128)(2,1)S(1)}, bf16[1,120,768]{2,1,0:T(8,128)(2,1)S(1)}, u32[]{:S(2)}, u32[]{:S(2)}) collective-permute-start(bf16[1,120,768]{2,1,0:T(8,128)(2,1)S(1)} %slice.268), channel_id=1, source_target_pairs={{0,16},{4,20},{8,24},{12,28},{16,0},{20,4},{24,8},{28,12},{1,17},{... | collective-permute-start | bytes 552968 | tf_op jit(solution)/shard_map/ppermute | solution.py:25
  279.6 22.7 %collective-permute-start.56 = (bf16[1,96,768]{2,1,0:T(8,128)(2,1)S(1)}, bf16[1,96,768]{2,1,0:T(8,128)(2,1)S(1)}, u32[]{:S(2)}, u32[]{:S(2)}) collective-permute-start(bf16[1,96,768]{2,1,0:T(8,128)(2,1)S(1)} %fusion.16), channel_id=1, source_target_pairs={{0,16},{4,20},{8,24},{12,28},{16,0},{20,4},{24,8},{28,12},{1,17},{... | collective-permute-start | bytes 442376 | tf_op jit(solution)/shard_map/ppermute | solution.py:25
  312.0 34.3 %collective-permute-start.50 = (bf16[4,120,768]{2,1,0:T(8,128)(2,1)S(1)}, bf16[4,120,768]{2,1,0:T(8,128)(2,1)}, u32[]{:S(2)}, u32[]{:S(2)}) collective-permute-start(bf16[4,120,768]{2,1,0:T(8,128)(2,1)S(1)} %pad_maximum_fusion.2.refs_0_), channel_id=1, source_target_pairs={{0,8},{4,12},{8,0},{12,4},{16,24},{20,28},{24,16},{28,20},{1,9},{5... | collective-permute-start | bytes 2211848 | tf_op jit(solution)/shard_map/ppermute | solution.py:25
  315.5 28.0 %collective-permute-start.58 = (bf16[4,96,768]{2,1,0:T(8,128)(2,1)S(1)}, bf16[4,96,768]{2,1,0:T(8,128)(2,1)}, u32[]{:S(2)}, u32[]{:S(2)}) collective-permute-start(bf16[4,96,768]{2,1,0:T(8,128)(2,1)S(1)} %pad_maximum_fusion.3.refs_0_), channel_id=1, source_target_pairs={{0,4},{4,0},{8,12},{12,8},{16,20},{20,16},{24,28},{28,24},{1,5},{5... | collective-permute-start | bytes 1769480 | tf_op jit(solution)/shard_map/ppermute | solution.py:25
  (81 other events, 816.1 us)
where the time goes:
time: 350 us; the launch traced here: 349 us
  waiting for transfers between devices  168 us (48%)
  Pallas kernels  69.2 us (20%)
  starting transfers between devices  62.1 us (18%)
  other arithmetic  28.6 us (8%)
  local copies, waits for them, and re-layouts  19.9 us (6%)
    ppermute x59, waiting for transfers between devices, swap(): lax.ppermute(x, axis, [(i, i ^ by) for i in range(lax.axis_size(axis))])  168 us
    ppermute x59, starting transfers between devices, swap(): lax.ppermute(x, axis, [(i, i ^ by) for i in range(lax.axis_size(axis))])  62.1 us
    pallas_call x1, Pallas kernels, middle(): pl.pallas_call(middle_kernel, in_specs=[pl.BlockSpec(memory_space=pltpu.S...  32.4 us
    pallas_call x1, Pallas kernels, attend_back(): pl.pallas_call(attend_back_kernel, grid=(documents,), in_specs=[pl.BlockS...  17.5 us
    pallas_call x1, Pallas kernels, attend(): pl.pallas_call(attend_kernel, grid=(documents,), in_specs=[pl.BlockSpec(m...  10.6 us
    pallas_call x3, Pallas kernels, settle(): pl.pallas_call(functools.partial(settle_kernel, order=order, store=store)...  8.65 us
  transfers between devices with their start and end apart: 59, of which 23 were waited for; matrix products, arithmetic and copies ran while one was open for 12% of the time, Pallas kernels for 10%

commit v1 on v0

v1 whole, which is shorter than its diff:
```python
import functools
import math

import jax
import jax.numpy as jnp
from jax import lax
from jax.experimental import pallas as pl
from jax.experimental.pallas import tpu as pltpu
from jax.sharding import PartitionSpec as P

HEAD_DIM = 64
EPS_NORM = 1e-12
EPS_BATCH = 1e-05
F32 = jnp.float32
BF16 = jnp.bfloat16
GELU_IN = math.sqrt(2.0 / math.pi)
GELU_CUBE = 0.044715
PIECES = 8
NEAR = 4
DOWN_ORDER = (2, 1, 4)
UP_ORDER = (1, 2, 4)
HEAD_ORDER = (1, 2, 4)


def swap(x, axis, by):
    return lax.ppermute(x, axis, [(i, i ^ by) for i in range(lax.axis_size(axis))])


def bits(axis):
    found, by = [], 1
    while by < lax.axis_size(axis):
        found.append(by)
        by *= 2
    return found


def sum_all(x):
    for axis in ("seq", "dp"):
        for by in bits(axis):
            x = x + swap(x, axis, by)
    return x


def nn(a, b):
    return jnp.dot(a, b, preferred_element_type=F32)


def tn(a, b):
    return lax.dot_general(a, b, (((0,), (0,)), ((), ())), preferred_element_type=F32)


def nt(a, b):
    return lax.dot_general(a, b, (((1,), (1,)), ((), ())), preferred_element_type=F32)


def norm_parts(x):
    centred = x - jnp.mean(x, axis=-1, keepdims=True)
    scale = lax.rsqrt(jnp.mean(centred * centred, axis=-1, keepdims=True) + EPS_NORM)
    return centred * scale, scale


def norm_back(grad, unit, scale, gain):
    g = grad * gain
    return scale * (
        g
        - jnp.mean(g, axis=-1, keepdims=True)
        - unit * jnp.mean(g * unit, axis=-1, keepdims=True)
    )


def gather_rows(x):
    two = swap(x, "seq", 2)
    one, three = swap(x, "seq", 1), swap(two, "seq", 1)
    return [x, one, two, three]


def gather_weight(halves, mine, by):
    near = swap(mine, "seq", 2)
    far = swap(near, "dp", by)
    return [halves, near, far, swap(halves, "seq", 1), swap(near, "seq", 1), swap(far, "seq", 1)]


def scatter_pairs(keep, give):
    got = swap(give, "seq", 1)
    pass_on = (keep[1].astype(F32) + got[1].astype(F32)).astype(BF16)
    own = keep[0].astype(F32) + got[0].astype(F32)
    return own + swap(pass_on, "seq", 2).astype(F32)


def exchange_blocks(blocks):
    return [blocks[0]] + [swap(blocks[r], "seq", r) for r in (1, 2, 3)]


def params(mebibytes):
    return pltpu.CompilerParams(vmem_limit_bytes=mebibytes * 1024 * 1024)


def whole_spec():
    return pl.BlockSpec(memory_space=pltpu.VMEM)


def pack_heads_kernel(place_ref, q_ref, k_ref, v_ref, *head_refs):
    seq = place_ref[0]
    part = q_ref.shape[0]
    for c in range(4):
        for r in range(4):

            @pl.when(seq == c ^ r)
            def _(c=c, r=r):
                for i, ref in enumerate((q_ref, k_ref, v_ref)):
                    head_refs[r][:, i * part : (i + 1) * part] = ref[:, c * part : (c + 1) * part]


def pack_halves_kernel(place_ref, out_ref, up_ref, halves_ref, near_ref):
    bit = place_ref[1] % 2
    half = out_ref.shape[0] // 2
    wide = out_ref.shape[1]

    def cut(rows):
        blocks = [out_ref[rows, :]] + [up_ref[rows, j * wide : (j + 1) * wide] for j in range(4)]
        return jnp.concatenate(blocks, axis=0)

    for h in range(2):
        halves_ref[h] = cut(pl.ds(h * half, half))
    near_ref[...] = cut(pl.ds(pl.multiple_of(bit * half, half), half))


def pack(place_word, query, key, value, out, up):
    part, features = out.shape
    tall = part // 2 * 5
    heads = pl.pallas_call(
        pack_heads_kernel,
        in_specs=[pl.BlockSpec(memory_space=pltpu.SMEM)] + [whole_spec()] * 3,
        out_specs=[whole_spec()] * 4,
        out_shape=[shaped(part, 3 * part)] * 4,
        compiler_params=params(56),
        cost_estimate=pl.CostEstimate(flops=0, bytes_accessed=2 * 1024 * 1024, transcendentals=0),
        name="pack_heads",
    )(place_word, query, key, value)
    halves, near = pl.pallas_call(
        pack_halves_kernel,
        in_specs=[pl.BlockSpec(memory_space=pltpu.SMEM)] + [whole_spec()] * 2,
        out_specs=[whole_spec()] * 2,
        out_shape=[shaped(2, tall, features), shaped(tall, features)],
        compiler_params=params(56),
        cost_estimate=pl.CostEstimate(flops=0, bytes_accessed=4 * 1024 * 1024, transcendentals=0),
        name="pack_halves",
    )(place_word, out, up)
    return heads, halves, near


def attend_kernel(seq_ref, *refs, waits):
    x_refs, w_refs, bias_ref, refs = refs[:4], refs[4:8], refs[8], refs[9 + waits :]
    q_ref, k_ref, v_ref, wc_ref, out_refs = refs[0], refs[1], refs[2], refs[3], refs[4:]
    part = w_refs[0].shape[0]
    span = x_refs[0].shape[1]

    @pl.when(pl.program_id(0) == 0)
    def _():
        for r in range(4):
            at = pl.multiple_of((seq_ref[0] ^ r) * part, part)
            for i in range(3):
                wc_ref[i, pl.ds(at, part), :] = w_refs[r][:, i * part : (i + 1) * part]

    x = jnp.concatenate([ref[0] for ref in x_refs], axis=0)
    for i, ref in enumerate((q_ref, k_ref, v_ref)):
        ref[0] = (nn(x, wc_ref[i]) + bias_ref[i]).astype(BF16)
    q, k, v = q_ref[0], k_ref[0], v_ref[0]
    lane = lax.broadcasted_iota(jnp.int32, (1, part), 1) // HEAD_DIM
    for h in range(part // HEAD_DIM):
        pick = jnp.where(lane == h, 1.0 / math.sqrt(HEAD_DIM), 0.0).astype(BF16)
        scores = nt(k, q * pick)
        raised = jnp.exp(scores - jnp.max(scores, axis=0, keepdims=True))
        chances = (raised * (1.0 / jnp.sum(raised, axis=0, keepdims=True))).astype(BF16)
        attended = tn(v, chances)[h * HEAD_DIM : (h + 1) * HEAD_DIM].astype(BF16)
        for r in range(4):
            out_refs[r][h * HEAD_DIM : (h + 1) * HEAD_DIM, :] = attended[:, r * span : (r + 1) * span]


def attend(seq, x_blocks, w_blocks, bias, after):
    documents, span, features = x_blocks[0].shape
    part = w_blocks[0].shape[0]
    length = 4 * span
    flops = documents * (2 * length * features * 3 * part + 4 * length * length * part)
    per_doc = pl.BlockSpec((1, length, part), lambda d: (d, 0, 0))
    return pl.pallas_call(
        functools.partial(attend_kernel, waits=len(after)),
        grid=(documents,),
        in_specs=[pl.BlockSpec(memory_space=pltpu.SMEM)]
        + [pl.BlockSpec((1, span, features), lambda d: (d, 0, 0))] * 4
        + [pl.BlockSpec((part, 3 * part), lambda d: (0, 0))] * 4
        + [pl.BlockSpec((3, 1, part), lambda d: (0, 0, 0))]
        + [any_spec()] * len(after),
        out_specs=[per_doc] * 3
        + [pl.BlockSpec((3, features, part), lambda d: (0, 0, 0))]
        + [pl.BlockSpec((part, span), lambda d: (0, d))] * 4,
        out_shape=[jax.ShapeDtypeStruct((documents, length, part), BF16)] * 3
        + [jax.ShapeDtypeStruct((3, features, part), BF16)]
        + [jax.ShapeDtypeStruct((part, documents * span), BF16)] * 4,
        compiler_params=params(56),
        cost_estimate=pl.CostEstimate(
            flops=flops, bytes_accessed=8 * 1024 * 1024, transcendentals=documents * length * length * 3
        ),
        name="attend",
    )(seq, *x_blocks, *w_blocks, bias, *after)


def attend_back_kernel(place_ref, *refs, waits):
    g_refs, x_refs = refs[:4], refs[4:8]
    q_ref, k_ref, v_ref, wc_ref = refs[8:12]
    keep_ref, give_ref, dw_keep_ref, dw_give_ref, sums_ref, acc_ref = refs[12 + waits :]
    part = q_ref.shape[2]
    span = x_refs[0].shape[1]
    first = pl.program_id(0) == 0
    q, k, v = q_ref[0], k_ref[0], v_ref[0]
    g = jnp.concatenate([ref[...] for ref in g_refs], axis=1)
    lane = lax.broadcasted_iota(jnp.int32, (1, part), 1) // HEAD_DIM
    scale = 1.0 / math.sqrt(HEAD_DIM)
    dq = dk = dv = None
    for h in range(part // HEAD_DIM):
        on = lane == h
        pick = jnp.where(on, scale, 0.0).astype(BF16)
        mask = jnp.where(on, 1.0, 0.0)
        scores = nt(k, q * pick)
        raised = jnp.exp(scores - jnp.max(scores, axis=0, keepdims=True))
        chances = raised * (1.0 / jnp.sum(raised, axis=0, keepdims=True))
        grad = nn(v * mask.astype(BF16), g)
        both = chances * grad
        grad = (both - chances * jnp.sum(both, axis=0, keepdims=True)).astype(BF16)
        part_v = nt(chances.astype(BF16), g) * mask
        part_k = nn(grad, q) * (mask * scale)
        part_q = tn(grad, k) * (mask * scale)
        dq = part_q if dq is None else dq + part_q
        dk = part_k if dk is None else dk + part_k
        dv = part_v if dv is None else dv + part_v
    low = [t.astype(BF16) for t in (dq, dk, dv)]
    sums = jnp.concatenate(
        [jnp.sum(low[i].astype(F32), axis=0, keepdims=True) for i in (0, 2)], axis=0
    )
    x = jnp.concatenate([ref[0] for ref in x_refs], axis=0)
    x_t = x.T
    inner = nt(low[0], wc_ref[0]) + nt(low[1], wc_ref[1]) + nt(low[2], wc_ref[2])
    inner = inner.astype(BF16)
    for r in range(4):
        (give_ref if r % 2 else keep_ref)[r // 2, 0] = inner[r * span : (r + 1) * span]

    @pl.when(first)
    def _():
        sums_ref[...] = sums
        for i in range(3):
            acc_ref[i] = nn(x_t, low[i])

    @pl.when(jnp.logical_not(first))
    def _():
        sums_ref[...] += sums
        for i in range(3):
            acc_ref[i] += nn(x_t, low[i])

    @pl.when(pl.program_id(0) == pl.num_programs(0) - 1)
    def _():
        tall = part // PIECES
        dp = place_ref[1] % NEAR
        first = HEAD_ORDER[0]
        for p in range(PIECES):
            spot = place(p ^ dp, HEAD_ORDER[1:])
            for mine, ref in ((True, dw_keep_ref), (False, dw_give_ref)):

                @pl.when(((p ^ dp) // first % 2 == 0) == mine)
                def _(p=p, spot=spot, ref=ref):
                    for block in range(4):
                        at = block * part + p * tall
                        for i in range(3):
                            ref[spot, place_ref[0] ^ block, :, i * part : (i + 1) * part] = acc_ref[
                                i, at : at + tall, :
                            ].astype(BF16)


def attend_back(place_word, g_blocks, x_blocks, q, k, v, wc, after):
    documents, span, features = x_blocks[0].shape
    part = q.shape[2]
    length = 4 * span
    flops = documents * (4 * length * features * 3 * part + 10 * length * length * part)
    per_doc = pl.BlockSpec((1, length, part), lambda d: (d, 0, 0))
    pair = pl.BlockSpec((2, 1, span, features), lambda d: (0, d, 0, 0))
    return pl.pallas_call(
        functools.partial(attend_back_kernel, waits=len(after)),
        grid=(documents,),
        in_specs=[pl.BlockSpec(memory_space=pltpu.SMEM)]
        + [pl.BlockSpec((part, span), lambda d: (0, d))] * 4
        + [pl.BlockSpec((1, span, features), lambda d: (d, 0, 0))] * 4
        + [per_doc] * 3
        + [pl.BlockSpec((3, features, part), lambda d: (0, 0, 0))]
        + [any_spec()] * len(after),
        out_specs=[
            pair,
            pair,
            pl.BlockSpec((PIECES // 2, 4, part // PIECES, 3 * part), lambda d: (0, 0, 0, 0)),
            pl.BlockSpec((PIECES // 2, 4, part // PIECES, 3 * part), lambda d: (0, 0, 0, 0)),
            pl.BlockSpec((2, part), lambda d: (0, 0)),
        ],
        out_shape=[jax.ShapeDtypeStruct((2, documents, span, features), BF16)] * 2
        + [
            jax.ShapeDtypeStruct((PIECES // 2, 4, part // PIECES, 3 * part), BF16),
            jax.ShapeDtypeStruct((PIECES // 2, 4, part // PIECES, 3 * part), BF16),
            jax.ShapeDtypeStruct((2, part), F32),
        ],
        scratch_shapes=[pltpu.VMEM((3, features, part), F32)],
        compiler_params=params(56),
        cost_estimate=pl.CostEstimate(
            flops=flops, bytes_accessed=12 * 1024 * 1024, transcendentals=documents * length * length * 3
        ),
        name="attend_back",
    )(place_word, *g_blocks, *x_blocks, q, k, v, wc, *after)


def gelu_parts(x):
    square = x * x
    bend = jnp.tanh(GELU_IN * x * (1.0 + GELU_CUBE * square))
    gate = 0.5 * (1.0 + bend)
    rise = 0.5 * x * (1.0 - bend * bend) * (GELU_IN + 3.0 * GELU_IN * GELU_CUBE * square)
    return x * gate, gate + rise


def place(index, order):
    at = 0
    for by in order:
        at = 2 * at + (index // by) % 2
    return at


def weight_copies(place_ref, pieces, wo, up, down, sems):
    seq, dp = place_ref[0], place_ref[1]
    part = wo.shape[1]
    half = part // 2
    wo_copies, up_copies, down_copies = [], [[] for _ in range(4)], [[] for _ in range(4)]

    def bring(found, source, target):
        found.append(pltpu.make_async_copy(source, target, sems.at[sum(used)]))
        used.append(1)

    used = []
    own, near, far, one, near_one, far_one = pieces[:6]
    bit = dp % 2
    parts = [(own.at[h], 0, h) for h in range(2)] + [(one.at[h], 1, h) for h in range(2)]
    parts += [(near, 2, bit), (far, 2, 1 - bit), (near_one, 3, bit), (far_one, 3, 1 - bit)]
    for source, r, h in parts:
        at = pl.multiple_of(h * half, half)
        bring(wo_copies, source.at[pl.ds(0, half)], wo.at[r, pl.ds(at, half)])
        if up is None:
            continue
        at = pl.multiple_of((seq ^ r) * part + h * half, half)
        for i in range(4):
            start = pl.multiple_of(half * (1 + (seq ^ i)), half)
            bring(up_copies[i], source.at[pl.ds(start, half)], up.at[i, pl.ds(at, half)])
    for r in range(4 if down is not None else 0):
        bring(down_copies[r], pieces[6 + r], down.at[r])
    return wo_copies, up_copies, down_copies


def start_all(copies):
    for copy in copies:
        copy.start()


def wait_all(copies):
    for copy in copies:
        copy.wait()


def forward_kernel(place_ref, *refs):
    (a_refs, in_ref, cot_ref, vec_ref, upb_ref), refs = (refs[:4], *refs[4:8]), refs[8:]
    pieces, refs = refs[:10], refs[10:]
    out_ref, unit_ref, scale_ref, grad_ref, sums_ref, upsum_ref = refs[:6]
    outs = (refs[6:9], refs[9:12])
    wo, up, down, act, slope, low_t, spare, terms, sems, out_sems = refs[12:]
    seq, dp = place_ref[0], place_ref[1]
    part = wo.shape[1]
    half = part // 2
    size = terms.shape[3]

    wo_copies, up_copies, down_copies = weight_copies(place_ref, pieces, wo, up, down, sems)
    start_all(wo_copies + up_copies[0] + up_copies[1])
    out_bias, gain1, shift1, down_bias, gain2, shift2 = (vec_ref[i : i + 1, :] for i in range(6))
    residual = in_ref[...] + out_bias
    wait_all(wo_copies)
    joined = jnp.concatenate([ref[...] for ref in a_refs], axis=0)
    residual += tn(joined, wo[...].reshape(joined.shape[0], -1))
    unit1, scale1 = norm_parts(residual)
    unit_ref[...] = unit1
    scale_ref[...] = scale1
    first_out = unit1 * gain1 + shift1
    low = first_out.astype(BF16)
    for r in range(4):
        wait_all(up_copies[r])
        start_all(up_copies[r + 2] if r < 2 else down_copies[2 * r - 4] + down_copies[2 * r - 3])
        x = nn(low, up[r]) + upb_ref[pl.ds(seq ^ r, 1), :]
        value, rise = gelu_parts(x)
        act[r] = value.astype(BF16)
        slope[r] = rise
    second_in = first_out + down_bias
    for r in range(4):
        wait_all(down_copies[r])
        second_in += nn(act[r], down[r])
    unit2, scale2 = norm_parts(second_in)
    out_ref[...] = (unit2 * gain2 + shift2).astype(BF16)
    incoming = cot_ref[...].astype(F32)
    grad_first = norm_back(incoming, unit2, scale2, gain2)
    grad_down = grad_first.astype(BF16)
    sums_ref[0:1, :] = jnp.sum(incoming * unit2, axis=0, keepdims=True)
    sums_ref[1:2, :] = jnp.sum(incoming, axis=0, keepdims=True)
    sums_ref[2:3, :] = jnp.sum(grad_down.astype(F32), axis=0, keepdims=True)
    spare[...] = low.T
    for i in range(4):
        low_t[i * part : (i + 1) * part, :] = spare[pl.ds(pl.multiple_of((seq ^ i) * part, part), part), :]
    for r in range(4):
        grad_act = nt(grad_down, down[r]).astype(BF16).astype(F32)
        grad_up = (grad_act * slope[r]).astype(BF16)
        upsum_ref[pl.ds(seq ^ r, 1), :] = jnp.sum(grad_up.astype(F32), axis=0, keepdims=True)
        grad_first += nt(grad_up, up[r])
        value = nn(low_t[...], grad_up).astype(BF16)
        for i in range(4):
            for h in range(2):
                spot = place((2 * (seq ^ r) + h) ^ (dp % NEAR), UP_ORDER)
                at = i * part + h * half
                terms[1, i, spot] = value[at : at + half]
    grad_ref[...] = grad_first

    def send(which, r):
        keep_out, far_out, give_out = outs[which]
        target = (keep_out, give_out.at[0], far_out, give_out.at[1])[r]
        return pltpu.make_async_copy(terms.at[which, r], target, out_sems.at[which, r])

    start_all([send(1, r) for r in range(4)])
    for r in range(4):
        value = tn(act[r], grad_down)
        for p in range(PIECES):
            spot = place(p ^ (dp % NEAR), DOWN_ORDER)
            terms[0, r, spot] = value[p * size : (p + 1) * size].astype(BF16)
        send(0, r).start()
    wait_all([send(which, r) for which in range(2) for r in range(4)])


def backward_kernel(place_ref, *refs):
    (a_refs, unit_ref, scale_ref, grad_ref, vec_ref), refs = (refs[:4], *refs[4:8]), refs[8:]
    pieces, refs = refs[:6], refs[6:]
    res_ref, g_refs, sums_ref, keep_ref, far_ref, give_ref, wo, sems = refs[0], refs[1:5], *refs[5:]
    dp = place_ref[1]
    part = wo.shape[1]
    tall = part // PIECES
    copies = weight_copies(place_ref, pieces, wo, None, None, sems)[0]
    start_all(copies)
    unit1 = unit_ref[...]
    grad_first = grad_ref[...]
    grad_residual = norm_back(grad_first, unit1, scale_ref[...], vec_ref[1:2, :])
    res_ref[...] = grad_residual
    grad_out = grad_residual.astype(BF16)
    joined = jnp.concatenate([ref[...] for ref in a_refs], axis=0)
    value = nn(joined, grad_out)
    for r in range(4):
        for p in range(PIECES):
            spot = place(p ^ (dp % NEAR), DOWN_ORDER)
            piece = value[r * part + p * tall : r * part + (p + 1) * tall].astype(BF16)
            if r % 2:
                give_ref[r // 2, spot] = piece
            else:
                (far_ref if r else keep_ref)[spot] = piece
    sums_ref[0:1, :] = jnp.sum(grad_first * unit1, axis=0, keepdims=True)
    sums_ref[1:2, :] = jnp.sum(grad_first, axis=0, keepdims=True)
    sums_ref[2:3, :] = jnp.sum(grad_out.astype(F32), axis=0, keepdims=True)
    wait_all(copies)
    back = nt(wo[...].reshape(joined.shape[0], -1), grad_out).astype(BF16)
    for r in range(4):
        g_refs[r][...] = back[r * part : (r + 1) * part]


def shaped(*shape, dtype=BF16):
    return jax.ShapeDtypeStruct(shape, dtype)


def any_spec():
    return pl.BlockSpec(memory_space=pl.ANY)


def forward(place_word, attended, embedded, cotangent, vectors, up_bias, pieces):
    rows, features = embedded.shape
    part = attended[0].shape[0]
    size = features // PIECES
    term = [shaped(PIECES, size, features)] * 2 + [shaped(2, PIECES, size, features)]
    return pl.pallas_call(
        forward_kernel,
        in_specs=[pl.BlockSpec(memory_space=pltpu.SMEM)] + [whole_spec()] * 8 + [any_spec()] * 10,
        out_specs=[whole_spec()] * 6 + [any_spec()] * 6,
        out_shape=[
            shaped(rows, features),
            shaped(rows, features, dtype=F32),
            shaped(rows, 1, dtype=F32),
            shaped(rows, features, dtype=F32),
            shaped(3, features, dtype=F32),
            shaped(4, features, dtype=F32),
        ]
        + term
        + term,
        scratch_shapes=[
            pltpu.VMEM((4, part, features), BF16),
            pltpu.VMEM((4, features, features), BF16),
            pltpu.VMEM((4, features, features), BF16),
            pltpu.VMEM((4, rows, features), BF16),
            pltpu.VMEM((4, rows, features), F32),
            pltpu.VMEM((features, rows), BF16),
            pltpu.VMEM((features, rows), BF16),
            pltpu.VMEM((2, 4, PIECES, size, features), BF16),
            pltpu.SemaphoreType.DMA((44,)),
            pltpu.SemaphoreType.DMA((2, 4)),
        ],
        compiler_params=params(56),
        cost_estimate=pl.CostEstimate(
            flops=12 * rows * features * 4 * features,
            bytes_accessed=26 * 1024 * 1024,
            transcendentals=rows * 4 * features,
        ),
        name="forward",
    )(place_word, *attended, embedded, cotangent, vectors, up_bias, *pieces)


def backward(place_word, attended, unit, scale, grad, vectors, pieces):
    rows, features = unit.shape
    part = attended[0].shape[0]
    piece = (PIECES, part // PIECES, features)
    return pl.pallas_call(
        backward_kernel,
        in_specs=[pl.BlockSpec(memory_space=pltpu.SMEM)] + [whole_spec()] * 8 + [any_spec()] * 6,
        out_specs=[whole_spec()] * 9,
        out_shape=[shaped(rows, features, dtype=F32)]
        + [shaped(part, rows)] * 4
        + [shaped(3, features, dtype=F32), shaped(*piece), shaped(*piece), shaped(2, *piece)],
        scratch_shapes=[pltpu.VMEM((4, part, features), BF16), pltpu.SemaphoreType.DMA((44,))],
        compiler_params=params(56),
        cost_estimate=pl.CostEstimate(
            flops=4 * rows * features * features, bytes_accessed=6 * 1024 * 1024, transcendentals=rows
        ),
        name="backward",
    )(place_word, *attended, unit, scale, grad, vectors, *pieces)


def fold_kernel(*refs, body, inputs, waits):
    body(refs[:inputs], refs[inputs + waits :])


def fold(body, arrays, shapes, after, name):
    return pl.pallas_call(
        functools.partial(fold_kernel, body=body, inputs=len(arrays), waits=len(after)),
        in_specs=[whole_spec()] * len(arrays) + [any_spec()] * len(after),
        out_specs=[whole_spec()] * len(shapes),
        out_shape=[shaped(*shape) for shape in shapes],
        compiler_params=params(40),
        cost_estimate=pl.CostEstimate(flops=0, bytes_accessed=4 * 1024 * 1024, transcendentals=0),
        name=name,
    )(*arrays, *after)


def added(*values):
    return sum(v.astype(F32) for v in values[1:]) + values[0].astype(F32)


def fold_down_core(ins, outs):
    keeps, fars, gots = ins[0:2], ins[2:4], ins[4:6]
    size = keeps[0].shape[1]
    half = keeps[0].shape[0] // 2
    for i, mine in enumerate((keeps, fars)):
        for ref, got, rows in zip(mine, gots, (slice(0, size), slice(size, None))):
            total = added(ref[...], got[i]).astype(BF16)
            outs[0][:, i, rows] = total[:half]
            outs[1][:, i, rows] = total[half:]


def fold_up_core(ins, outs):
    keep, far, got = ins
    outs[0][...] = added(keep[...], got[0]).astype(BF16)
    outs[1][...] = added(far[...], got[1]).astype(BF16)


def fold_both(ins, outs):
    down, down_got, up, up_got = ins
    half = up.shape[0] // 2
    outs[0][...] = added(down[:, 0], down_got[:, 0]).astype(BF16)
    outs[1][...] = added(down[:, 1], down_got[:, 1]).astype(BF16)
    outs[2][...] = added(up[:half], up_got[:half]).astype(BF16)
    outs[3][...] = added(up[half:], up_got[half:]).astype(BF16)


def settle_kernel(place_ref, *refs, order, store):
    held, outs = refs[:2], refs[2:]
    seq, dp = place_ref[0], place_ref[1] % NEAR
    half = PIECES // 2
    for index in range(PIECES):
        spot = place(index, order)
        store(outs, held[spot // half].at[spot % half], index ^ dp, seq)


def store_down(outs, piece, p, seq):
    size, tall = (ref.shape[0] // PIECES for ref in outs)
    outs[0][pl.ds(pl.multiple_of(p * size, size), size), :] = piece[:size].astype(F32)
    outs[1][pl.ds(pl.multiple_of(p * tall, 8), tall), :] = piece[size:].astype(F32)


def store_up(outs, piece, p, seq):
    size, wide = piece.shape
    row, column = pl.multiple_of((p % 2) * size, size), pl.multiple_of((p // 2) * wide, wide)
    outs[0][pl.ds(row, size), pl.ds(column, wide)] = piece[...].astype(F32)


def store_heads(outs, piece, p, seq):
    tall, part = piece.shape[1], piece.shape[2] // 3
    rows = pl.ds(pl.multiple_of(p * tall, 8), tall)
    for c in range(4):
        columns = slice(c * part, (c + 1) * part)
        block = piece[seq ^ c].astype(F32)
        for i in range(3):
            outs[i][rows, columns] = block[:, i * part : (i + 1) * part]


def settle(place_word, held, order, store, shapes):
    return pl.pallas_call(
        functools.partial(settle_kernel, order=order, store=store),
        in_specs=[pl.BlockSpec(memory_space=pltpu.SMEM)] + [whole_spec()] * 2,
        out_specs=[whole_spec()] * len(shapes),
        out_shape=[jax.ShapeDtypeStruct(shape, F32) for shape in shapes],
        compiler_params=params(56),
        cost_estimate=pl.CostEstimate(flops=0, bytes_accessed=4 * 1024 * 1024, transcendentals=0),
        name="settle",
    )(place_word, *held)


def follow(x, *others):
    for other in others:
        x = x + jnp.minimum(jnp.abs(other[(0,) * other.ndim].astype(F32)), 0.0).astype(x.dtype)
    return x


def reduce_dp(x, orders):
    for by in orders:
        half = x.shape[0] // 2
        x = x[:half].astype(F32) + swap(x[half:].astype(BF16), "dp", by).astype(F32)
    return x


def reduce_rest(x, last):
    for by in (last, *bits("dp")[3:]):
        x = x.astype(BF16)
        x = x.astype(F32) + swap(x, "dp", by).astype(F32)
    return x.astype(BF16)


def spread_dp(x, order):
    for by in reversed(order[1:-1]):
        x = jnp.concatenate([x, swap(x, "dp", by)])
    return x, swap(x, "dp", order[0])


def body(
    text_embed,
    region_feature,
    token_mask,
    segment_mask,
    mask_vector,
    batch_gain,
    batch_shift,
    query_weight,
    query_bias,
    key_weight,
    value_weight,
    value_bias,
    output_weight,
    output_bias,
    first_gain,
    first_shift,
    up_weight,
    up_bias,
    down_weight,
    down_bias,
    second_gain,
    second_shift,
    cotangent,
):
    documents, span, features = text_embed.shape
    rows = documents * span
    seq, dp = lax.axis_index("seq"), lax.axis_index("dp")
    group = lax.axis_size("seq")
    population = rows * lax.axis_size("dp") * group
    score_scale = 1.0 / math.sqrt(HEAD_DIM)
    part = features // group
    heads = part // HEAD_DIM

    place_word = jnp.stack([seq, dp]).astype(jnp.int32)
    cut, halves, mine = pack(
        place_word, query_weight, key_weight, value_weight, output_weight, up_weight
    )

    region = region_feature.astype(F32).reshape(rows, features)
    sums = jnp.stack([jnp.sum(region, axis=0), jnp.sum(region * region, axis=0)])
    chip_sums = sums + swap(sums, "seq", 2)
    chip_sums = follow(chip_sums, cut[0], mine)
    sums = chip_sums + swap(chip_sums, "seq", 1)
    for by in bits("dp"):
        sums = sums + swap(sums, "dp", by)
    average = sums[0] / population
    inverse = lax.rsqrt(sums[1] / population - average * average + EPS_BATCH)

    head_blocks = exchange_blocks(cut)
    bias3 = jnp.stack([query_bias, jnp.zeros_like(query_bias), value_bias]).reshape(3, group, part)
    head_bias = lax.dynamic_slice_in_dim(bias3, seq, 1, 1)
    pieces = gather_weight(halves, mine, 1)

    standard = (region - average) * inverse
    token_hit = token_mask.astype(F32).reshape(rows, 1)
    segment_keep = 1.0 - segment_mask.astype(F32).reshape(rows, 1)
    embedded = (
        text_embed.astype(F32).reshape(rows, features) * (1.0 - token_hit)
        + token_hit * mask_vector
        + segment_keep * (standard * batch_gain + batch_shift)
    )
    low_in = follow(embedded, head_blocks[2], head_blocks[3]).astype(BF16).reshape(documents, span, features)
    x_blocks = gather_rows(low_in)
    far = swap(follow(down_weight, low_in, pieces[1]), "seq", 2)
    q, k, v, head_weight, *attended = attend(place_word, x_blocks, head_blocks, head_bias, [])
    attn_blocks = exchange_blocks(attended)
    far = follow(far, attended[0])
    pieces += [down_weight, swap(down_weight, "seq", 1), far, swap(far, "seq", 1)]
    vectors = jnp.stack([output_bias, first_gain, first_shift, down_bias, second_gain, second_shift])
    layer_output, unit, scale, grad_first, second_sums, up_sums, *terms = forward(
        place_word,
        attn_blocks,
        embedded,
        cotangent.reshape(rows, features),
        vectors,
        up_bias.reshape(group, features),
        pieces,
    )
    grad_residual, *rest = backward(place_word, attn_blocks, unit, scale, grad_first, vectors, pieces[:6])
    grad_attn, first_sums, (out_keep, out_far, out_give) = rest[:4], rest[4], rest[5:]
    down_keep, down_far, down_give = terms[:3]
    up_keep, up_far, up_give = terms[3:]

    half = PIECES // 2
    size, tall = features // PIECES, part // PIECES
    g_blocks = exchange_blocks(grad_attn)
    down, down_send = fold(
        fold_down_core,
        [down_keep, out_keep, down_far, out_far, swap(down_give, "seq", 1), swap(out_give, "seq", 1)],
        [(half, 2, size + tall, features)] * 2,
        [],
        "down_core",
    )
    up, up_send = fold(
        fold_up_core,
        [up_keep, up_far, swap(up_give, "seq", 1)],
        [(PIECES, size, features)] * 2,
        [g_blocks[2], g_blocks[3]],
        "up_core",
    )

    keep, give, heads, heads_send, head_sums = attend_back(
        place_word, g_blocks, x_blocks, q, k, v, head_weight, [down_send, up_send]
    )
    query_sums, value_sums = head_sums[0], head_sums[1]

    got = swap(give, "seq", 1)
    inner_send = (keep[1].astype(F32) + got[1].astype(F32)).astype(BF16)
    inner_own = keep[0].astype(F32) + got[0].astype(F32)

    down, down_send, up, up_send = fold(
        fold_both,
        [down, swap(down_send, "dp", DOWN_ORDER[0]), up, swap(up_send, "seq", 2)],
        [(half, size + tall, features)] * 2 + [(half, size, features)] * 2,
        [inner_send],
        "both",
    )
    own = up.astype(F32) + swap(up_send, "dp", UP_ORDER[0]).astype(F32)
    own = reduce_rest(reduce_dp(own, UP_ORDER[1:-1]), UP_ORDER[-1])
    (total_up,) = settle(place_word, spread_dp(own, UP_ORDER), UP_ORDER, store_up, [up_weight.shape])

    own = down.astype(F32) + swap(down_send, "seq", 2).astype(F32)
    own = reduce_rest(reduce_dp(own, DOWN_ORDER[1:-1]), DOWN_ORDER[-1])
    total_down, total_out = settle(
        place_word,
        spread_dp(own, DOWN_ORDER),
        DOWN_ORDER,
        store_down,
        [down_weight.shape, output_weight.shape],
    )

    inner = (inner_own + swap(inner_send, "seq", 2).astype(F32)).reshape(rows, features)
    heads = heads.astype(F32) + swap(heads_send, "dp", HEAD_ORDER[0]).astype(F32)
    own = reduce_rest(reduce_dp(heads, HEAD_ORDER[1:-1]), HEAD_ORDER[-1])
    own = jnp.stack(exchange_blocks([own[:, r] for r in range(group)]), axis=1)
    total_query, total_key, total_value = settle(
        place_word, spread_dp(own, HEAD_ORDER), HEAD_ORDER, store_heads, [query_weight.shape] * 3
    )

    grad_embedded = grad_residual + inner
    text_gradient = (grad_embedded * (1.0 - token_hit)).astype(BF16)
    grad_normed = grad_embedded * segment_keep

    def widen(x):
        return lax.dynamic_update_slice_in_dim(jnp.zeros((features,), F32), x, seq * part, 0)

    sums = sum_all(
        jnp.concatenate(
            [
                jnp.stack(
                    [
                        jnp.sum(grad_normed * standard, axis=0),
                        jnp.sum(grad_normed, axis=0),
                        jnp.sum(grad_embedded * token_hit, axis=0),
                        widen(query_sums),
                        widen(value_sums),
                    ]
                ),
                second_sums,
                first_sums,
                up_sums,
            ]
        )
    )
    (
        sum_gain,
        sum_shift,
        sum_mask,
        sum_query_bias,
        sum_value_bias,
        sum_second_gain,
        sum_second_shift,
        sum_down_bias,
        sum_first_gain,
        sum_first_shift,
        sum_output_bias,
    ) = sums[:11]
    sum_up_bias = sums[11:].reshape(-1)

    region_gradient = (
        batch_gain
        * inverse
        * (grad_normed - sum_shift / population - standard * (sum_gain / population))
    ).astype(BF16)
    shape = (documents, span, features)
    return (
        layer_output.reshape(shape),
        text_gradient.reshape(shape),
        region_gradient.reshape(shape),
        sum_mask,
        sum_gain,
        sum_shift,
        total_query,
        sum_query_bias,
        total_key,
        total_value,
        sum_value_bias,
        total_out,
        sum_output_bias,
        sum_first_gain,
        sum_first_shift,
        total_up,
        sum_up_bias,
        total_down,
        sum_down_bias,
        sum_second_gain,
        sum_second_shift,
    )


def solution(mesh):
    rows, weight, copied = P("dp", "seq", None), P("seq", None), P()
    mask = P("dp", "seq")
    in_specs = (
        (rows, rows, mask, mask, copied, copied, copied)
        + (weight, copied, weight, weight, copied, weight, copied, copied, copied)
        + (weight, copied, weight, copied, copied, copied, rows)
    )
    out_specs = (
        (rows, rows, rows, copied, copied, copied)
        + (weight, copied, weight, weight, copied, weight, copied, copied, copied)
        + (weight, copied, weight, copied, copied, copied)
    )
    return jax.shard_map(body, mesh=mesh, in_specs=in_specs, out_specs=out_specs, check_vma=False)
```

time: 350 us -> 316 us (0.903); the launches traced: 349 us -> 310 us
  waiting for transfers between devices: 168 us -> 131 us
  Pallas kernels: 69.2 us -> 81.1 us
  other arithmetic: 28.6 us -> 19 us
  starting transfers between devices: 62.1 us -> 53.1 us
  between operations: 1.59 us -> 6.32 us
    ppermute x59 -> x55, waiting for transfers between devices: 168 us -> 131 us  [swap(): lax.ppermute(x, axis, [(i, i ^ by) for i in range(lax.axis_size(axis))])]
    pallas_call x3 -> x9, Pallas kernels: 60.5 us -> 72.4 us  [the longest x1 25.3 us: forward(): pl.pallas_call(forward_kernel, in_specs=[pl.BlockSpec(memory_space=pltpu....]
    ppermute x59 -> x55, starting transfers between devices: 62.1 us -> 53.1 us  [swap(): lax.ppermute(x, axis, [(i, i ^ by) for i in range(lax.axis_size(axis))])]
    slice x0 -> x7, local copies, waits for them, and re-layouts: none -> 6.58 us  [follow(): other[(0,) * other.ndim].astype(F32)]
    add x9 -> x11, other arithmetic: 8.23 us -> 5.22 us  [the longest x3 3.55 us: follow(): x + jnp.minimum(jnp.abs(other[(0,) * other.ndim].astype(F32)), 0.0).astyp...]
    unnamed x110 -> x112, local copies, waits for them, and re-layouts: 6.91 us -> 8.9 us
  transfers between devices with their start and end apart: 59 -> 55, of which waited for: 23 -> 25; matrix products, arithmetic and copies ran while one was open for 12% -> 9% of each run, Pallas kernels for 10% -> 17%
where the time goes in v1:
time: 316 us; the launch traced here: 310 us
  waiting for transfers between devices  131 us (41%)
  Pallas kernels  81.1 us (26%)
  starting transfers between devices  53.1 us (17%)
  local copies, waits for them, and re-layouts  19.5 us (6%)
  other arithmetic  19 us (6%)
  between operations  6.32 us (2%)
    ppermute x55, waiting for transfers between devices, swap(): lax.ppermute(x, axis, [(i, i ^ by) for i in range(lax.axis_size(axis))])  131 us
    ppermute x55, starting transfers between devices, swap(): lax.ppermute(x, axis, [(i, i ^ by) for i in range(lax.axis_size(axis))])  53.1 us
    pallas_call x1, Pallas kernels, forward(): pl.pallas_call(forward_kernel, in_specs=[pl.BlockSpec(memory_space=pltpu....  25.3 us
    pallas_call x1, Pallas kernels, attend_back(): pl.pallas_call(functools.partial(attend_back_kernel, waits=len(after)), g...  18.3 us
    pallas_call x1, Pallas kernels, attend(): pl.pallas_call(functools.partial(attend_kernel, waits=len(after)), grid=(...  11.1 us
    unnamed x112, local copies, waits for them, and re-layouts  8.9 us
    pallas_call x3, Pallas kernels, settle(): pl.pallas_call(functools.partial(settle_kernel, order=order, store=store)...  8.65 us
    slice x7, local copies, waits for them, and re-layouts, follow(): other[(0,) * other.ndim].astype(F32)  6.58 us
  transfers between devices with their start and end apart: 55, of which 25 were waited for; matrix products, arithmetic and copies ran while one was open for 9% of the time, Pallas kernels for 17%

profile of v1, /device:TPU:0, one launch (start us, length us, event | category | flops | bytes accessed | tf_op | source)
XLA Modules:
  0.0 310.0 jit_solution(10838906516931340603)
XLA Ops:
  1.9 3.0 collective-permute-start
  5.6 2.6 pack_heads.1
  10.2 2.9 pack_halves.1
  24.6 2.6 collective-permute-start.4
  29.1 10.8 %collective-permute-done.5.refs_6_ = bf16[192,576]{1,0:T(8,128)(2,1)S(1)} collective-permute-done((bf16[192,576]{1,0:T(8,128)(2,1)S(1)}, bf16[192,576]{1,0:T(8,128)(2,1)S(1)}, u32[]{:S(2)}, u32[]{:S(2)}) %collective-permute-start.5) | collective-permute-done | bytes 221216 | tf_op jit(solution)/shard_map/ppermute | solution.py:26
  41.1 3.2 %collective-permute-done.6.refs_7_ = bf16[192,576]{1,0:T(8,128)(2,1)S(1)} collective-permute-done((bf16[192,576]{1,0:T(8,128)(2,1)S(1)}, bf16[192,576]{1,0:T(8,128)(2,1)S(1)}, u32[]{:S(2)}, u32[]{:S(2)}) %collective-permute-start.6) | collective-permute-done | bytes 221216 | tf_op jit(solution)/shard_map/ppermute | solution.py:26
  53.3 10.1 %collective-permute-done.8.refs_2_.refs_6_ = bf16[3,128,768]{2,1,0:T(8,128)(2,1)} collective-permute-done((bf16[3,128,768]{2,1,0:T(8,128)(2,1)}, bf16[3,128,768]{2,1,0:T(8,128)(2,1)}, u32[]{:S(2)}, u32[]{:S(2)}) %collective-permute-start.8) | collective-permute-done | bytes 589856 | tf_op jit(solution)/shard_map/ppermute | solution.py:26
  68.1 11.1 %attend.1 = (bf16[3,512,192]{2,1,0:T(8,128)(2,1)}, bf16[3,512,192]{2,1,0:T(8,128)(2,1)}, bf16[3,512,192]{2,1,0:T(8,128)(2,1)}, bf16[3,768,192]{2,1,0:T(8,128)(2,...) custom-call(s32[2]{0:T(128)} %pad_add_fusion.place_ref.seq_ref, ...), custom_call_target="tpu_custom_call" | custom-call | flops 1962934272 | bytes 8388608 | tf_op jit(solution)/shard_map/attend/pallas_call | solution.py:186
  81.0 7.0 %collective-permute-done.20 = bf16[768,768]{1,0:T(8,128)(2,1)} collective-permute-done((bf16[768,768]{1,0:T(8,128)(2,1)}, bf16[768,768]{1,0:T(8,128)(2,1)}, u32[]{:S(2)}, u32[]{:S(2)}) %collective-permute-start.20) | collective-permute-done | bytes 1179680 | tf_op jit(solution)/shard_map/ppermute | solution.py:26
  88.1 2.4 broadcast_add_fusion.refs_16_
  98.4 3.7 %collective-permute-done.12.refs_2_ = bf16[192,384]{1,0:T(8,128)(2,1)S(1)} collective-permute-done((bf16[192,384]{1,0:T(8,128)(2,1)}, bf16[192,384]{1,0:T(8,128)(2,1)S(1)}, u32[]{:S(2)}, u32[]{:S(2)}) %collective-permute-start.12) | collective-permute-done | bytes 147488 | tf_op jit(solution)/shard_map/ppermute | solution.py:26
  104.8 25.3 %forward.1 = (bf16[384,768]{1,0:T(8,128)(2,1)}, f32[384,768]{1,0:T(8,128)}, f32[384,1]{1,0:T(8,128)}, f32[384,768]{1,0:T(8,128)}, f32[3,768]{1,0:T(4,128)}, /*in...) custom-call(s32[2]{0:T(128)} %pad_add_fusion.place_ref.seq_ref, ...), custom_call_target="tpu_custom_call" | custom-call | flops 10871635968 | bytes 27262976 | tf_op jit(solution)/shard_map/forward/pallas_call | solution.py:489
  130.7 6.6 %backward.1 = (f32[384,768]{1,0:T(8,128)}, bf16[192,384]{1,0:T(8,128)(2,1)}, bf16[192,384]{1,0:T(8,128)(2,1)}, bf16[192,384]{1,0:T(8,128)(2,1)}, bf16[192,384]{1...) custom-call(s32[2]{0:T(128)} %pad_add_fusion.place_ref.seq_ref, ...), custom_call_target="tpu_custom_call" | custom-call | flops 905969664 | bytes 6291456 | tf_op jit(solution)/shard_map/backward/pallas_call | solution.py:529
  149.6 18.3 %attend_back.1 = (bf16[2,3,128,768]{3,2,1,0:T(8,128)(2,1)}, bf16[2,3,128,768]{3,2,1,0:T(8,128)(2,1)}, bf16[4,4,24,576]{3,2,1,0:T(8,128)(2,1)}, bf16[4,4,24,576]{3,2,1,0:T(8,128)(2,1)}, f32[2,192]{1,0:T(2,128)}) custom-call(s32[2]{0:T(128)} %pad_add_fusion.place_ref.seq_ref, bf16[192,384]{1,0:T(8,128)(2,1)} %get-tuple-element.89.refs_0_, ...), custom_call_target="tpu_custom_call" | custom-call | flops 4227858432 | bytes 12582912 | tf_op jit(solution)/shard_map/attend_back/pallas_call | solution.py:285
  171.1 11.5 %collective-permute-done.35 = bf16[4,4,24,576]{3,2,0,1:T(8,128)(2,1)S(1)} collective-permute-done((bf16[4,4,24,576]{3,2,0,1:T(8,128)(2,1)S(1)}, bf16[4,4,24,576]{3,2,0,1:T(8,128)(2,1)S(1)}, u32[]{:S(2)}, u32[]{:S(2)}) %collective-permute-start.35) | collective-permute-done | bytes 442400 | tf_op jit(solution)/shard_map/ppermute | solution.py:26
  185.4 6.0 %collective-permute-done.36 = bf16[2,4,24,576]{3,2,0,1:T(8,128)(2,1)S(1)} collective-permute-done((bf16[2,4,24,576]{3,2,0,1:T(8,128)(2,1)S(1)}, bf16[2,4,24,576]{3,2,0,1:T(8,128)(2,1)S(1)}, u32[]{:S(2)}, u32[]{:S(2)}) %collective-permute-start.36) | collective-permute-done | bytes 221216 | tf_op jit(solution)/shard_map/ppermute | solution.py:26
  192.5 2.7 collective-permute-start.37
  196.6 2.8 collective-permute-done.44.refs_3_
  199.3 2.5 both.1
  209.7 14.1 %collective-permute-done.39 = bf16[2,24,576]{2,1,0:T(8,128)(2,1)S(1)} collective-permute-done((bf16[2,24,576]{2,1,0:T(8,128)(2,1)S(1)}, bf16[2,24,576]{2,1,0:T(8,128)(2,1)S(1)}, u32[]{:S(2)}, u32[]{:S(2)}) %collective-permute-start.39) | collective-permute-done | bytes 55328 | tf_op jit(solution)/shard_map/ppermute | solution.py:26
  227.7 5.0 %collective-permute-done.41 = bf16[2,4,24,576]{3,2,1,0:T(8,128)(2,1)S(1)} collective-permute-done((bf16[2,4,24,576]{3,2,1,0:T(8,128)(2,1)S(1)}, bf16[2,4,24,576]{3,2,1,0:T(8,128)(2,1)S(1)}, u32[]{:S(2)}, u32[]{:S(2)}) %collective-permute-start.41) | collective-permute-done | bytes 221216 | tf_op jit(solution)/shard_map/ppermute | solution.py:26
  234.1 2.3 collective-permute-done.46
  236.5 2.6 collective-permute-start.47
  239.2 2.6 collective-permute-start.52
  243.0 19.7 %collective-permute-done.47 = bf16[2,120,768]{2,1,0:T(8,128)(2,1)S(1)} collective-permute-done((bf16[2,120,768]{2,1,0:T(8,128)(2,1)S(1)}, bf16[2,120,768]{2,1,0:T(8,128)(2,1)S(1)}, u32[]{:S(2)}, u32[]{:S(2)}) %collective-permute-start.47) | collective-permute-done | bytes 368672 | tf_op jit(solution)/shard_map/ppermute | solution.py:26
  263.6 3.5 %collective-permute-done.52 = bf16[2,96,768]{2,1,0:T(8,128)(2,1)S(1)} collective-permute-done((bf16[2,96,768]{2,1,0:T(8,128)(2,1)S(1)}, bf16[2,96,768]{2,1,0:T(8,128)(2,1)S(1)}, u32[]{:S(2)}, u32[]{:S(2)}) %collective-permute-start.52) | collective-permute-done | bytes 294944 | tf_op jit(solution)/shard_map/ppermute | solution.py:26
  279.3 10.9 %collective-permute-done.32 = f32[15,768]{1,0:T(8,128)S(1)} collective-permute-done((f32[15,768]{1,0:T(8,128)S(1)}, f32[15,768]{1,0:T(8,128)S(1)}, u32[]{:S(2)}, u32[]{:S(2)}) %collective-permute-start.32) | collective-permute-done | bytes 46112 | tf_op jit(solution)/shard_map/ppermute | solution.py:26
  292.2 2.3 collective-permute-done.33
  294.4 3.8 %collective-permute-start.34 = (f32[15,768]{1,0:T(8,128)S(1)}, f32[15,768]{1,0:T(8,128)S(1)}, u32[]{:S(2)}, u32[]{:S(2)}) collective-permute-start(f32[15,768]{1,0:T(8,128)S(1)} %add.198), channel_id=1, source_target_pairs={{0,16},{4,20},{8,24},{12,28},{16,0},{20,4},{24,8},{28,12},{1,17},{... | collective-permute-start | bytes 138248 | tf_op jit(solution)/shard_map/ppermute | solution.py:26
  298.3 2.6 settle.3
  303.7 2.9 settle.5
  306.6 3.1 %settle.4 = (f32[768,768]{1,0:T(8,128)}, f32[192,768]{1,0:T(8,128)}) custom-call(s32[2]{0:T(128)} %pad_add_fusion.place_ref.seq_ref, bf16[4,120,768]{2,1,0:T(8,128)(2,1)} %copy-done.17, bf16[4,120,768]{2,1,0:T(8,128)(2,1)} %collective-permute-done.49.refs_1_), custom_call_target="tpu_custom_call" | custom-call | bytes 4194304 | tf_op jit(solution)/shard_map/settle/pallas_call | solution.py:623
  (280 shorter events, 93.1 us)
Async XLA Ops:
  1.9 13.1 %collective-permute-start = (f32[2,768]{1,0:T(2,128)S(1)}, f32[2,768]{1,0:T(2,128)S(1)}, u32[]{:S(2)}, u32[]{:S(2)}) collective-permute-start(f32[2,768]{1,0:T(2,128)S(1)} %pad_maximum_fusion.4), channel_id=1, source_target_pairs={{0,2},{1,3},{2,0},{3,1},{4,6},{5,7},{6,4},{7,5},{8,10},{9,11},{10,... | collective-permute-start | bytes 18440 | tf_op jit(solution)/shard_map/ppermute | solution.py:26
  15.1 34.2 %collective-permute-start.14 = (bf16[480,768]{1,0:T(8,128)(2,1)}, bf16[480,768]{1,0:T(8,128)(2,1)S(1)}, u32[]{:S(2)}, u32[]{:S(2)}) collective-permute-start(bf16[480,768]{1,0:T(8,128)(2,1)} %get-tuple-element.75), channel_id=1, source_target_pairs={{0,2},{1,3},{2,0},{3,1},{4,6},{5,7},{6,4},{7,5},{8,10},{9,11},{10,... | collective-permute-start | bytes 2211848 | tf_op jit(solution)/shard_map/ppermute | solution.py:26
  15.2 24.7 %collective-permute-start.5 = (bf16[192,576]{1,0:T(8,128)(2,1)S(1)}, bf16[192,576]{1,0:T(8,128)(2,1)S(1)}, u32[]{:S(2)}, u32[]{:S(2)}) collective-permute-start(bf16[192,576]{1,0:T(8,128)(2,1)S(1)} %copy-done.54), channel_id=1, source_target_pairs={{0,2},{1,3},{2,0},{3,1},{4,6},{5,7},{6,4},{7,5},{8,10},{9,11},{10,... | collective-permute-start | bytes 663560 | tf_op jit(solution)/shard_map/ppermute | solution.py:26
  17.2 27.1 %collective-permute-start.6 = (bf16[192,576]{1,0:T(8,128)(2,1)S(1)}, bf16[192,576]{1,0:T(8,128)(2,1)S(1)}, u32[]{:S(2)}, u32[]{:S(2)}) collective-permute-start(bf16[192,576]{1,0:T(8,128)(2,1)S(1)} %copy-done.53), channel_id=1, source_target_pairs={{0,3},{1,2},{2,1},{3,0},{4,7},{5,6},{6,5},{7,4},{8,11},{9,10},{10,... | collective-permute-start | bytes 663560 | tf_op jit(solution)/shard_map/ppermute | solution.py:26
  46.9 16.5 %collective-permute-start.8 = (bf16[3,128,768]{2,1,0:T(8,128)(2,1)}, bf16[3,128,768]{2,1,0:T(8,128)(2,1)}, u32[]{:S(2)}, u32[]{:S(2)}) collective-permute-start(bf16[3,128,768]{2,1,0:T(8,128)(2,1)} %add_convert_fusion.1.refs_0_.refs_4_), channel_id=1, source_target_pairs={{0,2},{1,3},{2,0},{3,1},{4,6},{5,7},{6,4},{7,5},{8,10},{9,11},{10,... | collective-permute-start | bytes 1769480 | tf_op jit(solution)/shard_map/ppermute | solution.py:26
  51.7 36.3 %collective-permute-start.20 = (bf16[768,768]{1,0:T(8,128)(2,1)}, bf16[768,768]{1,0:T(8,128)(2,1)}, u32[]{:S(2)}, u32[]{:S(2)}) collective-permute-start(bf16[768,768]{1,0:T(8,128)(2,1)} %add_add_fusion), channel_id=1, source_target_pairs={{0,2},{1,3},{2,0},{3,1},{4,6},{5,7},{6,4},{7,5},{8,10},{9,11},{10,... | collective-permute-start | bytes 3538952 | tf_op jit(solution)/shard_map/ppermute | solution.py:26
  53.3 13.3 %collective-permute-start.7 = (bf16[3,128,768]{2,1,0:T(8,128)(2,1)}, bf16[3,128,768]{2,1,0:T(8,128)(2,1)}, u32[]{:S(2)}, u32[]{:S(2)}) collective-permute-start(bf16[3,128,768]{2,1,0:T(8,128)(2,1)} %add_convert_fusion.1.refs_0_.refs_4_), channel_id=1, source_target_pairs={{0,1},{1,0},{2,3},{3,2},{4,5},{5,4},{6,7},{7,6},{8,9},{9,8},{10,11... | collective-permute-start | bytes 1769480 | tf_op jit(solution)/shard_map/ppermute | solution.py:26
  63.9 31.6 %collective-permute-start.16 = (bf16[2,480,768]{2,1,0:T(8,128)(2,1)S(1)}, bf16[2,480,768]{2,1,0:T(8,128)(2,1)}, u32[]{:S(2)}, u32[]{:S(2)}) collective-permute-start(bf16[2,480,768]{2,1,0:T(8,128)(2,1)S(1)} %copy-done.20), channel_id=1, source_target_pairs={{0,1},{1,0},{2,3},{3,2},{4,5},{5,4},{6,7},{7,6},{8,9},{9,8},{10,11... | collective-permute-start | bytes 4423688 | tf_op jit(solution)/shard_map/ppermute | solution.py:26
  66.4 26.0 %collective-permute-start.19 = (bf16[768,768]{1,0:T(8,128)(2,1)}, bf16[768,768]{1,0:T(8,128)(2,1)}, u32[]{:S(2)}, u32[]{:S(2)}) collective-permute-start(bf16[768,768]{1,0:T(8,128)(2,1)} %refs_14_.1), channel_id=1, source_target_pairs={{0,1},{1,0},{2,3},{3,2},{4,5},{5,4},{6,7},{7,6},{8,9},{9,8},{10,11... | collective-permute-start | bytes 3538952 | tf_op jit(solution)/shard_map/ppermute | solution.py:26
  66.6 24.4 %collective-permute-start.15 = (bf16[480,768]{1,0:T(8,128)(2,1)S(1)}, bf16[480,768]{1,0:T(8,128)(2,1)}, u32[]{:S(2)}, u32[]{:S(2)}) collective-permute-start(bf16[480,768]{1,0:T(8,128)(2,1)S(1)} %collective-permute-done.14.refs_9_), channel_id=1, source_target_pairs={{0,4},{4,0},{8,12},{12,8},{16,20},{20,16},{24,28},{28,24},{1,5},{5... | collective-permute-start | bytes 2211848 | tf_op jit(solution)/shard_map/ppermute | solution.py:26
  90.5 13.7 %collective-permute-start.21 = (bf16[768,768]{1,0:T(8,128)(2,1)}, bf16[768,768]{1,0:T(8,128)(2,1)}, u32[]{:S(2)}, u32[]{:S(2)}) collective-permute-start(bf16[768,768]{1,0:T(8,128)(2,1)} %broadcast_add_fusion.refs_16_), channel_id=1, source_target_pairs={{0,1},{1,0},{2,3},{3,2},{4,5},{5,4},{6,7},{7,6},{8,9},{9,8},{10,11... | collective-permute-start | bytes 3538952 | tf_op jit(solution)/shard_map/ppermute | solution.py:26
  91.0 13.1 %collective-permute-start.18 = (bf16[480,768]{1,0:T(8,128)(2,1)}, bf16[480,768]{1,0:T(8,128)(2,1)}, u32[]{:S(2)}, u32[]{:S(2)}) collective-permute-start(bf16[480,768]{1,0:T(8,128)(2,1)} %collective-permute-done.15.refs_10_), channel_id=1, source_target_pairs={{0,1},{1,0},{2,3},{3,2},{4,5},{5,4},{6,7},{7,6},{8,9},{9,8},{10,11... | collective-permute-start | bytes 2211848 | tf_op jit(solution)/shard_map/ppermute | solution.py:26
  130.1 9.8 %collective-permute-start.25 = (bf16[2,8,96,768]{3,2,1,0:T(8,128)(2,1)}, bf16[2,8,96,768]{3,2,1,0:T(8,128)(2,1)S(1)}, u32[]{:S(2)}, u32[]{:S(2)}) collective-permute-start(bf16[2,8,96,768]{3,2,1,0:T(8,128)(2,1)} %get-tuple-element.101), channel_id=1, source_target_pairs={{0,1},{1,0},{2,3},{3,2},{4,5},{5,4},{6,7},{7,6},{8,9},{9,8},{10,11... | collective-permute-start | bytes 7077896 | tf_op jit(solution)/shard_map/ppermute | solution.py:26
  130.5 15.9 %collective-permute-start.27 = (bf16[2,8,96,768]{3,2,1,0:T(8,128)(2,1)}, bf16[2,8,96,768]{3,2,1,0:T(8,128)(2,1)S(1)}, u32[]{:S(2)}, u32[]{:S(2)}) collective-permute-start(bf16[2,8,96,768]{3,2,1,0:T(8,128)(2,1)} %get-tuple-element.106), channel_id=1, source_target_pairs={{0,1},{1,0},{2,3},{3,2},{4,5},{5,4},{6,7},{7,6},{8,9},{9,8},{10,11... | collective-permute-start | bytes 7077896 | tf_op jit(solution)/shard_map/ppermute | solution.py:26
  144.8 54.5 %collective-permute-start.43 = (bf16[4,2,120,768]{3,2,1,0:T(8,128)(2,1)}, bf16[4,2,120,768]{3,2,1,0:T(8,128)(2,1)S(1)}, u32[]{:S(2)}, u32[]{:S(2)}) collective-permute-start(bf16[4,2,120,768]{3,2,1,0:T(8,128)(2,1)} %get-tuple-element.103.refs_12_), channel_id=1, source_target_pairs={{0,8},{4,12},{8,0},{12,4},{16,24},{20,28},{24,16},{28,20},{1,9},{5... | collective-permute-start | bytes 4423688 | tf_op jit(solution)/shard_map/ppermute | solution.py:26
  169.1 13.5 %collective-permute-start.35 = (bf16[4,4,24,576]{3,2,0,1:T(8,128)(2,1)S(1)}, bf16[4,4,24,576]{3,2,0,1:T(8,128)(2,1)S(1)}, u32[]{:S(2)}, u32[]{:S(2)}) collective-permute-start(bf16[4,4,24,576]{3,2,0,1:T(8,128)(2,1)S(1)} %copy.45), channel_id=1, source_target_pairs={{0,4},{4,0},{8,12},{12,8},{16,20},{20,16},{24,28},{28,24},{1,5},{5... | collective-permute-start | bytes 1327112 | tf_op jit(solution)/shard_map/ppermute | solution.py:26
  170.6 24.6 %collective-permute-start.28 = (bf16[2,3,128,768]{3,2,1,0:T(8,128)(2,1)}, bf16[2,3,128,768]{3,2,1,0:T(8,128)(2,1)}, u32[]{:S(2)}, u32[]{:S(2)}) collective-permute-start(bf16[2,3,128,768]{3,2,1,0:T(8,128)(2,1)} %get-tuple-element.109), channel_id=1, source_target_pairs={{0,1},{1,0},{2,3},{3,2},{4,5},{5,4},{6,7},{7,6},{8,9},{9,8},{10,11... | collective-permute-start | bytes 3538952 | tf_op jit(solution)/shard_map/ppermute | solution.py:26
  170.7 28.6 %collective-permute-start.44 = (bf16[8,96,768]{2,1,0:T(8,128)(2,1)}, bf16[8,96,768]{2,1,0:T(8,128)(2,1)}, u32[]{:S(2)}, u32[]{:S(2)}) collective-permute-start(bf16[8,96,768]{2,1,0:T(8,128)(2,1)} %get-tuple-element.107.refs_13_), channel_id=1, source_target_pairs={{0,2},{1,3},{2,0},{3,1},{4,6},{5,7},{6,4},{7,5},{8,10},{9,11},{10,... | collective-permute-start | bytes 3538952 | tf_op jit(solution)/shard_map/ppermute | solution.py:26
  192.5 13.0 %collective-permute-start.37 = (bf16[2,4,24,576]{3,2,0,1:T(8,128)(2,1)S(1)}, bf16[2,4,24,576]{3,2,0,1:T(8,128)(2,1)S(1)}, u32[]{:S(2)}, u32[]{:S(2)}) collective-permute-start(bf16[2,4,24,576]{3,2,0,1:T(8,128)(2,1)S(1)} %fusion.6), channel_id=1, source_target_pairs={{0,16},{4,20},{8,24},{12,28},{16,0},{20,4},{24,8},{28,12},{1,17},{... | collective-permute-start | bytes 663560 | tf_op jit(solution)/shard_map/ppermute | solution.py:26
  203.6 21.8 %collective-permute-start.45 = (bf16[4,120,768]{2,1,0:T(8,128)(2,1)}, bf16[4,120,768]{2,1,0:T(8,128)(2,1)S(1)}, u32[]{:S(2)}, u32[]{:S(2)}) collective-permute-start(bf16[4,120,768]{2,1,0:T(8,128)(2,1)} %get-tuple-element.122), channel_id=1, source_target_pairs={{0,2},{1,3},{2,0},{3,1},{4,6},{5,7},{6,4},{7,5},{8,10},{9,11},{10,... | collective-permute-start | bytes 2211848 | tf_op jit(solution)/shard_map/ppermute | solution.py:26
  205.7 18.1 %collective-permute-start.39 = (bf16[2,24,576]{2,1,0:T(8,128)(2,1)S(1)}, bf16[2,24,576]{2,1,0:T(8,128)(2,1)S(1)}, u32[]{:S(2)}, u32[]{:S(2)}) collective-permute-start(bf16[2,24,576]{2,1,0:T(8,128)(2,1)S(1)} %get-tuple-element.152), channel_id=1, source_target_pairs={{0,2},{1,3},{2,0},{3,1},{4,6},{5,7},{6,4},{7,5},{8,10},{9,11},{10,... | collective-permute-start | bytes 165896 | tf_op jit(solution)/shard_map/ppermute | solution.py:26
  206.5 17.3 %collective-permute-start.40 = (bf16[2,24,576]{2,1,0:T(8,128)(2,1)S(1)}, bf16[2,24,576]{2,1,0:T(8,128)(2,1)S(1)}, u32[]{:S(2)}, u32[]{:S(2)}) collective-permute-start(bf16[2,24,576]{2,1,0:T(8,128)(2,1)S(1)} %get-tuple-element.151), channel_id=1, source_target_pairs={{0,3},{1,2},{2,1},{3,0},{4,7},{5,6},{6,5},{7,4},{8,11},{9,10},{10,... | collective-permute-start | bytes 165896 | tf_op jit(solution)/shard_map/ppermute | solution.py:26
  207.6 18.6 %collective-permute-start.50 = (bf16[4,96,768]{2,1,0:T(8,128)(2,1)}, bf16[4,96,768]{2,1,0:T(8,128)(2,1)S(1)}, u32[]{:S(2)}, u32[]{:S(2)}) collective-permute-start(bf16[4,96,768]{2,1,0:T(8,128)(2,1)} %get-tuple-element.125), channel_id=1, source_target_pairs={{0,4},{4,0},{8,12},{12,8},{16,20},{20,16},{24,28},{28,24},{1,5},{5... | collective-permute-start | bytes 1769480 | tf_op jit(solution)/shard_map/ppermute | solution.py:26
  224.8 16.9 %collective-permute-start.29 = (bf16[3,128,768]{2,1,0:T(8,128)(2,1)S(1)}, bf16[3,128,768]{2,1,0:T(8,128)(2,1)S(1)}, u32[]{:S(2)}, u32[]{:S(2)}) collective-permute-start(bf16[3,128,768]{2,1,0:T(8,128)(2,1)S(1)} %fusion.4.refs_4_), channel_id=1, source_target_pairs={{0,2},{1,3},{2,0},{3,1},{4,6},{5,7},{6,4},{7,5},{8,10},{9,11},{10,... | collective-permute-start | bytes 1769480 | tf_op jit(solution)/shard_map/ppermute | solution.py:26
  225.6 10.8 %collective-permute-start.46 = (bf16[2,120,768]{2,1,0:T(8,128)(2,1)S(1)}, bf16[2,120,768]{2,1,0:T(8,128)(2,1)S(1)}, u32[]{:S(2)}, u32[]{:S(2)}) collective-permute-start(bf16[2,120,768]{2,1,0:T(8,128)(2,1)S(1)} %slice.168), channel_id=1, source_target_pairs={{0,4},{4,0},{8,12},{12,8},{16,20},{20,16},{24,28},{28,24},{1,5},{5... | collective-permute-start | bytes 1105928 | tf_op jit(solution)/shard_map/ppermute | solution.py:26
  226.6 12.5 %collective-permute-start.51 = (bf16[2,96,768]{2,1,0:T(8,128)(2,1)S(1)}, bf16[2,96,768]{2,1,0:T(8,128)(2,1)S(1)}, u32[]{:S(2)}, u32[]{:S(2)}) collective-permute-start(bf16[2,96,768]{2,1,0:T(8,128)(2,1)S(1)} %slice.169), channel_id=1, source_target_pairs={{0,8},{4,12},{8,0},{12,4},{16,24},{20,28},{24,16},{28,20},{1,9},{5... | collective-permute-start | bytes 884744 | tf_op jit(solution)/shard_map/ppermute | solution.py:26
  233.6 64.7 %collective-permute-start.42 = (bf16[4,4,24,576]{3,2,1,0:T(8,128)(2,1)}, bf16[4,4,24,576]{3,2,1,0:T(8,128)(2,1)}, u32[]{:S(2)}, u32[]{:S(2)}) collective-permute-start(bf16[4,4,24,576]{3,2,1,0:T(8,128)(2,1)} %pad_maximum_fusion.2.refs_0_), channel_id=1, source_target_pairs={{0,4},{4,0},{8,12},{12,8},{16,20},{20,16},{24,28},{28,24},{1,5},{5... | collective-permute-start | bytes 1327112 | tf_op jit(solution)/shard_map/ppermute | solution.py:26
  236.5 26.3 %collective-permute-start.47 = (bf16[2,120,768]{2,1,0:T(8,128)(2,1)S(1)}, bf16[2,120,768]{2,1,0:T(8,128)(2,1)S(1)}, u32[]{:S(2)}, u32[]{:S(2)}) collective-permute-start(bf16[2,120,768]{2,1,0:T(8,128)(2,1)S(1)} %fusion.3), channel_id=1, source_target_pairs={{0,16},{4,20},{8,24},{12,28},{16,0},{20,4},{24,8},{28,12},{1,17},{... | collective-permute-start | bytes 1105928 | tf_op jit(solution)/shard_map/ppermute | solution.py:26
  239.2 28.0 %collective-permute-start.52 = (bf16[2,96,768]{2,1,0:T(8,128)(2,1)S(1)}, bf16[2,96,768]{2,1,0:T(8,128)(2,1)S(1)}, u32[]{:S(2)}, u32[]{:S(2)}) collective-permute-start(bf16[2,96,768]{2,1,0:T(8,128)(2,1)S(1)} %fusion.5), channel_id=1, source_target_pairs={{0,16},{4,20},{8,24},{12,28},{16,0},{20,4},{24,8},{28,12},{1,17},{... | collective-permute-start | bytes 884744 | tf_op jit(solution)/shard_map/ppermute | solution.py:26
  271.6 35.0 %collective-permute-start.49 = (bf16[4,120,768]{2,1,0:T(8,128)(2,1)S(1)}, bf16[4,120,768]{2,1,0:T(8,128)(2,1)}, u32[]{:S(2)}, u32[]{:S(2)}) collective-permute-start(bf16[4,120,768]{2,1,0:T(8,128)(2,1)S(1)} %pad_maximum_fusion.refs_0_), channel_id=1, source_target_pairs={{0,8},{4,12},{8,0},{12,4},{16,24},{20,28},{24,16},{28,20},{1,9},{5... | collective-permute-start | bytes 2211848 | tf_op jit(solution)/shard_map/ppermute | solution.py:26
  277.2 26.5 %collective-permute-start.54 = (bf16[4,96,768]{2,1,0:T(8,128)(2,1)S(1)}, bf16[4,96,768]{2,1,0:T(8,128)(2,1)}, u32[]{:S(2)}, u32[]{:S(2)}) collective-permute-start(bf16[4,96,768]{2,1,0:T(8,128)(2,1)S(1)} %pad_maximum_fusion.1.refs_0_), channel_id=1, source_target_pairs={{0,4},{4,0},{8,12},{12,8},{16,20},{20,16},{24,28},{28,24},{1,5},{5... | collective-permute-start | bytes 1769480 | tf_op jit(solution)/shard_map/ppermute | solution.py:26
  279.2 11.1 %collective-permute-start.32 = (f32[15,768]{1,0:T(8,128)S(1)}, f32[15,768]{1,0:T(8,128)S(1)}, u32[]{:S(2)}, u32[]{:S(2)}) collective-permute-start(f32[15,768]{1,0:T(8,128)S(1)} %add.196), channel_id=1, source_target_pairs={{0,4},{4,0},{8,12},{12,8},{16,20},{20,16},{24,28},{28,24},{1,5},{5... | collective-permute-start | bytes 138248 | tf_op jit(solution)/shard_map/ppermute | solution.py:26
  (79 other events, 888.6 us)

commit v2 on v1

--- a/solution.py
+++ b/solution.py
@@ -32,13 +32,6 @@
         found.append(by)
         by *= 2
     return found
-
-
-def sum_all(x):
-    for axis in ("seq", "dp"):
-        for by in bits(axis):
-            x = x + swap(x, axis, by)
-    return x
 
 
 def nn(a, b):
@@ -458,7 +451,7 @@
     value = nn(joined, grad_out)
     for r in range(4):
         for p in range(PIECES):
-            spot = place(p ^ (dp % NEAR), DOWN_ORDER)
+            spot = place(p ^ (dp % NEAR), UP_ORDER)
             piece = value[r * part + p * tall : r * part + (p + 1) * tall].astype(BF16)
             if r % 2:
                 give_ref[r // 2, spot] = piece
@@ -563,20 +556,18 @@
 
 
 def fold_down_core(ins, outs):
-    keeps, fars, gots = ins[0:2], ins[2:4], ins[4:6]
-    size = keeps[0].shape[1]
-    half = keeps[0].shape[0] // 2
-    for i, mine in enumerate((keeps, fars)):
-        for ref, got, rows in zip(mine, gots, (slice(0, size), slice(size, None))):
-            total = added(ref[...], got[i]).astype(BF16)
-            outs[0][:, i, rows] = total[:half]
-            outs[1][:, i, rows] = total[half:]
+    keeps, got = ins[:2], ins[2]
+    half = got.shape[1] // 2
+    for i, mine in enumerate(keeps):
+        outs[0][:, i] = added(mine[:half], got[i, :half]).astype(BF16)
+        outs[1][:, i] = added(mine[half:], got[i, half:]).astype(BF16)
 
 
 def fold_up_core(ins, outs):
-    keep, far, got = ins
-    outs[0][...] = added(keep[...], got[0]).astype(BF16)
-    outs[1][...] = added(far[...], got[1]).astype(BF16)
+    size = ins[0].shape[1]
+    for keep, far, got, rows in ((*ins[:3], slice(0, size)), (*ins[3:], slice(size, None))):
+        outs[0][:, rows] = added(keep[...], got[0]).astype(BF16)
+        outs[1][:, rows] = added(far[...], got[1]).astype(BF16)
 
 
 def fold_both(ins, outs):
@@ -588,6 +579,19 @@
     outs[3][...] = added(up[half:], up_got[half:]).astype(BF16)
 
 
+def fold_half(ins, outs):
+    mine, got = ins
+    half = mine.shape[0] // 2
+    outs[0][...] = added(mine[:half], got[:half]).astype(BF16)
+    outs[1][...] = added(mine[half:], got[half:]).astype(BF16)
+
+
+def fold_inner(ins, outs):
+    mine, got = ins
+    for i in range(2):
+        outs[i][...] = added(mine[i], got[i]).astype(BF16)
+
+
 def settle_kernel(place_ref, *refs, order, store):
     held, outs = refs[:2], refs[2:]
     seq, dp = place_ref[0], place_ref[1] % NEAR
@@ -598,15 +602,16 @@
 
 
 def store_down(outs, piece, p, seq):
-    size, tall = (ref.shape[0] // PIECES for ref in outs)
-    outs[0][pl.ds(pl.multiple_of(p * size, size), size), :] = piece[:size].astype(F32)
+    size = piece.shape[0]
+    outs[0][pl.ds(pl.multiple_of(p * size, size), size), :] = piece[...].astype(F32)
+
+
+def store_up(outs, piece, p, seq):
+    size, wide = outs[0].shape[0] // 2, piece.shape[1]
+    tall = piece.shape[0] - size
+    row, column = pl.multiple_of((p % 2) * size, size), pl.multiple_of((p // 2) * wide, wide)
+    outs[0][pl.ds(row, size), pl.ds(column, wide)] = piece[:size].astype(F32)
     outs[1][pl.ds(pl.multiple_of(p * tall, 8), tall), :] = piece[size:].astype(F32)
-
-
-def store_up(outs, piece, p, seq):
-    size, wide = piece.shape
-    row, column = pl.multiple_of((p % 2) * size, size), pl.multiple_of((p // 2) * wide, wide)
-    outs[0][pl.ds(row, size), pl.ds(column, wide)] = piece[...].astype(F32)
 
 
 def store_heads(outs, piece, p, seq):
@@ -631,10 +636,20 @@
     )(place_word, *held)
 
 
-def follow(x, *others):
-    for other in others:
-        x = x + jnp.minimum(jnp.abs(other[(0,) * other.ndim].astype(F32)), 0.0).astype(x.dtype)
-    return x
+def gate_kernel(*refs):
+    pass
+
+
+def gate(x, *after):
+    return pl.pallas_call(
+        gate_kernel,
+        in_specs=[any_spec()] * (1 + len(after)),
+        out_specs=any_spec(),
+        out_shape=shaped(*x.shape, dtype=x.dtype),
+        input_output_aliases={0: 0},
+        cost_estimate=pl.CostEstimate(flops=0, bytes_accessed=0, transcendentals=0),
+        name="gate",
+    )(x, *after)
 
 
 def reduce_dp(x, orders):
@@ -644,17 +659,20 @@
     return x
 
 
-def reduce_rest(x, last):
+def reduce_rest(x, last, *after):
     for by in (last, *bits("dp")[3:]):
         x = x.astype(BF16)
-        x = x.astype(F32) + swap(x, "dp", by).astype(F32)
+        got = swap(x, "dp", by)
+        if after and by == last:
+            got = gate(got, *after)
+        x = x.astype(F32) + got.astype(F32)
     return x.astype(BF16)
 
 
-def spread_dp(x, order):
-    for by in reversed(order[1:-1]):
-        x = jnp.concatenate([x, swap(x, "dp", by)])
-    return x, swap(x, "dp", order[0])
+def spread_dp(x, first, last, *after):
+    got = swap(x, "dp", first)
+    x = jnp.concatenate([x, gate(got, *after) if after else got])
+    return x, swap(x, "dp", last)
 
 
 def body(
@@ -699,14 +717,16 @@
     region = region_feature.astype(F32).reshape(rows, features)
     sums = jnp.stack([jnp.sum(region, axis=0), jnp.sum(region * region, axis=0)])
     chip_sums = sums + swap(sums, "seq", 2)
-    chip_sums = follow(chip_sums, cut[0], mine)
+    chip_sums = gate(chip_sums, cut[0])
     sums = chip_sums + swap(chip_sums, "seq", 1)
+    head_blocks = exchange_blocks(cut)
     for by in bits("dp"):
+        if by == 4:
+            sums = gate(sums, head_blocks[2], head_blocks[3])
         sums = sums + swap(sums, "dp", by)
     average = sums[0] / population
     inverse = lax.rsqrt(sums[1] / population - average * average + EPS_BATCH)
 
-    head_blocks = exchange_blocks(cut)
     bias3 = jnp.stack([query_bias, jnp.zeros_like(query_bias), value_bias]).reshape(3, group, part)
     head_bias = lax.dynamic_slice_in_dim(bias3, seq, 1, 1)
     pieces = gather_weight(halves, mine, 1)
@@ -719,12 +739,12 @@
         + token_hit * mask_vector
         + segment_keep * (standard * batch_gain + batch_shift)
     )
-    low_in = follow(embedded, head_blocks[2], head_blocks[3]).astype(BF16).reshape(documents, span, features)
+    low_in = embedded.astype(BF16).reshape(documents, span, features)
     x_blocks = gather_rows(low_in)
-    far = swap(follow(down_weight, low_in, pieces[1]), "seq", 2)
+    far = swap(gate(down_weight, low_in, pieces[1]), "seq", 2)
     q, k, v, head_weight, *attended = attend(place_word, x_blocks, head_blocks, head_bias, [])
     attn_blocks = exchange_blocks(attended)
-    far = follow(far, attended[0])
+    far = gate(far, attn_blocks[3])
     pieces += [down_weight, swap(down_weight, "seq", 1), far, swap(far, "seq", 1)]
     vectors = jnp.stack([output_bias, first_gain, first_shift, down_bias, second_gain, second_shift])
     layer_output, unit, scale, grad_first, second_sums, up_sums, *terms = forward(
@@ -746,82 +766,99 @@
     g_blocks = exchange_blocks(grad_attn)
     down, down_send = fold(
         fold_down_core,
-        [down_keep, out_keep, down_far, out_far, swap(down_give, "seq", 1), swap(out_give, "seq", 1)],
-        [(half, 2, size + tall, features)] * 2,
-        [],
+        [down_keep, down_far, swap(down_give, "seq", 1)],
+        [(half, 2, size, features)] * 2,
+        [g_blocks[2], g_blocks[3]],
         "down_core",
     )
     up, up_send = fold(
         fold_up_core,
-        [up_keep, up_far, swap(up_give, "seq", 1)],
-        [(PIECES, size, features)] * 2,
-        [g_blocks[2], g_blocks[3]],
+        [up_keep, up_far, swap(up_give, "seq", 1), out_keep, out_far, swap(out_give, "seq", 1)],
+        [(PIECES, size + tall, features)] * 2,
+        [down_send],
         "up_core",
     )
 
     keep, give, heads, heads_send, head_sums = attend_back(
-        place_word, g_blocks, x_blocks, q, k, v, head_weight, [down_send, up_send]
+        place_word, g_blocks, x_blocks, q, k, v, head_weight, [up_send]
     )
     query_sums, value_sums = head_sums[0], head_sums[1]
 
-    got = swap(give, "seq", 1)
-    inner_send = (keep[1].astype(F32) + got[1].astype(F32)).astype(BF16)
-    inner_own = keep[0].astype(F32) + got[0].astype(F32)
-
+    heads_got = swap(heads_send, "dp", HEAD_ORDER[0])
     down, down_send, up, up_send = fold(
         fold_both,
         [down, swap(down_send, "dp", DOWN_ORDER[0]), up, swap(up_send, "seq", 2)],
-        [(half, size + tall, features)] * 2 + [(half, size, features)] * 2,
+        [(half, size, features)] * 2 + [(half, size + tall, features)] * 2,
+        [heads_got],
+        "both",
+    )
+    inner_own, inner_send = fold(
+        fold_inner, [keep, swap(give, "seq", 1)], [keep.shape[1:]] * 2, [up_send], "inner"
+    )
+    heads, heads_send = fold(
+        fold_half,
+        [heads, heads_got],
+        [(half // 2, group, tall, 3 * part)] * 2,
         [inner_send],
-        "both",
-    )
-    own = up.astype(F32) + swap(up_send, "dp", UP_ORDER[0]).astype(F32)
-    own = reduce_rest(reduce_dp(own, UP_ORDER[1:-1]), UP_ORDER[-1])
-    (total_up,) = settle(place_word, spread_dp(own, UP_ORDER), UP_ORDER, store_up, [up_weight.shape])
-
-    own = down.astype(F32) + swap(down_send, "seq", 2).astype(F32)
-    own = reduce_rest(reduce_dp(own, DOWN_ORDER[1:-1]), DOWN_ORDER[-1])
-    total_down, total_out = settle(
-        place_word,
-        spread_dp(own, DOWN_ORDER),
-        DOWN_ORDER,
-        store_down,
-        [down_weight.shape, output_weight.shape],
-    )
-
-    inner = (inner_own + swap(inner_send, "seq", 2).astype(F32)).reshape(rows, features)
-    heads = heads.astype(F32) + swap(heads_send, "dp", HEAD_ORDER[0]).astype(F32)
-    own = reduce_rest(reduce_dp(heads, HEAD_ORDER[1:-1]), HEAD_ORDER[-1])
-    own = jnp.stack(exchange_blocks([own[:, r] for r in range(group)]), axis=1)
-    total_query, total_key, total_value = settle(
-        place_word, spread_dp(own, HEAD_ORDER), HEAD_ORDER, store_heads, [query_weight.shape] * 3
-    )
-
-    grad_embedded = grad_residual + inner
+        "heads",
+    )
+    up = up.astype(F32) + gate(swap(up_send, "dp", UP_ORDER[0]), heads_send).astype(F32)
+    down = down.astype(F32) + gate(swap(down_send, "seq", 2), up).astype(F32)
+    heads = heads.astype(F32) + gate(swap(heads_send, "dp", HEAD_ORDER[1]), up).astype(F32)
+    inner_got = swap(inner_send, "seq", 2)
+    quarter = half // 2
+    got = gate(swap(up[quarter:].astype(BF16), "dp", UP_ORDER[1]), inner_got, down)
+    up = up[:quarter] + got.astype(F32)
+    down = reduce_dp(down, DOWN_ORDER[1:-1])
+
+    inner = inner_own.astype(F32) + inner_got.astype(F32)
+    grad_embedded = grad_residual + inner.reshape(rows, features)
     text_gradient = (grad_embedded * (1.0 - token_hit)).astype(BF16)
     grad_normed = grad_embedded * segment_keep
 
     def widen(x):
         return lax.dynamic_update_slice_in_dim(jnp.zeros((features,), F32), x, seq * part, 0)
 
-    sums = sum_all(
-        jnp.concatenate(
-            [
-                jnp.stack(
-                    [
-                        jnp.sum(grad_normed * standard, axis=0),
-                        jnp.sum(grad_normed, axis=0),
-                        jnp.sum(grad_embedded * token_hit, axis=0),
-                        widen(query_sums),
-                        widen(value_sums),
-                    ]
-                ),
-                second_sums,
-                first_sums,
-                up_sums,
-            ]
-        )
-    )
+    sums = jnp.concatenate(
+        [
+            jnp.stack(
+                [
+                    jnp.sum(grad_normed * standard, axis=0),
+                    jnp.sum(grad_normed, axis=0),
+                    jnp.sum(grad_embedded * token_hit, axis=0),
+                    widen(query_sums),
+                    widen(value_sums),
+                ]
+            ),
+            second_sums,
+            first_sums,
+            up_sums,
+        ]
+    )
+    for by in bits("seq"):
+        sums = sums + swap(sums, "seq", by)
+
+    own = reduce_rest(heads, HEAD_ORDER[-1], up, down)
+    own = jnp.stack(exchange_blocks([own[:, r] for r in range(group)]), axis=1)
+    held_heads = spread_dp(own, 1, 2)
+    total_query, total_key, total_value = settle(
+        place_word, held_heads, (2, 1, 4), store_heads, [query_weight.shape] * 3
+    )
+
+    up = reduce_rest(up, UP_ORDER[-1], sums)
+    sums = sums + swap(sums, "dp", 1)
+    down = reduce_rest(down, DOWN_ORDER[-1], up, sums)
+    total_up, total_out = settle(
+        place_word, spread_dp(up, 2, 1, down), (1, 2, 4), store_up, [up_weight.shape, output_weight.shape]
+    )
+    (total_down,) = settle(
+        place_word, spread_dp(down, 1, 2, held_heads[1]), (2, 1, 4), store_down, [down_weight.shape]
+    )
+
+    for by, ready in zip(bits("dp")[1:], (total_query, total_up)):
+        sums = sums + gate(swap(sums, "dp", by), ready)
+    for by in bits("dp")[3:]:
+        sums = sums + swap(sums, "dp", by)
     (
         sum_gain,
         sum_shift,

time: 316 us -> 307 us (0.972)
  waiting for transfers between devices: 131 us -> 122 us
  starting transfers between devices: 53.1 us -> 44.7 us
  other arithmetic: 19 us -> 25.8 us
  local copies, waits for them, and re-layouts: 19.5 us -> 25.6 us
  between operations: 6.32 us -> 1.74 us
    unnamed x112 -> x157, local copies, waits for them, and re-layouts: 8.9 us -> 21.2 us
    ppermute x55, waiting for transfers between devices: 131 us -> 122 us  [swap(): lax.ppermute(x, axis, [(i, i ^ by) for i in range(lax.axis_size(axis))])]
    ppermute x55, starting transfers between devices: 53.1 us -> 44.7 us  [swap(): lax.ppermute(x, axis, [(i, i ^ by) for i in range(lax.axis_size(axis))])]
    slice x7 -> x1, local copies, waits for them, and re-layouts: 6.58 us -> 0.04 us  [body(): up[quarter:].astype(BF16)]
    convert_element_type x3, other arithmetic: 0.23 us -> 4.74 us  [reduce_rest(): return x.astype(BF16)]
  transfers between devices with their start and end apart: 55 -> 55, of which waited for: 25 -> 25; matrix products, arithmetic and copies ran while one was open for 9% -> 8% of each run, Pallas kernels for 17% -> 18%
where the time goes in v2:
time: 307 us; the launch traced here: 301 us
  waiting for transfers between devices  122 us (40%)
  Pallas kernels  81.5 us (27%)
  starting transfers between devices  44.7 us (15%)
  other arithmetic  25.8 us (8%)
  local copies, waits for them, and re-layouts  25.6 us (8%)
    ppermute x55, waiting for transfers between devices, swap(): lax.ppermute(x, axis, [(i, i ^ by) for i in range(lax.axis_size(axis))])  122 us
    ppermute x55, starting transfers between devices, swap(): lax.ppermute(x, axis, [(i, i ^ by) for i in range(lax.axis_size(axis))])  44.7 us
    pallas_call x1, Pallas kernels, forward(): pl.pallas_call(forward_kernel, in_specs=[pl.BlockSpec(memory_space=pltpu....  25.2 us
    unnamed x157, local copies, waits for them, and re-layouts  21.2 us
    pallas_call x1, Pallas kernels, attend_back(): pl.pallas_call(functools.partial(attend_back_kernel, waits=len(after)), g...  18.3 us
    pallas_call x1, Pallas kernels, attend(): pl.pallas_call(functools.partial(attend_kernel, waits=len(after)), grid=(...  11.1 us
    pallas_call x3, Pallas kernels, settle(): pl.pallas_call(functools.partial(settle_kernel, order=order, store=store)...  8.65 us
    pallas_call x1, Pallas kernels, backward(): pl.pallas_call(backward_kernel, in_specs=[pl.BlockSpec(memory_space=pltpu...  6.78 us
  transfers between devices with their start and end apart: 55, of which 25 were waited for; matrix products, arithmetic and copies ran while one was open for 8% of the time, Pallas kernels for 18%

profile of v2, /device:TPU:0, one launch (start us, length us, event | category | flops | bytes accessed | tf_op | source)
XLA Modules:
  0.0 301.3 jit_solution(5987575707016626670)
XLA Ops:
  1.9 3.0 %collective-permute-start = (f32[2,768]{1,0:T(2,128)S(1)}, f32[2,768]{1,0:T(2,128)S(1)}, u32[]{:S(2)}, u32[]{:S(2)}) collective-permute-start(f32[2,768]{1,0:T(2,128)S(1)} %pad_maximum_fusion.4), channel_id=1, source_target_pairs={{0,2},{1,3},{2,0},{3,1},{4,6},{5,7},{6,4},{7,5},{8,10},{9,11},{10,... | collective-permute-start | bytes 18440 | tf_op jit(solution)/shard_map/ppermute | solution.py:26
  5.6 2.5 pack_heads.1
  10.7 2.9 pack_halves.1
  23.4 2.6 collective-permute-start.6
  26.0 2.1 collective-permute-done.6
  31.0 2.4 copy.71.refs_0_
  33.4 5.6 %collective-permute-done.14.refs_2_.refs_9_ = bf16[480,768]{1,0:T(8,128)(2,1)S(1)} collective-permute-done((bf16[480,768]{1,0:T(8,128)(2,1)}, bf16[480,768]{1,0:T(8,128)(2,1)S(1)}, u32[]{:S(2)}, u32[]{:S(2)}) %collective-permute-start.14) | collective-permute-done | bytes 737312 | tf_op jit(solution)/shard_map/ppermute | solution.py:26
  40.3 11.4 %collective-permute-done.8.refs_2_.refs_6_ = bf16[3,128,768]{2,1,0:T(8,128)(2,1)} collective-permute-done((bf16[3,128,768]{2,1,0:T(8,128)(2,1)S(1)}, bf16[3,128,768]{2,1,0:T(8,128)(2,1)}, u32[]{:S(2)}, u32[]{:S(2)}) %collective-permute-start.8) | collective-permute-done | bytes 589856 | tf_op jit(solution)/shard_map/ppermute | solution.py:26
  57.7 11.1 %attend.1 = (bf16[3,512,192]{2,1,0:T(8,128)(2,1)}, bf16[3,512,192]{2,1,0:T(8,128)(2,1)}, bf16[3,512,192]{2,1,0:T(8,128)(2,1)}, bf16[3,768,192]{2,1,0:T(8,128)(2,...) custom-call(s32[2]{0:T(128)} %pad_add_fusion.place_ref.seq_ref, ...), custom_call_target="tpu_custom_call" | custom-call | flops 1962934272 | bytes 8388608 | tf_op jit(solution)/shard_map/attend/pallas_call | solution.py:179
  69.1 10.0 %collective-permute-done.13.refs_1_.refs_3_ = bf16[192,384]{1,0:T(8,128)(2,1)S(1)} collective-permute-done((bf16[192,384]{1,0:T(8,128)(2,1)}, bf16[192,384]{1,0:T(8,128)(2,1)S(1)}, u32[]{:S(2)}, u32[]{:S(2)}) %collective-permute-start.13) | collective-permute-done | bytes 147488 | tf_op jit(solution)/shard_map/ppermute | solution.py:26
  85.8 4.0 %collective-permute-done.12.refs_2_ = bf16[192,384]{1,0:T(8,128)(2,1)S(1)} collective-permute-done((bf16[192,384]{1,0:T(8,128)(2,1)S(1)}, bf16[192,384]{1,0:T(8,128)(2,1)S(1)}, u32[]{:S(2)}, u32[]{:S(2)}) %collective-permute-start.12) | collective-permute-done | bytes 147488 | tf_op jit(solution)/shard_map/ppermute | solution.py:26
  90.5 25.2 %forward.1 = (bf16[384,768]{1,0:T(8,128)(2,1)}, f32[384,768]{1,0:T(8,128)}, f32[384,1]{1,0:T(8,128)}, f32[384,768]{1,0:T(8,128)}, f32[3,768]{1,0:T(4,128)}, /*in...) custom-call(s32[2]{0:T(128)} %pad_add_fusion.place_ref.seq_ref, ...), custom_call_target="tpu_custom_call" | custom-call | flops 10871635968 | bytes 27262976 | tf_op jit(solution)/shard_map/forward/pallas_call | solution.py:482
  116.3 6.8 %backward.1 = (f32[384,768]{1,0:T(8,128)}, bf16[192,384]{1,0:T(8,128)(2,1)}, bf16[192,384]{1,0:T(8,128)(2,1)}, bf16[192,384]{1,0:T(8,128)(2,1)}, bf16[192,384]{1...) custom-call(s32[2]{0:T(128)} %pad_add_fusion.place_ref.seq_ref, ...), custom_call_target="tpu_custom_call" | custom-call | flops 905969664 | bytes 6291456 | tf_op jit(solution)/shard_map/backward/pallas_call | solution.py:522
  125.0 5.1 %collective-permute-done.23.refs_3_.refs_2_ = bf16[192,384]{1,0:T(8,128)(2,1)S(1)} collective-permute-done((bf16[192,384]{1,0:T(8,128)(2,1)}, bf16[192,384]{1,0:T(8,128)(2,1)S(1)}, u32[]{:S(2)}, u32[]{:S(2)}) %collective-permute-start.23) | collective-permute-done | bytes 147488 | tf_op jit(solution)/shard_map/ppermute | solution.py:26
  130.1 2.3 collective-permute-done.24.refs_4_.refs_3_
  140.4 18.3 %attend_back.1 = (bf16[2,3,128,768]{3,2,1,0:T(8,128)(2,1)}, bf16[2,3,128,768]{3,2,1,0:T(8,128)(2,1)}, bf16[4,4,24,576]{3,2,1,0:T(8,128)(2,1)}, bf16[4,4,24,576]{3,2,1,0:T(8,128)(2,1)}, f32[2,192]{1,0:T(2,128)}) custom-call(s32[2]{0:T(128)} %pad_add_fusion.place_ref.seq_ref, bf16[192,384]{1,0:T(8,128)(2,1)} %get-tuple-element.93.refs_0_, ...), custom_call_target="tpu_custom_call" | custom-call | flops 4227858432 | bytes 12582912 | tf_op jit(solution)/shard_map/attend_back/pallas_call | solution.py:278
  160.4 12.2 %collective-permute-done.31.refs_4_.refs_1_ = bf16[4,4,24,576]{3,2,1,0:T(8,128)(2,1)S(1)} collective-permute-done((bf16[4,4,24,576]{3,2,1,0:T(8,128)(2,1)}, bf16[4,4,24,576]{3,2,1,0:T(8,128)(2,1)S(1)}, u32[]{:S(2)}, u32[]{:S(2)}) %collective-permute-start.31) | collective-permute-done | bytes 442400 | tf_op jit(solution)/shard_map/ppermute | solution.py:26
  181.4 2.3 inner.1
  185.0 11.4 %collective-permute-done.38.refs_0_ = bf16[4,120,768]{2,1,0:T(8,128)(2,1)} collective-permute-done((bf16[4,120,768]{2,1,0:T(8,128)(2,1)S(1)}, bf16[4,120,768]{2,1,0:T(8,128)(2,1)}, u32[]{:S(2)}, u32[]{:S(2)}) %collective-permute-start.38) | collective-permute-done | bytes 737312 | tf_op jit(solution)/shard_map/ppermute | solution.py:26
  204.4 2.7 collective-permute-start.39
  208.4 8.5 %collective-permute-done.39 = bf16[2,4,24,576]{3,2,0,1:T(8,128)(2,1)S(1)} collective-permute-done((bf16[2,4,24,576]{3,2,0,1:T(8,128)(2,1)S(1)}, bf16[2,4,24,576]{3,2,0,1:T(8,128)(2,1)S(1)}, u32[]{:S(2)}, u32[]{:S(2)}) %collective-permute-start.39) | collective-permute-done | bytes 221216 | tf_op jit(solution)/shard_map/ppermute | solution.py:26
  225.4 2.3 collective-permute-done.44
  233.0 2.8 collective-permute-done.34
  237.4 2.6 collective-permute-done.35
  241.7 3.4 %collective-permute-start.47 = (bf16[4,4,24,576]{3,2,1,0:T(8,128)(2,1)S(1)}, bf16[4,4,24,576]{3,2,1,0:T(8,128)(2,1)S(1)}, u32[]{:S(2)}, u32[]{:S(2)}) collective-permute-start(bf16[4,4,24,576]{3,2,1,0:T(8,128)(2,1)S(1)} %pad_maximum_fusion.2.refs_0_), channel_id=1, source_target_pairs={{0,8},{4,12},{8,0},{12,4},{16,24},{20,28},{24,16},{28,20},{1,9},{5... | collective-permute-start | bytes 1327112 | tf_op jit(solution)/shard_map/ppermute | solution.py:26
  245.1 6.6 %collective-permute-done.49.refs_0_ = bf16[2,120,768]{2,1,0:T(8,128)(2,1)S(1)} collective-permute-done((bf16[2,120,768]{2,1,0:T(8,128)(2,1)S(1)}, bf16[2,120,768]{2,1,0:T(8,128)(2,1)S(1)}, u32[]{:S(2)}, u32[]{:S(2)}) %collective-permute-start.49) | collective-permute-done | bytes 368672 | tf_op jit(solution)/shard_map/ppermute | solution.py:26
  254.2 3.7 %collective-permute-done.51.refs_0_ = bf16[2,96,768]{2,1,0:T(8,128)(2,1)} collective-permute-done((bf16[2,96,768]{2,1,0:T(8,128)(2,1)}, bf16[2,96,768]{2,1,0:T(8,128)(2,1)}, u32[]{:S(2)}, u32[]{:S(2)}) %collective-permute-start.51) | collective-permute-done | bytes 294944 | tf_op jit(solution)/shard_map/ppermute | solution.py:26
  260.3 10.6 %collective-permute-done.50.refs_0_ = bf16[2,120,768]{2,1,0:T(8,128)(2,1)S(1)} collective-permute-done((bf16[2,120,768]{2,1,0:T(8,128)(2,1)}, bf16[2,120,768]{2,1,0:T(8,128)(2,1)S(1)}, u32[]{:S(2)}, u32[]{:S(2)}) %collective-permute-start.50) | collective-permute-done | bytes 368672 | tf_op jit(solution)/shard_map/ppermute | solution.py:26
  277.4 2.6 settle.3
  280.1 9.0 %collective-permute-done.36.refs_0_ = f32[15,768]{1,0:T(8,128)S(1)} collective-permute-done((f32[15,768]{1,0:T(8,128)S(1)}, f32[15,768]{1,0:T(8,128)S(1)}, u32[]{:S(2)}, u32[]{:S(2)}) %collective-permute-start.36) | collective-permute-done | bytes 46112 | tf_op jit(solution)/shard_map/ppermute | solution.py:26
  290.9 2.8 settle.5
  293.7 3.2 %settle.4 = (f32[192,3072]{1,0:T(8,128)}, f32[192,768]{1,0:T(8,128)}) custom-call(s32[2]{0:T(128)} %pad_add_fusion.place_ref.seq_ref, bf16[4,120,768]{2,1,0:T(8,128)(2,1)} %copy-done.24, bf16[4,120,768]{2,1,0:T(8,128)(2,1)} %collective-permute-done.52.refs_1_), custom_call_target="tpu_custom_call" | custom-call | bytes 4194304 | tf_op jit(solution)/shard_map/settle/pallas_call | solution.py:628
  (330 shorter events, 97.7 us)
Async XLA Ops:
  8.8 13.2 %collective-permute-start.4 = (bf16[192,576]{1,0:T(8,128)(2,1)}, bf16[192,576]{1,0:T(8,128)(2,1)S(1)}, u32[]{:S(2)}, u32[]{:S(2)}) collective-permute-start(bf16[192,576]{1,0:T(8,128)(2,1)} %get-tuple-element.79), channel_id=1, source_target_pairs={{0,2},{1,3},{2,0},{3,1},{4,6},{5,7},{6,4},{7,5},{8,10},{9,11},{10,... | collective-permute-start | bytes 663560 | tf_op jit(solution)/shard_map/ppermute | solution.py:26
  9.4 12.8 %collective-permute-start.5 = (bf16[192,576]{1,0:T(8,128)(2,1)}, bf16[192,576]{1,0:T(8,128)(2,1)S(1)}, u32[]{:S(2)}, u32[]{:S(2)}) collective-permute-start(bf16[192,576]{1,0:T(8,128)(2,1)} %get-tuple-element.80), channel_id=1, source_target_pairs={{0,3},{1,2},{2,1},{3,0},{4,7},{5,6},{6,5},{7,4},{8,11},{9,10},{10,... | collective-permute-start | bytes 663560 | tf_op jit(solution)/shard_map/ppermute | solution.py:26
  13.6 25.4 %collective-permute-start.14 = (bf16[480,768]{1,0:T(8,128)(2,1)}, bf16[480,768]{1,0:T(8,128)(2,1)S(1)}, u32[]{:S(2)}, u32[]{:S(2)}) collective-permute-start(bf16[480,768]{1,0:T(8,128)(2,1)} %get-tuple-element.87), channel_id=1, source_target_pairs={{0,2},{1,3},{2,0},{3,1},{4,6},{5,7},{6,4},{7,5},{8,10},{9,11},{10,... | collective-permute-start | bytes 2211848 | tf_op jit(solution)/shard_map/ppermute | solution.py:26
  29.4 22.3 %collective-permute-start.8 = (bf16[3,128,768]{2,1,0:T(8,128)(2,1)S(1)}, bf16[3,128,768]{2,1,0:T(8,128)(2,1)}, u32[]{:S(2)}, u32[]{:S(2)}) collective-permute-start(bf16[3,128,768]{2,1,0:T(8,128)(2,1)S(1)} %add_convert_fusion.refs_0_.refs_1_.refs_4_), channel_id=1, source_target_pairs={{0,2},{1,3},{2,0},{3,1},{4,6},{5,7},{6,4},{7,5},{8,10},{9,11},{10,... | collective-permute-start | bytes 1769480 | tf_op jit(solution)/shard_map/ppermute | solution.py:26
  39.8 39.3 %collective-permute-start.20 = (bf16[768,768]{1,0:T(8,128)(2,1)}, bf16[768,768]{1,0:T(8,128)(2,1)}, u32[]{:S(2)}, u32[]{:S(2)}) collective-permute-start(bf16[768,768]{1,0:T(8,128)(2,1)} %gate.17), channel_id=1, source_target_pairs={{0,2},{1,3},{2,0},{3,1},{4,6},{5,7},{6,4},{7,5},{8,10},{9,11},{10,... | collective-permute-start | bytes 3538952 | tf_op jit(solution)/shard_map/ppermute | solution.py:26
  40.3 15.0 %collective-permute-start.7 = (bf16[3,128,768]{2,1,0:T(8,128)(2,1)}, bf16[3,128,768]{2,1,0:T(8,128)(2,1)S(1)}, u32[]{:S(2)}, u32[]{:S(2)}) collective-permute-start(bf16[3,128,768]{2,1,0:T(8,128)(2,1)} %copy-done.27), channel_id=1, source_target_pairs={{0,1},{1,0},{2,3},{3,2},{4,5},{5,4},{6,7},{7,6},{8,9},{9,8},{10,11... | collective-permute-start | bytes 1769480 | tf_op jit(solution)/shard_map/ppermute | solution.py:26
  51.7 30.2 %collective-permute-start.19 = (bf16[768,768]{1,0:T(8,128)(2,1)}, bf16[768,768]{1,0:T(8,128)(2,1)}, u32[]{:S(2)}, u32[]{:S(2)}) collective-permute-start(bf16[768,768]{1,0:T(8,128)(2,1)} %refs_14_.1), channel_id=1, source_target_pairs={{0,1},{1,0},{2,3},{3,2},{4,5},{5,4},{6,7},{7,6},{8,9},{9,8},{10,11... | collective-permute-start | bytes 3538952 | tf_op jit(solution)/shard_map/ppermute | solution.py:26
  55.2 30.6 %collective-permute-start.16 = (bf16[2,480,768]{2,1,0:T(8,128)(2,1)}, bf16[2,480,768]{2,1,0:T(8,128)(2,1)}, u32[]{:S(2)}, u32[]{:S(2)}) collective-permute-start(bf16[2,480,768]{2,1,0:T(8,128)(2,1)} %get-tuple-element.86.refs_8_), channel_id=1, source_target_pairs={{0,1},{1,0},{2,3},{3,2},{4,5},{5,4},{6,7},{7,6},{8,9},{9,8},{10,11... | collective-permute-start | bytes 4423688 | tf_op jit(solution)/shard_map/ppermute | solution.py:26
  55.3 24.9 %collective-permute-start.15 = (bf16[480,768]{1,0:T(8,128)(2,1)}, bf16[480,768]{1,0:T(8,128)(2,1)S(1)}, u32[]{:S(2)}, u32[]{:S(2)}) collective-permute-start(bf16[480,768]{1,0:T(8,128)(2,1)} %copy-done.25), channel_id=1, source_target_pairs={{0,4},{4,0},{8,12},{12,8},{16,20},{20,16},{24,28},{28,24},{1,5},{5... | collective-permute-start | bytes 2211848 | tf_op jit(solution)/shard_map/ppermute | solution.py:26
  115.7 16.6 %collective-permute-start.27 = (bf16[2,8,96,768]{3,2,1,0:T(8,128)(2,1)}, bf16[2,8,96,768]{3,2,1,0:T(8,128)(2,1)S(1)}, u32[]{:S(2)}, u32[]{:S(2)}) collective-permute-start(bf16[2,8,96,768]{3,2,1,0:T(8,128)(2,1)} %get-tuple-element.109), channel_id=1, source_target_pairs={{0,1},{1,0},{2,3},{3,2},{4,5},{5,4},{6,7},{7,6},{8,9},{9,8},{10,11... | collective-permute-start | bytes 7077896 | tf_op jit(solution)/shard_map/ppermute | solution.py:26
  115.8 18.2 %collective-permute-start.25 = (bf16[2,8,96,768]{3,2,1,0:T(8,128)(2,1)}, bf16[2,8,96,768]{3,2,1,0:T(8,128)(2,1)S(1)}, u32[]{:S(2)}, u32[]{:S(2)}) collective-permute-start(bf16[2,8,96,768]{3,2,1,0:T(8,128)(2,1)} %get-tuple-element.103), channel_id=1, source_target_pairs={{0,1},{1,0},{2,3},{3,2},{4,5},{5,4},{6,7},{7,6},{8,9},{9,8},{10,11... | collective-permute-start | bytes 7077896 | tf_op jit(solution)/shard_map/ppermute | solution.py:26
  123.1 10.9 %collective-permute-start.26 = (bf16[2,8,24,768]{3,2,1,0:T(8,128)(2,1)}, bf16[2,8,24,768]{3,2,1,0:T(8,128)(2,1)S(1)}, u32[]{:S(2)}, u32[]{:S(2)}) collective-permute-start(bf16[2,8,24,768]{3,2,1,0:T(8,128)(2,1)} %get-tuple-element.106), channel_id=1, source_target_pairs={{0,1},{1,0},{2,3},{3,2},{4,5},{5,4},{6,7},{7,6},{8,9},{9,8},{10,11... | collective-permute-start | bytes 1769480 | tf_op jit(solution)/shard_map/ppermute | solution.py:26
  136.3 37.4 %collective-permute-start.30 = (bf16[8,120,768]{2,1,0:T(8,128)(2,1)}, bf16[8,120,768]{2,1,0:T(8,128)(2,1)S(1)}, u32[]{:S(2)}, u32[]{:S(2)}) collective-permute-start(bf16[8,120,768]{2,1,0:T(8,128)(2,1)} %get-tuple-element.111.refs_12_), channel_id=1, source_target_pairs={{0,2},{1,3},{2,0},{3,1},{4,6},{5,7},{6,4},{7,5},{8,10},{9,11},{10,... | collective-permute-start | bytes 4423688 | tf_op jit(solution)/shard_map/ppermute | solution.py:26
  136.8 35.8 %collective-permute-start.29 = (bf16[4,2,96,768]{3,2,1,0:T(8,128)(2,1)S(1)}, bf16[4,2,96,768]{3,2,1,0:T(8,128)(2,1)S(1)}, u32[]{:S(2)}, u32[]{:S(2)}) collective-permute-start(bf16[4,2,96,768]{3,2,1,0:T(8,128)(2,1)S(1)} %get-tuple-element.110.refs_6_), channel_id=1, source_target_pairs={{0,8},{4,12},{8,0},{12,4},{16,24},{20,28},{24,16},{28,20},{1,9},{5... | collective-permute-start | bytes 3538952 | tf_op jit(solution)/shard_map/ppermute | solution.py:26
  158.7 22.7 %collective-permute-start.28 = (bf16[2,3,128,768]{3,2,1,0:T(8,128)(2,1)}, bf16[2,3,128,768]{3,2,1,0:T(8,128)(2,1)}, u32[]{:S(2)}, u32[]{:S(2)}) collective-permute-start(bf16[2,3,128,768]{3,2,1,0:T(8,128)(2,1)} %get-tuple-element.113), channel_id=1, source_target_pairs={{0,1},{1,0},{2,3},{3,2},{4,5},{5,4},{6,7},{7,6},{8,9},{9,8},{10,11... | collective-permute-start | bytes 3538952 | tf_op jit(solution)/shard_map/ppermute | solution.py:26
  158.9 13.7 %collective-permute-start.31 = (bf16[4,4,24,576]{3,2,1,0:T(8,128)(2,1)}, bf16[4,4,24,576]{3,2,1,0:T(8,128)(2,1)S(1)}, u32[]{:S(2)}, u32[]{:S(2)}) collective-permute-start(bf16[4,4,24,576]{3,2,1,0:T(8,128)(2,1)} %get-tuple-element.116), channel_id=1, source_target_pairs={{0,4},{4,0},{8,12},{12,8},{16,20},{20,16},{24,28},{28,24},{1,5},{5... | collective-permute-start | bytes 1327112 | tf_op jit(solution)/shard_map/ppermute | solution.py:26
  178.4 18.0 %collective-permute-start.38 = (bf16[4,120,768]{2,1,0:T(8,128)(2,1)S(1)}, bf16[4,120,768]{2,1,0:T(8,128)(2,1)}, u32[]{:S(2)}, u32[]{:S(2)}) collective-permute-start(bf16[4,120,768]{2,1,0:T(8,128)(2,1)S(1)} %get-tuple-element.117.refs_2_), channel_id=1, source_target_pairs={{0,4},{4,0},{8,12},{12,8},{16,20},{20,16},{24,28},{28,24},{1,5},{5... | collective-permute-start | bytes 2211848 | tf_op jit(solution)/shard_map/ppermute | solution.py:26
  179.9 19.5 %collective-permute-start.41 = (bf16[4,96,768]{2,1,0:T(8,128)(2,1)}, bf16[4,96,768]{2,1,0:T(8,128)(2,1)}, u32[]{:S(2)}, u32[]{:S(2)}) collective-permute-start(bf16[4,96,768]{2,1,0:T(8,128)(2,1)} %get-tuple-element.129), channel_id=1, source_target_pairs={{0,2},{1,3},{2,0},{3,1},{4,6},{5,7},{6,4},{7,5},{8,10},{9,11},{10,... | collective-permute-start | bytes 1769480 | tf_op jit(solution)/shard_map/ppermute | solution.py:26
  183.7 34.9 %collective-permute-start.32 = (bf16[3,128,768]{2,1,0:T(8,128)(2,1)}, bf16[3,128,768]{2,1,0:T(8,128)(2,1)S(1)}, u32[]{:S(2)}, u32[]{:S(2)}) collective-permute-start(bf16[3,128,768]{2,1,0:T(8,128)(2,1)} %get-tuple-element.119.refs_2_), channel_id=1, source_target_pairs={{0,2},{1,3},{2,0},{3,1},{4,6},{5,7},{6,4},{7,5},{8,10},{9,11},{10,... | collective-permute-start | bytes 1769480 | tf_op jit(solution)/shard_map/ppermute | solution.py:26
  184.5 18.2 %collective-permute-start.37 = (bf16[2,4,24,576]{3,2,1,0:T(8,128)(2,1)S(1)}, bf16[2,4,24,576]{3,2,1,0:T(8,128)(2,1)S(1)}, u32[]{:S(2)}, u32[]{:S(2)}) collective-permute-start(bf16[2,4,24,576]{3,2,1,0:T(8,128)(2,1)S(1)} %get-tuple-element.126.refs_1_), channel_id=1, source_target_pairs={{0,8},{4,12},{8,0},{12,4},{16,24},{20,28},{24,16},{28,20},{1,9},{5... | collective-permute-start | bytes 663560 | tf_op jit(solution)/shard_map/ppermute | solution.py:26
  198.8 19.8 %collective-permute-start.40 = (bf16[2,120,768]{2,1,0:T(8,128)(2,1)S(1)}, bf16[2,120,768]{2,1,0:T(8,128)(2,1)}, u32[]{:S(2)}, u32[]{:S(2)}) collective-permute-start(bf16[2,120,768]{2,1,0:T(8,128)(2,1)S(1)} %slice.95), channel_id=1, source_target_pairs={{0,8},{4,12},{8,0},{12,4},{16,24},{20,28},{24,16},{28,20},{1,9},{5... | collective-permute-start | bytes 1105928 | tf_op jit(solution)/shard_map/ppermute | solution.py:26
  201.1 16.5 %collective-permute-start.42 = (bf16[2,96,768]{2,1,0:T(8,128)(2,1)S(1)}, bf16[2,96,768]{2,1,0:T(8,128)(2,1)S(1)}, u32[]{:S(2)}, u32[]{:S(2)}) collective-permute-start(bf16[2,96,768]{2,1,0:T(8,128)(2,1)S(1)} %slice.96), channel_id=1, source_target_pairs={{0,4},{4,0},{8,12},{12,8},{16,20},{20,16},{24,28},{28,24},{1,5},{5... | collective-permute-start | bytes 884744 | tf_op jit(solution)/shard_map/ppermute | solution.py:26
  204.4 12.5 %collective-permute-start.39 = (bf16[2,4,24,576]{3,2,0,1:T(8,128)(2,1)S(1)}, bf16[2,4,24,576]{3,2,0,1:T(8,128)(2,1)S(1)}, u32[]{:S(2)}, u32[]{:S(2)}) collective-permute-start(bf16[2,4,24,576]{3,2,0,1:T(8,128)(2,1)S(1)} %add_convert_fusion.4), channel_id=1, source_target_pairs={{0,16},{4,20},{8,24},{12,28},{16,0},{20,4},{24,8},{28,12},{1,17},{... | collective-permute-start | bytes 663560 | tf_op jit(solution)/shard_map/ppermute | solution.py:26
  225.3 26.3 %collective-permute-start.49 = (bf16[2,120,768]{2,1,0:T(8,128)(2,1)S(1)}, bf16[2,120,768]{2,1,0:T(8,128)(2,1)S(1)}, u32[]{:S(2)}, u32[]{:S(2)}) collective-permute-start(bf16[2,120,768]{2,1,0:T(8,128)(2,1)S(1)} %get-tuple-element.157), channel_id=1, source_target_pairs={{0,16},{4,20},{8,24},{12,28},{16,0},{20,4},{24,8},{28,12},{1,17},{... | collective-permute-start | bytes 1105928 | tf_op jit(solution)/shard_map/ppermute | solution.py:26
  229.0 11.7 %collective-permute-start.46 = (bf16[2,4,24,576]{3,2,1,0:T(8,128)(2,1)S(1)}, bf16[2,4,24,576]{3,2,1,0:T(8,128)(2,1)}, u32[]{:S(2)}, u32[]{:S(2)}) collective-permute-start(bf16[2,4,24,576]{3,2,1,0:T(8,128)(2,1)S(1)} %pad_maximum_fusion.3), channel_id=1, source_target_pairs={{0,4},{4,0},{8,12},{12,8},{16,20},{20,16},{24,28},{28,24},{1,5},{5... | collective-permute-start | bytes 663560 | tf_op jit(solution)/shard_map/ppermute | solution.py:26
  240.6 17.3 %collective-permute-start.51 = (bf16[2,96,768]{2,1,0:T(8,128)(2,1)}, bf16[2,96,768]{2,1,0:T(8,128)(2,1)}, u32[]{:S(2)}, u32[]{:S(2)}) collective-permute-start(bf16[2,96,768]{2,1,0:T(8,128)(2,1)} %get-tuple-element.155), channel_id=1, source_target_pairs={{0,16},{4,20},{8,24},{12,28},{16,0},{20,4},{24,8},{28,12},{1,17},{... | collective-permute-start | bytes 884744 | tf_op jit(solution)/shard_map/ppermute | solution.py:26
  241.7 31.7 %collective-permute-start.47 = (bf16[4,4,24,576]{3,2,1,0:T(8,128)(2,1)S(1)}, bf16[4,4,24,576]{3,2,1,0:T(8,128)(2,1)S(1)}, u32[]{:S(2)}, u32[]{:S(2)}) collective-permute-start(bf16[4,4,24,576]{3,2,1,0:T(8,128)(2,1)S(1)} %pad_maximum_fusion.2.refs_0_), channel_id=1, source_target_pairs={{0,8},{4,12},{8,0},{12,4},{16,24},{20,28},{24,16},{28,20},{1,9},{5... | collective-permute-start | bytes 1327112 | tf_op jit(solution)/shard_map/ppermute | solution.py:26
  254.2 16.7 %collective-permute-start.50 = (bf16[2,120,768]{2,1,0:T(8,128)(2,1)}, bf16[2,120,768]{2,1,0:T(8,128)(2,1)S(1)}, u32[]{:S(2)}, u32[]{:S(2)}) collective-permute-start(bf16[2,120,768]{2,1,0:T(8,128)(2,1)} %add_convert_fusion.1.refs_1_), channel_id=1, source_target_pairs={{0,8},{4,12},{8,0},{12,4},{16,24},{20,28},{24,16},{28,20},{1,9},{5... | collective-permute-start | bytes 1105928 | tf_op jit(solution)/shard_map/ppermute | solution.py:26
  259.7 13.7 %collective-permute-start.53 = (bf16[2,96,768]{2,1,0:T(8,128)(2,1)}, bf16[2,96,768]{2,1,0:T(8,128)(2,1)}, u32[]{:S(2)}, u32[]{:S(2)}) collective-permute-start(bf16[2,96,768]{2,1,0:T(8,128)(2,1)} %add_convert_fusion.2.refs_1_), channel_id=1, source_target_pairs={{0,4},{4,0},{8,12},{12,8},{16,20},{20,16},{24,28},{28,24},{1,5},{5... | collective-permute-start | bytes 884744 | tf_op jit(solution)/shard_map/ppermute | solution.py:26
  272.8 20.9 %collective-permute-start.52 = (bf16[4,120,768]{2,1,0:T(8,128)(2,1)S(1)}, bf16[4,120,768]{2,1,0:T(8,128)(2,1)}, u32[]{:S(2)}, u32[]{:S(2)}) collective-permute-start(bf16[4,120,768]{2,1,0:T(8,128)(2,1)S(1)} %pad_maximum_fusion.refs_0_), channel_id=1, source_target_pairs={{0,4},{4,0},{8,12},{12,8},{16,20},{20,16},{24,28},{28,24},{1,5},{5... | collective-permute-start | bytes 2211848 | tf_op jit(solution)/shard_map/ppermute | solution.py:26
  275.3 15.5 %collective-permute-start.54 = (bf16[4,96,768]{2,1,0:T(8,128)(2,1)S(1)}, bf16[4,96,768]{2,1,0:T(8,128)(2,1)}, u32[]{:S(2)}, u32[]{:S(2)}) collective-permute-start(bf16[4,96,768]{2,1,0:T(8,128)(2,1)S(1)} %pad_maximum_fusion.1.refs_0_), channel_id=1, source_target_pairs={{0,8},{4,12},{8,0},{12,4},{16,24},{20,28},{24,16},{28,20},{1,9},{5... | collective-permute-start | bytes 1769480 | tf_op jit(solution)/shard_map/ppermute | solution.py:26
  275.4 13.7 %collective-permute-start.36 = (f32[15,768]{1,0:T(8,128)S(1)}, f32[15,768]{1,0:T(8,128)S(1)}, u32[]{:S(2)}, u32[]{:S(2)}) collective-permute-start(f32[15,768]{1,0:T(8,128)S(1)} %copy-done.40), channel_id=1, source_target_pairs={{0,8},{4,12},{8,0},{12,4},{16,24},{20,28},{24,16},{28,20},{1,9},{5... | collective-permute-start | bytes 138248 | tf_op jit(solution)/shard_map/ppermute | solution.py:26
  (101 other events, 710.6 us)

commit v3 on v2

--- a/solution.py
+++ b/solution.py
@@ -144,7 +144,7 @@
 
 def attend_kernel(seq_ref, *refs, waits):
     x_refs, w_refs, bias_ref, refs = refs[:4], refs[4:8], refs[8], refs[9 + waits :]
-    q_ref, k_ref, v_ref, wc_ref, out_refs = refs[0], refs[1], refs[2], refs[3], refs[4:]
+    q_ref, k_ref, v_ref, wc_ref, log_ref, out_refs = refs[0], refs[1], refs[2], refs[3], refs[4], refs[5:]
     part = w_refs[0].shape[0]
     span = x_refs[0].shape[1]
 
@@ -163,9 +163,12 @@
     for h in range(part // HEAD_DIM):
         pick = jnp.where(lane == h, 1.0 / math.sqrt(HEAD_DIM), 0.0).astype(BF16)
         scores = nt(k, q * pick)
-        raised = jnp.exp(scores - jnp.max(scores, axis=0, keepdims=True))
-        chances = (raised * (1.0 / jnp.sum(raised, axis=0, keepdims=True))).astype(BF16)
-        attended = tn(v, chances)[h * HEAD_DIM : (h + 1) * HEAD_DIM].astype(BF16)
+        top = jnp.max(scores, axis=0, keepdims=True)
+        raised = jnp.exp(scores - top)
+        total = jnp.sum(raised, axis=0, keepdims=True)
+        log_ref[0, h : h + 1, :] = top + jnp.log(total)
+        attended = tn(v, raised.astype(BF16))[h * HEAD_DIM : (h + 1) * HEAD_DIM]
+        attended = (attended * (1.0 / total)).astype(BF16)
         for r in range(4):
             out_refs[r][h * HEAD_DIM : (h + 1) * HEAD_DIM, :] = attended[:, r * span : (r + 1) * span]
 
@@ -186,9 +189,11 @@
         + [any_spec()] * len(after),
         out_specs=[per_doc] * 3
         + [pl.BlockSpec((3, features, part), lambda d: (0, 0, 0))]
+        + [pl.BlockSpec((1, part // HEAD_DIM, length), lambda d: (d, 0, 0))]
         + [pl.BlockSpec((part, span), lambda d: (0, d))] * 4,
         out_shape=[jax.ShapeDtypeStruct((documents, length, part), BF16)] * 3
         + [jax.ShapeDtypeStruct((3, features, part), BF16)]
+        + [jax.ShapeDtypeStruct((documents, part // HEAD_DIM, length), F32)]
         + [jax.ShapeDtypeStruct((part, documents * span), BF16)] * 4,
         compiler_params=params(56),
         cost_estimate=pl.CostEstimate(
@@ -199,34 +204,32 @@
 
 
 def attend_back_kernel(place_ref, *refs, waits):
-    g_refs, x_refs = refs[:4], refs[4:8]
-    q_ref, k_ref, v_ref, wc_ref = refs[8:12]
-    keep_ref, give_ref, dw_keep_ref, dw_give_ref, sums_ref, acc_ref = refs[12 + waits :]
+    g_refs, x_refs, a_refs = refs[:4], refs[4:8], refs[8:12]
+    q_ref, k_ref, v_ref, wc_ref, log_ref = refs[12:17]
+    keep_ref, give_ref, dw_keep_ref, dw_give_ref, sums_ref, acc_ref = refs[17 + waits :]
     part = q_ref.shape[2]
     span = x_refs[0].shape[1]
     first = pl.program_id(0) == 0
     q, k, v = q_ref[0], k_ref[0], v_ref[0]
     g = jnp.concatenate([ref[...] for ref in g_refs], axis=1)
+    product = g.astype(F32) * jnp.concatenate([ref[...] for ref in a_refs], axis=1).astype(F32)
     lane = lax.broadcasted_iota(jnp.int32, (1, part), 1) // HEAD_DIM
     scale = 1.0 / math.sqrt(HEAD_DIM)
-    dq = dk = dv = None
+    k_t = k.T
+    dq, dk, dv = [], None, None
     for h in range(part // HEAD_DIM):
         on = lane == h
         pick = jnp.where(on, scale, 0.0).astype(BF16)
         mask = jnp.where(on, 1.0, 0.0)
-        scores = nt(k, q * pick)
-        raised = jnp.exp(scores - jnp.max(scores, axis=0, keepdims=True))
-        chances = raised * (1.0 / jnp.sum(raised, axis=0, keepdims=True))
-        grad = nn(v * mask.astype(BF16), g)
-        both = chances * grad
-        grad = (both - chances * jnp.sum(both, axis=0, keepdims=True)).astype(BF16)
+        chances = jnp.exp(nt(k, q * pick) - log_ref[0, h : h + 1, :])
+        drift = jnp.sum(product[h * HEAD_DIM : (h + 1) * HEAD_DIM], axis=0, keepdims=True)
+        grad = (chances * (nn(v * mask.astype(BF16), g) - drift)).astype(BF16)
         part_v = nt(chances.astype(BF16), g) * mask
         part_k = nn(grad, q) * (mask * scale)
-        part_q = tn(grad, k) * (mask * scale)
-        dq = part_q if dq is None else dq + part_q
+        dq.append(nn(k_t[h * HEAD_DIM : (h + 1) * HEAD_DIM], grad) * scale)
         dk = part_k if dk is None else dk + part_k
         dv = part_v if dv is None else dv + part_v
-    low = [t.astype(BF16) for t in (dq, dk, dv)]
+    low = [t.astype(BF16) for t in (jnp.concatenate(dq, axis=0).T, dk, dv)]
     sums = jnp.concatenate(
         [jnp.sum(low[i].astype(F32), axis=0, keepdims=True) for i in (0, 2)], axis=0
     )
@@ -268,7 +271,7 @@
                             ].astype(BF16)
 
 
-def attend_back(place_word, g_blocks, x_blocks, q, k, v, wc, after):
+def attend_back(place_word, g_blocks, x_blocks, attended, q, k, v, wc, logs, after):
     documents, span, features = x_blocks[0].shape
     part = q.shape[2]
     length = 4 * span
@@ -281,8 +284,10 @@
         in_specs=[pl.BlockSpec(memory_space=pltpu.SMEM)]
         + [pl.BlockSpec((part, span), lambda d: (0, d))] * 4
         + [pl.BlockSpec((1, span, features), lambda d: (d, 0, 0))] * 4
+        + [pl.BlockSpec((part, span), lambda d: (0, d))] * 4
         + [per_doc] * 3
         + [pl.BlockSpec((3, features, part), lambda d: (0, 0, 0))]
+        + [pl.BlockSpec((1, part // HEAD_DIM, length), lambda d: (d, 0, 0))]
         + [any_spec()] * len(after),
         out_specs=[
             pair,
@@ -303,7 +308,7 @@
             flops=flops, bytes_accessed=12 * 1024 * 1024, transcendentals=documents * length * length * 3
         ),
         name="attend_back",
-    )(place_word, *g_blocks, *x_blocks, q, k, v, wc, *after)
+    )(place_word, *g_blocks, *x_blocks, *attended, q, k, v, wc, logs, *after)
 
 
 def gelu_parts(x):
@@ -559,24 +564,25 @@
     keeps, got = ins[:2], ins[2]
     half = got.shape[1] // 2
     for i, mine in enumerate(keeps):
-        outs[0][:, i] = added(mine[:half], got[i, :half]).astype(BF16)
-        outs[1][:, i] = added(mine[half:], got[i, half:]).astype(BF16)
+        outs[i][...] = added(mine[:half], got[i, :half]).astype(BF16)
+        outs[2 + i][...] = added(mine[half:], got[i, half:]).astype(BF16)
 
 
 def fold_up_core(ins, outs):
     size = ins[0].shape[1]
+    half = ins[0].shape[0] // 2
     for keep, far, got, rows in ((*ins[:3], slice(0, size)), (*ins[3:], slice(size, None))):
-        outs[0][:, rows] = added(keep[...], got[0]).astype(BF16)
-        outs[1][:, rows] = added(far[...], got[1]).astype(BF16)
+        for i, part in enumerate((slice(0, half), slice(half, None))):
+            outs[i][:, rows] = added(keep[part], got[0, part]).astype(BF16)
+            outs[2 + i][:, rows] = added(far[part], got[1, part]).astype(BF16)
 
 
 def fold_both(ins, outs):
     down, down_got, up, up_got = ins
+    outs[0][...] = added(down[...], down_got[...]).astype(BF16)
     half = up.shape[0] // 2
-    outs[0][...] = added(down[:, 0], down_got[:, 0]).astype(BF16)
-    outs[1][...] = added(down[:, 1], down_got[:, 1]).astype(BF16)
-    outs[2][...] = added(up[:half], up_got[:half]).astype(BF16)
-    outs[3][...] = added(up[half:], up_got[half:]).astype(BF16)
+    outs[1][...] = added(up[:half], up_got[:half]).astype(BF16)
+    outs[2][...] = added(up[half:], up_got[half:]).astype(BF16)
 
 
 def fold_half(ins, outs):
@@ -586,19 +592,22 @@
     outs[1][...] = added(mine[half:], got[half:]).astype(BF16)
 
 
+def fold_sum(ins, outs):
+    outs[0][...] = added(ins[0][...], ins[1][...]).astype(BF16)
+
+
 def fold_inner(ins, outs):
     mine, got = ins
     for i in range(2):
         outs[i][...] = added(mine[i], got[i]).astype(BF16)
 
 
-def settle_kernel(place_ref, *refs, order, store):
-    held, outs = refs[:2], refs[2:]
+def settle_kernel(place_ref, *refs, order, store, waits):
+    held, outs = refs[:4], refs[4 + waits :]
     seq, dp = place_ref[0], place_ref[1] % NEAR
-    half = PIECES // 2
     for index in range(PIECES):
         spot = place(index, order)
-        store(outs, held[spot // half].at[spot % half], index ^ dp, seq)
+        store(outs, held[spot // 2].at[spot % 2], index ^ dp, seq)
 
 
 def store_down(outs, piece, p, seq):
@@ -624,16 +633,16 @@
             outs[i][rows, columns] = block[:, i * part : (i + 1) * part]
 
 
-def settle(place_word, held, order, store, shapes):
+def settle(place_word, held, order, store, shapes, after=()):
     return pl.pallas_call(
-        functools.partial(settle_kernel, order=order, store=store),
-        in_specs=[pl.BlockSpec(memory_space=pltpu.SMEM)] + [whole_spec()] * 2,
+        functools.partial(settle_kernel, order=order, store=store, waits=len(after)),
+        in_specs=[pl.BlockSpec(memory_space=pltpu.SMEM)] + [whole_spec()] * 4 + [any_spec()] * len(after),
         out_specs=[whole_spec()] * len(shapes),
         out_shape=[jax.ShapeDtypeStruct(shape, F32) for shape in shapes],
         compiler_params=params(56),
         cost_estimate=pl.CostEstimate(flops=0, bytes_accessed=4 * 1024 * 1024, transcendentals=0),
         name="settle",
-    )(place_word, *held)
+    )(place_word, *held, *after)
 
 
 def gate_kernel(*refs):
@@ -664,15 +673,17 @@
         x = x.astype(BF16)
         got = swap(x, "dp", by)
         if after and by == last:
-            got = gate(got, *after)
-        x = x.astype(F32) + got.astype(F32)
+            (x,) = fold(fold_sum, [x, got], [x.shape], after, "sum")
+        else:
+            x = x.astype(F32) + got.astype(F32)
     return x.astype(BF16)
 
 
 def spread_dp(x, first, last, *after):
     got = swap(x, "dp", first)
-    x = jnp.concatenate([x, gate(got, *after) if after else got])
-    return x, swap(x, "dp", last)
+    if after:
+        got = gate(got, *after)
+    return x, got, swap(x, "dp", last), swap(got, "dp", last)
 
 
 def body(
@@ -742,7 +753,7 @@
     low_in = embedded.astype(BF16).reshape(documents, span, features)
     x_blocks = gather_rows(low_in)
     far = swap(gate(down_weight, low_in, pieces[1]), "seq", 2)
-    q, k, v, head_weight, *attended = attend(place_word, x_blocks, head_blocks, head_bias, [])
+    q, k, v, head_weight, logs, *attended = attend(place_word, x_blocks, head_blocks, head_bias, [])
     attn_blocks = exchange_blocks(attended)
     far = gate(far, attn_blocks[3])
     pieces += [down_weight, swap(down_weight, "seq", 1), far, swap(far, "seq", 1)]
@@ -764,51 +775,58 @@
     half = PIECES // 2
     size, tall = features // PIECES, part // PIECES
     g_blocks = exchange_blocks(grad_attn)
-    down, down_send = fold(
+    down, down_far, down_near_send, down_far_send = fold(
         fold_down_core,
         [down_keep, down_far, swap(down_give, "seq", 1)],
-        [(half, 2, size, features)] * 2,
+        [(half, size, features)] * 4,
         [g_blocks[2], g_blocks[3]],
         "down_core",
     )
-    up, up_send = fold(
+    up, up_more, up_send, up_more_send = fold(
         fold_up_core,
         [up_keep, up_far, swap(up_give, "seq", 1), out_keep, out_far, swap(out_give, "seq", 1)],
-        [(PIECES, size + tall, features)] * 2,
-        [down_send],
+        [(half, size + tall, features)] * 4,
+        [down_far_send],
         "up_core",
     )
+    down_far_got = swap(down_far_send, "dp", DOWN_ORDER[0])
+    down_near_got = swap(down_near_send, "dp", DOWN_ORDER[0])
+    up_more_got = swap(up_more_send, "seq", 2)
+    up_got = swap(up_send, "seq", 2)
 
     keep, give, heads, heads_send, head_sums = attend_back(
-        place_word, g_blocks, x_blocks, q, k, v, head_weight, [up_send]
+        place_word, g_blocks, x_blocks, attended, q, k, v, head_weight, logs, [up_more_send]
     )
     query_sums, value_sums = head_sums[0], head_sums[1]
 
-    heads_got = swap(heads_send, "dp", HEAD_ORDER[0])
-    down, down_send, up, up_send = fold(
+    quarter = half // 2
+    down_send, up_send, up_more_send = fold(
         fold_both,
-        [down, swap(down_send, "dp", DOWN_ORDER[0]), up, swap(up_send, "seq", 2)],
-        [(half, size, features)] * 2 + [(half, size + tall, features)] * 2,
-        [heads_got],
+        [down_far, down_far_got, up_more, up_more_got],
+        [(half, size, features)] + [(quarter, size + tall, features)] * 2,
+        [head_sums],
         "both",
     )
     inner_own, inner_send = fold(
-        fold_inner, [keep, swap(give, "seq", 1)], [keep.shape[1:]] * 2, [up_send], "inner"
+        fold_inner, [keep, swap(gate(give, up_more_send), "seq", 1)], [keep.shape[1:]] * 2, [up_send, down_near_got], "inner"
     )
     heads, heads_send = fold(
         fold_half,
-        [heads, heads_got],
+        [heads, swap(gate(heads_send, up_more_send), "dp", HEAD_ORDER[0])],
         [(half // 2, group, tall, 3 * part)] * 2,
-        [inner_send],
+        [up_send, up_got],
         "heads",
     )
-    up = up.astype(F32) + gate(swap(up_send, "dp", UP_ORDER[0]), heads_send).astype(F32)
-    down = down.astype(F32) + gate(swap(down_send, "seq", 2), up).astype(F32)
-    heads = heads.astype(F32) + gate(swap(heads_send, "dp", HEAD_ORDER[1]), up).astype(F32)
     inner_got = swap(inner_send, "seq", 2)
-    quarter = half // 2
-    got = gate(swap(up[quarter:].astype(BF16), "dp", UP_ORDER[1]), inner_got, down)
-    up = up[:quarter] + got.astype(F32)
+    got = gate(swap(up_more_send, "dp", UP_ORDER[0]), heads_send)
+    up_more = up[quarter:].astype(F32) + up_got[quarter:].astype(F32) + got.astype(F32)
+    got = swap(up_send, "dp", UP_ORDER[0])
+    up = up[:quarter].astype(F32) + up_got[:quarter].astype(F32) + got.astype(F32)
+    got = gate(swap(down_send, "seq", 2), up_more)
+    down = down.astype(F32) + down_near_got.astype(F32) + got.astype(F32)
+    heads = heads.astype(F32) + gate(swap(heads_send, "dp", HEAD_ORDER[1]), down).astype(F32)
+    got = gate(swap(up_more.astype(BF16), "dp", UP_ORDER[1]), inner_got, down)
+    up = up + got.astype(F32)
     down = reduce_dp(down, DOWN_ORDER[1:-1])
 
     inner = inner_own.astype(F32) + inner_got.astype(F32)
@@ -848,17 +866,15 @@
     up = reduce_rest(up, UP_ORDER[-1], sums)
     sums = sums + swap(sums, "dp", 1)
     down = reduce_rest(down, DOWN_ORDER[-1], up, sums)
+    held_up = spread_dp(up, 2, 1, down)
+    held_down = spread_dp(down, 1, 2, held_heads[3])
+    for by in bits("dp")[1:]:
+        sums = sums + swap(sums, "dp", by)
+    (total_down,) = settle(place_word, held_down, (2, 1, 4), store_down, [down_weight.shape], [sums])
     total_up, total_out = settle(
-        place_word, spread_dp(up, 2, 1, down), (1, 2, 4), store_up, [up_weight.shape, output_weight.shape]
-    )
-    (total_down,) = settle(
-        place_word, spread_dp(down, 1, 2, held_heads[1]), (2, 1, 4), store_down, [down_weight.shape]
-    )
-
-    for by, ready in zip(bits("dp")[1:], (total_query, total_up)):
-        sums = sums + gate(swap(sums, "dp", by), ready)
-    for by in bits("dp")[3:]:
-        sums = sums + swap(sums, "dp", by)
+        place_word, held_up, (1, 2, 4), store_up, [up_weight.shape, output_weight.shape], [sums]
+    )
+
     (
         sum_gain,
         sum_shift,

time: 307 us -> 288 us (0.938)
  waiting for transfers between devices: 122 us -> 105 us
  starting transfers between devices: 44.7 us -> 53.6 us
  other arithmetic: 25.8 us -> 18.3 us
  Pallas kernels: 81.5 us -> 78.1 us
    ppermute x55 -> x61, waiting for transfers between devices: 122 us -> 105 us  [swap(): lax.ppermute(x, axis, [(i, i ^ by) for i in range(lax.axis_size(axis))])]
    ppermute x55 -> x61, starting transfers between devices: 44.7 us -> 53.6 us  [swap(): lax.ppermute(x, axis, [(i, i ^ by) for i in range(lax.axis_size(axis))])]
    concatenate x3 -> x0, other arithmetic: 3.31 us -> none  [spread_dp(): x = jnp.concatenate([x, gate(got, *after) if after else got])]
    unnamed x157 -> x161, local copies, waits for them, and re-layouts: 21.2 us -> 21.6 us
  transfers between devices with their start and end apart: 55 -> 61, of which waited for: 25 -> 25; matrix products, arithmetic and copies ran while one was open for 8% -> 8% of each run, Pallas kernels for 18% -> 17%
where the time goes in v3:
time: 288 us; the launch traced here: 282 us
  waiting for transfers between devices  105 us (36%)
  Pallas kernels  78.1 us (27%)
  starting transfers between devices  53.6 us (19%)
  local copies, waits for them, and re-layouts  25.2 us (9%)
  other arithmetic  18.3 us (6%)
    ppermute x61, waiting for transfers between devices, swap(): lax.ppermute(x, axis, [(i, i ^ by) for i in range(lax.axis_size(axis))])  105 us
    ppermute x61, starting transfers between devices, swap(): lax.ppermute(x, axis, [(i, i ^ by) for i in range(lax.axis_size(axis))])  53.6 us
    pallas_call x1, Pallas kernels, forward(): pl.pallas_call(forward_kernel, in_specs=[pl.BlockSpec(memory_space=pltpu....  25.2 us
    unnamed x161, local copies, waits for them, and re-layouts  21.6 us
    pallas_call x1, Pallas kernels, attend_back(): pl.pallas_call(functools.partial(attend_back_kernel, waits=len(after)), g...  16.1 us
    pallas_call x1, Pallas kernels, attend(): pl.pallas_call(functools.partial(attend_kernel, waits=len(after)), grid=(...  11 us
    pallas_call x3, Pallas kernels, settle(): pl.pallas_call(functools.partial(settle_kernel, order=order, store=store,...  8.74 us
    pallas_call x1, Pallas kernels, backward(): pl.pallas_call(backward_kernel, in_specs=[pl.BlockSpec(memory_space=pltpu...  6.79 us
  transfers between devices with their start and end apart: 61, of which 25 were waited for; matrix products, arithmetic and copies ran while one was open for 8% of the time, Pallas kernels for 17%

profile of v3, /device:TPU:0, one launch (start us, length us, event | category | flops | bytes accessed | tf_op | source)
XLA Modules:
  0.0 282.2 jit_solution(13786023799539985404)
XLA Ops:
  1.9 3.0 %collective-permute-start = (f32[2,768]{1,0:T(2,128)S(1)}, f32[2,768]{1,0:T(2,128)S(1)}, u32[]{:S(2)}, u32[]{:S(2)}) collective-permute-start(f32[2,768]{1,0:T(2,128)S(1)} %pad_maximum_fusion.1), channel_id=1, source_target_pairs={{0,2},{1,3},{2,0},{3,1},{4,6},{5,7},{6,4},{7,5},{8,10},{9,11},{10,... | collective-permute-start | bytes 18440 | tf_op jit(solution)/shard_map/ppermute | solution.py:26
  5.5 2.5 pack_heads.1
  10.7 2.9 %pack_halves.1 = (bf16[2,480,768]{2,1,0:T(8,128)(2,1)}, bf16[480,768]{1,0:T(8,128)(2,1)}) custom-call(s32[2]{0:T(128)} %pad_add_fusion.place_ref.seq_ref, bf16[192,768]{1,0:T(8,128)(2,1)} %out_ref.1, bf16[192,3072]{1,0:T(8,128)(2,1)} %up_ref.1), custom_call_target="tpu_custom_call" | custom-call | bytes 4194304 | tf_op jit(solution)/shard_map/pack_halves/pallas_call | solution.py:133
  15.6 2.1 collective-permute-done.2
  23.4 2.6 collective-permute-start.6
  26.0 2.1 collective-permute-done.6
  31.0 2.4 copy.64.refs_0_
  33.4 5.6 %collective-permute-done.14.refs_2_.refs_9_ = bf16[480,768]{1,0:T(8,128)(2,1)S(1)} collective-permute-done((bf16[480,768]{1,0:T(8,128)(2,1)}, bf16[480,768]{1,0:T(8,128)(2,1)S(1)}, u32[]{:S(2)}, u32[]{:S(2)}) %collective-permute-start.14) | collective-permute-done | bytes 737312 | tf_op jit(solution)/shard_map/ppermute | solution.py:26
  40.3 11.4 %collective-permute-done.8.refs_2_.refs_6_ = bf16[3,128,768]{2,1,0:T(8,128)(2,1)} collective-permute-done((bf16[3,128,768]{2,1,0:T(8,128)(2,1)S(1)}, bf16[3,128,768]{2,1,0:T(8,128)(2,1)}, u32[]{:S(2)}, u32[]{:S(2)}) %collective-permute-start.8) | collective-permute-done | bytes 589856 | tf_op jit(solution)/shard_map/ppermute | solution.py:26
  57.7 11.0 %attend.1 = (bf16[3,512,192]{2,1,0:T(8,128)(2,1)}, bf16[3,512,192]{2,1,0:T(8,128)(2,1)}, bf16[3,512,192]{2,1,0:T(8,128)(2,1)}, bf16[3,768,192]{2,1,0:T(8,128)(2,...) custom-call(s32[2]{0:T(128)} %pad_add_fusion.place_ref.seq_ref, ...), custom_call_target="tpu_custom_call" | custom-call | flops 1962934272 | bytes 8388608 | tf_op jit(solution)/shard_map/attend/pallas_call | solution.py:182
  69.1 10.0 %collective-permute-done.13.refs_1_.refs_3_ = bf16[192,384]{1,0:T(8,128)(2,1)S(1)} collective-permute-done((bf16[192,384]{1,0:T(8,128)(2,1)}, bf16[192,384]{1,0:T(8,128)(2,1)S(1)}, u32[]{:S(2)}, u32[]{:S(2)}) %collective-permute-start.13) | collective-permute-done | bytes 147488 | tf_op jit(solution)/shard_map/ppermute | solution.py:26
  85.8 4.0 %collective-permute-done.12.refs_2_ = bf16[192,384]{1,0:T(8,128)(2,1)S(1)} collective-permute-done((bf16[192,384]{1,0:T(8,128)(2,1)S(1)}, bf16[192,384]{1,0:T(8,128)(2,1)S(1)}, u32[]{:S(2)}, u32[]{:S(2)}) %collective-permute-start.12) | collective-permute-done | bytes 147488 | tf_op jit(solution)/shard_map/ppermute | solution.py:26
  90.5 25.2 %forward.1 = (bf16[384,768]{1,0:T(8,128)(2,1)}, f32[384,768]{1,0:T(8,128)}, f32[384,1]{1,0:T(8,128)}, f32[384,768]{1,0:T(8,128)}, f32[3,768]{1,0:T(4,128)}, /*in...) custom-call(s32[2]{0:T(128)} %pad_add_fusion.place_ref.seq_ref, ...), custom_call_target="tpu_custom_call" | custom-call | flops 10871635968 | bytes 27262976 | tf_op jit(solution)/shard_map/forward/pallas_call | solution.py:487
  116.3 6.8 %backward.1 = (f32[384,768]{1,0:T(8,128)}, bf16[192,384]{1,0:T(8,128)(2,1)}, bf16[192,384]{1,0:T(8,128)(2,1)}, bf16[192,384]{1,0:T(8,128)(2,1)}, bf16[192,384]{1...) custom-call(s32[2]{0:T(128)} %pad_add_fusion.place_ref.seq_ref, ...), custom_call_target="tpu_custom_call" | custom-call | flops 905969664 | bytes 6291456 | tf_op jit(solution)/shard_map/backward/pallas_call | solution.py:527
  125.1 5.1 %collective-permute-done.23.refs_3_.refs_2_ = bf16[192,384]{1,0:T(8,128)(2,1)S(1)} collective-permute-done((bf16[192,384]{1,0:T(8,128)(2,1)}, bf16[192,384]{1,0:T(8,128)(2,1)S(1)}, u32[]{:S(2)}, u32[]{:S(2)}) %collective-permute-start.23) | collective-permute-done | bytes 147488 | tf_op jit(solution)/shard_map/ppermute | solution.py:26
  130.1 2.3 collective-permute-done.24.refs_4_.refs_3_
  141.0 16.1 %attend_back.1 = (bf16[2,3,128,768]{3,2,1,0:T(8,128)(2,1)}, bf16[2,3,128,768]{3,2,1,0:T(8,128)(2,1)}, bf16[4,4,24,576]{3,2,1,0:T(8,128)(2,1)}, bf16[4,4,24,576]{3,2,1,0:T(8,128)(2,1)}, f32[2,192]{1,0:T(2,128)}) custom-call(s32[2]{0:T(128)} %pad_add_fusion.place_ref.seq_ref, bf16[192,384]{1,0:T(8,128)(2,1)} %get-tuple-element.97.refs_0_, ...), custom_call_target="tpu_custom_call" | custom-call | flops 4227858432 | bytes 12582912 | tf_op jit(solution)/shard_map/attend_back/pallas_call | solution.py:281
  164.8 14.5 %collective-permute-done.39.refs_3_ = bf16[4,120,768]{2,1,0:T(8,128)(2,1)S(1)} collective-permute-done((bf16[4,120,768]{2,1,0:T(8,128)(2,1)S(1)}, bf16[4,120,768]{2,1,0:T(8,128)(2,1)S(1)}, u32[]{:S(2)}, u32[]{:S(2)}) %collective-permute-start.39) | collective-permute-done | bytes 737312 | tf_op jit(solution)/shard_map/ppermute | solution.py:26
  187.2 2.3 inner.1
  193.6 2.3 collective-permute-done.41.refs_0_
  202.1 2.6 collective-permute-start.43
  208.3 2.7 collective-permute-start.53
  215.4 7.0 %collective-permute-done.43.refs_1_ = bf16[2,4,24,576]{3,2,1,0:T(8,128)(2,1)S(1)} collective-permute-done((bf16[2,4,24,576]{3,2,1,0:T(8,128)(2,1)S(1)}, bf16[2,4,24,576]{3,2,1,0:T(8,128)(2,1)S(1)}, u32[]{:S(2)}, u32[]{:S(2)}) %collective-permute-start.43) | collective-permute-done | bytes 221216 | tf_op jit(solution)/shard_map/ppermute | solution.py:26
  232.2 6.6 %collective-permute-done.35 = f32[15,768]{1,0:T(8,128)S(1)} collective-permute-done((f32[15,768]{1,0:T(8,128)S(1)}, f32[15,768]{1,0:T(8,128)S(1)}, u32[]{:S(2)}, u32[]{:S(2)}) %collective-permute-start.35) | collective-permute-done | bytes 46112 | tf_op jit(solution)/shard_map/ppermute | solution.py:26
  238.8 3.8 %collective-permute-done.55.refs_1_ = bf16[2,96,768]{2,1,0:T(8,128)(2,1)S(1)} collective-permute-done((bf16[2,96,768]{2,1,0:T(8,128)(2,1)S(1)}, bf16[2,96,768]{2,1,0:T(8,128)(2,1)S(1)}, u32[]{:S(2)}, u32[]{:S(2)}) %collective-permute-start.55) | collective-permute-done | bytes 294944 | tf_op jit(solution)/shard_map/ppermute | solution.py:26
  245.0 7.0 %collective-permute-done.36 = f32[15,768]{1,0:T(8,128)S(1)} collective-permute-done((f32[15,768]{1,0:T(8,128)S(1)}, f32[15,768]{1,0:T(8,128)S(1)}, u32[]{:S(2)}, u32[]{:S(2)}) %collective-permute-start.36) | collective-permute-done | bytes 46112 | tf_op jit(solution)/shard_map/ppermute | solution.py:26
  254.0 3.4 %collective-permute-done.37 = f32[15,768]{1,0:T(8,128)S(1)} collective-permute-done((f32[15,768]{1,0:T(8,128)S(1)}, f32[15,768]{1,0:T(8,128)S(1)}, u32[]{:S(2)}, u32[]{:S(2)}) %collective-permute-start.37) | collective-permute-done | bytes 46112 | tf_op jit(solution)/shard_map/ppermute | solution.py:26
  265.8 2.8 settle.3
  268.5 3.0 %collective-permute-done.59.refs_2_ = bf16[2,96,768]{2,1,0:T(8,128)(2,1)} collective-permute-done((bf16[2,96,768]{2,1,0:T(8,128)(2,1)}, bf16[2,96,768]{2,1,0:T(8,128)(2,1)}, u32[]{:S(2)}, u32[]{:S(2)}) %collective-permute-start.59) | collective-permute-done | bytes 294944 | tf_op jit(solution)/shard_map/ppermute | solution.py:26
  271.5 3.1 %collective-permute-done.60.refs_3_ = bf16[2,96,768]{2,1,0:T(8,128)(2,1)S(1)} collective-permute-done((bf16[2,96,768]{2,1,0:T(8,128)(2,1)}, bf16[2,96,768]{2,1,0:T(8,128)(2,1)S(1)}, u32[]{:S(2)}, u32[]{:S(2)}) %collective-permute-start.60) | collective-permute-done | bytes 294944 | tf_op jit(solution)/shard_map/ppermute | solution.py:26
  275.3 2.8 settle.5
  278.8 3.2 %settle.4 = (f32[192,3072]{1,0:T(8,128)}, f32[192,768]{1,0:T(8,128)}) custom-call(s32[2]{0:T(128)} %pad_add_fusion.place_ref.seq_ref, bf16[2,120,768]{2,1,0:T(8,128)(2,1)} %copy-done, bf16[2,120,768]{2,1,0:T(8,128)(2,1)} %gate.22.refs_1_, bf16[2,120,768]{2,1,0:T(8,128)(2,1)} %collective-permute-done.56.refs_2_, bf16[2,120,768]{2,1,0:T(8,128)(2,1)} %copy-done.46, ...), custom_call_target="tpu_custom_call" | custom-call | bytes 4194304 | tf_op jit(solution)/shard_map/settle/pallas_call | solution.py:637
  (338 shorter events, 98.4 us)
Async XLA Ops:
  8.8 13.2 %collective-permute-start.4 = (bf16[192,576]{1,0:T(8,128)(2,1)}, bf16[192,576]{1,0:T(8,128)(2,1)S(1)}, u32[]{:S(2)}, u32[]{:S(2)}) collective-permute-start(bf16[192,576]{1,0:T(8,128)(2,1)} %get-tuple-element.83), channel_id=1, source_target_pairs={{0,2},{1,3},{2,0},{3,1},{4,6},{5,7},{6,4},{7,5},{8,10},{9,11},{10,... | collective-permute-start | bytes 663560 | tf_op jit(solution)/shard_map/ppermute | solution.py:26
  13.6 25.4 %collective-permute-start.14 = (bf16[480,768]{1,0:T(8,128)(2,1)}, bf16[480,768]{1,0:T(8,128)(2,1)S(1)}, u32[]{:S(2)}, u32[]{:S(2)}) collective-permute-start(bf16[480,768]{1,0:T(8,128)(2,1)} %get-tuple-element.91), channel_id=1, source_target_pairs={{0,2},{1,3},{2,0},{3,1},{4,6},{5,7},{6,4},{7,5},{8,10},{9,11},{10,... | collective-permute-start | bytes 2211848 | tf_op jit(solution)/shard_map/ppermute | solution.py:26
  29.4 22.3 %collective-permute-start.8 = (bf16[3,128,768]{2,1,0:T(8,128)(2,1)S(1)}, bf16[3,128,768]{2,1,0:T(8,128)(2,1)}, u32[]{:S(2)}, u32[]{:S(2)}) collective-permute-start(bf16[3,128,768]{2,1,0:T(8,128)(2,1)S(1)} %add_convert_fusion.refs_0_.refs_1_.refs_4_), channel_id=1, source_target_pairs={{0,2},{1,3},{2,0},{3,1},{4,6},{5,7},{6,4},{7,5},{8,10},{9,11},{10,... | collective-permute-start | bytes 1769480 | tf_op jit(solution)/shard_map/ppermute | solution.py:26
  39.8 39.3 %collective-permute-start.20 = (bf16[768,768]{1,0:T(8,128)(2,1)}, bf16[768,768]{1,0:T(8,128)(2,1)}, u32[]{:S(2)}, u32[]{:S(2)}) collective-permute-start(bf16[768,768]{1,0:T(8,128)(2,1)} %gate.14), channel_id=1, source_target_pairs={{0,2},{1,3},{2,0},{3,1},{4,6},{5,7},{6,4},{7,5},{8,10},{9,11},{10,... | collective-permute-start | bytes 3538952 | tf_op jit(solution)/shard_map/ppermute | solution.py:26
  40.3 15.0 %collective-permute-start.7 = (bf16[3,128,768]{2,1,0:T(8,128)(2,1)}, bf16[3,128,768]{2,1,0:T(8,128)(2,1)S(1)}, u32[]{:S(2)}, u32[]{:S(2)}) collective-permute-start(bf16[3,128,768]{2,1,0:T(8,128)(2,1)} %copy-done.36), channel_id=1, source_target_pairs={{0,1},{1,0},{2,3},{3,2},{4,5},{5,4},{6,7},{7,6},{8,9},{9,8},{10,11... | collective-permute-start | bytes 1769480 | tf_op jit(solution)/shard_map/ppermute | solution.py:26
  51.7 30.3 %collective-permute-start.19 = (bf16[768,768]{1,0:T(8,128)(2,1)}, bf16[768,768]{1,0:T(8,128)(2,1)}, u32[]{:S(2)}, u32[]{:S(2)}) collective-permute-start(bf16[768,768]{1,0:T(8,128)(2,1)} %refs_14_.1), channel_id=1, source_target_pairs={{0,1},{1,0},{2,3},{3,2},{4,5},{5,4},{6,7},{7,6},{8,9},{9,8},{10,11... | collective-permute-start | bytes 3538952 | tf_op jit(solution)/shard_map/ppermute | solution.py:26
  55.2 30.6 %collective-permute-start.16 = (bf16[2,480,768]{2,1,0:T(8,128)(2,1)}, bf16[2,480,768]{2,1,0:T(8,128)(2,1)}, u32[]{:S(2)}, u32[]{:S(2)}) collective-permute-start(bf16[2,480,768]{2,1,0:T(8,128)(2,1)} %get-tuple-element.90.refs_8_), channel_id=1, source_target_pairs={{0,1},{1,0},{2,3},{3,2},{4,5},{5,4},{6,7},{7,6},{8,9},{9,8},{10,11... | collective-permute-start | bytes 4423688 | tf_op jit(solution)/shard_map/ppermute | solution.py:26
  55.3 25.0 %collective-permute-start.15 = (bf16[480,768]{1,0:T(8,128)(2,1)}, bf16[480,768]{1,0:T(8,128)(2,1)S(1)}, u32[]{:S(2)}, u32[]{:S(2)}) collective-permute-start(bf16[480,768]{1,0:T(8,128)(2,1)} %copy-done.34), channel_id=1, source_target_pairs={{0,4},{4,0},{8,12},{12,8},{16,20},{20,16},{24,28},{28,24},{1,5},{5... | collective-permute-start | bytes 2211848 | tf_op jit(solution)/shard_map/ppermute | solution.py:26
  115.8 16.6 %collective-permute-start.27 = (bf16[2,8,96,768]{3,2,1,0:T(8,128)(2,1)}, bf16[2,8,96,768]{3,2,1,0:T(8,128)(2,1)S(1)}, u32[]{:S(2)}, u32[]{:S(2)}) collective-permute-start(bf16[2,8,96,768]{3,2,1,0:T(8,128)(2,1)} %get-tuple-element.114), channel_id=1, source_target_pairs={{0,1},{1,0},{2,3},{3,2},{4,5},{5,4},{6,7},{7,6},{8,9},{9,8},{10,11... | collective-permute-start | bytes 7077896 | tf_op jit(solution)/shard_map/ppermute | solution.py:26
  115.8 18.0 %collective-permute-start.25 = (bf16[2,8,96,768]{3,2,1,0:T(8,128)(2,1)}, bf16[2,8,96,768]{3,2,1,0:T(8,128)(2,1)S(1)}, u32[]{:S(2)}, u32[]{:S(2)}) collective-permute-start(bf16[2,8,96,768]{3,2,1,0:T(8,128)(2,1)} %get-tuple-element.108), channel_id=1, source_target_pairs={{0,1},{1,0},{2,3},{3,2},{4,5},{5,4},{6,7},{7,6},{8,9},{9,8},{10,11... | collective-permute-start | bytes 7077896 | tf_op jit(solution)/shard_map/ppermute | solution.py:26
  136.9 20.2 %collective-permute-start.29 = (bf16[4,120,768]{2,1,0:T(8,128)(2,1)S(1)}, bf16[4,120,768]{2,1,0:T(8,128)(2,1)S(1)}, u32[]{:S(2)}, u32[]{:S(2)}) collective-permute-start(bf16[4,120,768]{2,1,0:T(8,128)(2,1)S(1)} %get-tuple-element.116.refs_17_), channel_id=1, source_target_pairs={{0,2},{1,3},{2,0},{3,1},{4,6},{5,7},{6,4},{7,5},{8,10},{9,11},{10,... | collective-permute-start | bytes 2211848 | tf_op jit(solution)/shard_map/ppermute | solution.py:26
  137.4 19.7 %collective-permute-start.28 = (bf16[4,96,768]{2,1,0:T(8,128)(2,1)S(1)}, bf16[4,96,768]{2,1,0:T(8,128)(2,1)S(1)}, u32[]{:S(2)}, u32[]{:S(2)}) collective-permute-start(bf16[4,96,768]{2,1,0:T(8,128)(2,1)S(1)} %get-tuple-element.115.refs_6_), channel_id=1, source_target_pairs={{0,8},{4,12},{8,0},{12,4},{16,24},{20,28},{24,16},{28,20},{1,9},{5... | collective-permute-start | bytes 1769480 | tf_op jit(solution)/shard_map/ppermute | solution.py:26
  159.6 27.4 %collective-permute-start.30 = (bf16[2,3,128,768]{3,2,1,0:T(8,128)(2,1)}, bf16[2,3,128,768]{3,2,1,0:T(8,128)(2,1)}, u32[]{:S(2)}, u32[]{:S(2)}) collective-permute-start(bf16[2,3,128,768]{3,2,1,0:T(8,128)(2,1)} %gate.16), channel_id=1, source_target_pairs={{0,1},{1,0},{2,3},{3,2},{4,5},{5,4},{6,7},{7,6},{8,9},{9,8},{10,11... | collective-permute-start | bytes 3538952 | tf_op jit(solution)/shard_map/ppermute | solution.py:26
  160.7 18.5 %collective-permute-start.39 = (bf16[4,120,768]{2,1,0:T(8,128)(2,1)S(1)}, bf16[4,120,768]{2,1,0:T(8,128)(2,1)S(1)}, u32[]{:S(2)}, u32[]{:S(2)}) collective-permute-start(bf16[4,120,768]{2,1,0:T(8,128)(2,1)S(1)} %copy-done.26), channel_id=1, source_target_pairs={{0,2},{1,3},{2,0},{3,1},{4,6},{5,7},{6,4},{7,5},{8,10},{9,11},{10,... | collective-permute-start | bytes 2211848 | tf_op jit(solution)/shard_map/ppermute | solution.py:26
  162.3 24.8 %collective-permute-start.31 = (bf16[4,96,768]{2,1,0:T(8,128)(2,1)}, bf16[4,96,768]{2,1,0:T(8,128)(2,1)S(1)}, u32[]{:S(2)}, u32[]{:S(2)}) collective-permute-start(bf16[4,96,768]{2,1,0:T(8,128)(2,1)} %copy-done.28), channel_id=1, source_target_pairs={{0,8},{4,12},{8,0},{12,4},{16,24},{20,28},{24,16},{28,20},{1,9},{5... | collective-permute-start | bytes 1769480 | tf_op jit(solution)/shard_map/ppermute | solution.py:26
  162.7 18.7 %collective-permute-start.38 = (bf16[4,4,24,576]{3,2,1,0:T(8,128)(2,1)}, bf16[4,4,24,576]{3,2,1,0:T(8,128)(2,1)S(1)}, u32[]{:S(2)}, u32[]{:S(2)}) collective-permute-start(bf16[4,4,24,576]{3,2,1,0:T(8,128)(2,1)} %gate.17), channel_id=1, source_target_pairs={{0,4},{4,0},{8,12},{12,8},{16,20},{20,16},{24,28},{28,24},{1,5},{5... | collective-permute-start | bytes 1327112 | tf_op jit(solution)/shard_map/ppermute | solution.py:26
  164.2 22.3 %collective-permute-start.42 = (bf16[2,120,768]{2,1,0:T(8,128)(2,1)S(1)}, bf16[2,120,768]{2,1,0:T(8,128)(2,1)}, u32[]{:S(2)}, u32[]{:S(2)}) collective-permute-start(bf16[2,120,768]{2,1,0:T(8,128)(2,1)S(1)} %copy-done.3), channel_id=1, source_target_pairs={{0,4},{4,0},{8,12},{12,8},{16,20},{20,16},{24,28},{28,24},{1,5},{5... | collective-permute-start | bytes 1105928 | tf_op jit(solution)/shard_map/ppermute | solution.py:26
  179.3 16.6 %collective-permute-start.41 = (bf16[4,96,768]{2,1,0:T(8,128)(2,1)}, bf16[4,96,768]{2,1,0:T(8,128)(2,1)}, u32[]{:S(2)}, u32[]{:S(2)}) collective-permute-start(bf16[4,96,768]{2,1,0:T(8,128)(2,1)} %copy-done.29), channel_id=1, source_target_pairs={{0,2},{1,3},{2,0},{3,1},{4,6},{5,7},{6,4},{7,5},{8,10},{9,11},{10,... | collective-permute-start | bytes 1769480 | tf_op jit(solution)/shard_map/ppermute | solution.py:26
  182.2 24.7 %collective-permute-start.44 = (bf16[2,120,768]{2,1,0:T(8,128)(2,1)S(1)}, bf16[2,120,768]{2,1,0:T(8,128)(2,1)}, u32[]{:S(2)}, u32[]{:S(2)}) collective-permute-start(bf16[2,120,768]{2,1,0:T(8,128)(2,1)S(1)} %get-tuple-element.123.refs_2_), channel_id=1, source_target_pairs={{0,4},{4,0},{8,12},{12,8},{16,20},{20,16},{24,28},{28,24},{1,5},{5... | collective-permute-start | bytes 1105928 | tf_op jit(solution)/shard_map/ppermute | solution.py:26
  186.6 13.8 %collective-permute-start.40 = (bf16[2,4,24,576]{3,2,1,0:T(8,128)(2,1)}, bf16[2,4,24,576]{3,2,1,0:T(8,128)(2,1)S(1)}, u32[]{:S(2)}, u32[]{:S(2)}) collective-permute-start(bf16[2,4,24,576]{3,2,1,0:T(8,128)(2,1)} %get-tuple-element.134.refs_1_), channel_id=1, source_target_pairs={{0,8},{4,12},{8,0},{12,4},{16,24},{20,28},{24,16},{28,20},{1,9},{5... | collective-permute-start | bytes 663560 | tf_op jit(solution)/shard_map/ppermute | solution.py:26
  189.5 17.4 %collective-permute-start.32 = (bf16[3,128,768]{2,1,0:T(8,128)(2,1)}, bf16[3,128,768]{2,1,0:T(8,128)(2,1)}, u32[]{:S(2)}, u32[]{:S(2)}) collective-permute-start(bf16[3,128,768]{2,1,0:T(8,128)(2,1)} %get-tuple-element.126), channel_id=1, source_target_pairs={{0,2},{1,3},{2,0},{3,1},{4,6},{5,7},{6,4},{7,5},{8,10},{9,11},{10,... | collective-permute-start | bytes 1769480 | tf_op jit(solution)/shard_map/ppermute | solution.py:26
  198.9 15.3 %collective-permute-start.46 = (bf16[2,96,768]{2,1,0:T(8,128)(2,1)}, bf16[2,96,768]{2,1,0:T(8,128)(2,1)}, u32[]{:S(2)}, u32[]{:S(2)}) collective-permute-start(bf16[2,96,768]{2,1,0:T(8,128)(2,1)} %slice.103), channel_id=1, source_target_pairs={{0,4},{4,0},{8,12},{12,8},{16,20},{20,16},{24,28},{28,24},{1,5},{5... | collective-permute-start | bytes 884744 | tf_op jit(solution)/shard_map/ppermute | solution.py:26
  202.1 20.3 %collective-permute-start.43 = (bf16[2,4,24,576]{3,2,1,0:T(8,128)(2,1)S(1)}, bf16[2,4,24,576]{3,2,1,0:T(8,128)(2,1)S(1)}, u32[]{:S(2)}, u32[]{:S(2)}) collective-permute-start(bf16[2,4,24,576]{3,2,1,0:T(8,128)(2,1)S(1)} %add_convert_fusion.1.refs_0_), channel_id=1, source_target_pairs={{0,16},{4,20},{8,24},{12,28},{16,0},{20,4},{24,8},{28,12},{1,17},{... | collective-permute-start | bytes 663560 | tf_op jit(solution)/shard_map/ppermute | solution.py:26
  208.3 20.3 %collective-permute-start.53 = (bf16[2,120,768]{2,1,0:T(8,128)(2,1)S(1)}, bf16[2,120,768]{2,1,0:T(8,128)(2,1)S(1)}, u32[]{:S(2)}, u32[]{:S(2)}) collective-permute-start(bf16[2,120,768]{2,1,0:T(8,128)(2,1)S(1)} %get-tuple-element.165.refs_0_), channel_id=1, source_target_pairs={{0,16},{4,20},{8,24},{12,28},{16,0},{20,4},{24,8},{28,12},{1,17},{... | collective-permute-start | bytes 1105928 | tf_op jit(solution)/shard_map/ppermute | solution.py:26
  226.6 16.0 %collective-permute-start.55 = (bf16[2,96,768]{2,1,0:T(8,128)(2,1)S(1)}, bf16[2,96,768]{2,1,0:T(8,128)(2,1)S(1)}, u32[]{:S(2)}, u32[]{:S(2)}) collective-permute-start(bf16[2,96,768]{2,1,0:T(8,128)(2,1)S(1)} %get-tuple-element.163.refs_0_), channel_id=1, source_target_pairs={{0,16},{4,20},{8,24},{12,28},{16,0},{20,4},{24,8},{28,12},{1,17},{... | collective-permute-start | bytes 884744 | tf_op jit(solution)/shard_map/ppermute | solution.py:26
  228.7 31.1 %collective-permute-start.54 = (bf16[2,120,768]{2,1,0:T(8,128)(2,1)S(1)}, bf16[2,120,768]{2,1,0:T(8,128)(2,1)S(1)}, u32[]{:S(2)}, u32[]{:S(2)}) collective-permute-start(bf16[2,120,768]{2,1,0:T(8,128)(2,1)S(1)} %sum.4.refs_2_.refs_0_), channel_id=1, source_target_pairs={{0,8},{4,12},{8,0},{12,4},{16,24},{20,28},{24,16},{28,20},{1,9},{5... | collective-permute-start | bytes 1105928 | tf_op jit(solution)/shard_map/ppermute | solution.py:26
  230.1 12.9 %collective-permute-start.50 = (bf16[2,4,24,576]{3,2,1,0:T(8,128)(2,1)S(1)}, bf16[2,4,24,576]{3,2,1,0:T(8,128)(2,1)}, u32[]{:S(2)}, u32[]{:S(2)}) collective-permute-start(bf16[2,4,24,576]{3,2,1,0:T(8,128)(2,1)S(1)} %pad_maximum_fusion.refs_0_), channel_id=1, source_target_pairs={{0,4},{4,0},{8,12},{12,8},{16,20},{20,16},{24,28},{28,24},{1,5},{5... | collective-permute-start | bytes 663560 | tf_op jit(solution)/shard_map/ppermute | solution.py:26
  242.7 19.1 %collective-permute-start.58 = (bf16[2,96,768]{2,1,0:T(8,128)(2,1)S(1)}, bf16[2,96,768]{2,1,0:T(8,128)(2,1)S(1)}, u32[]{:S(2)}, u32[]{:S(2)}) collective-permute-start(bf16[2,96,768]{2,1,0:T(8,128)(2,1)S(1)} %sum.5.refs_1_.refs_0_), channel_id=1, source_target_pairs={{0,4},{4,0},{8,12},{12,8},{16,20},{20,16},{24,28},{28,24},{1,5},{5... | collective-permute-start | bytes 884744 | tf_op jit(solution)/shard_map/ppermute | solution.py:26
  242.9 18.6 %collective-permute-start.52 = (bf16[2,4,24,576]{3,2,1,0:T(8,128)(2,1)}, bf16[2,4,24,576]{3,2,1,0:T(8,128)(2,1)}, u32[]{:S(2)}, u32[]{:S(2)}) collective-permute-start(bf16[2,4,24,576]{3,2,1,0:T(8,128)(2,1)} %collective-permute-done.50.refs_1_), channel_id=1, source_target_pairs={{0,8},{4,12},{8,0},{12,4},{16,24},{20,28},{24,16},{28,20},{1,9},{5... | collective-permute-start | bytes 663560 | tf_op jit(solution)/shard_map/ppermute | solution.py:26
  252.3 13.5 %collective-permute-start.51 = (bf16[2,4,24,576]{3,2,1,0:T(8,128)(2,1)S(1)}, bf16[2,4,24,576]{3,2,1,0:T(8,128)(2,1)}, u32[]{:S(2)}, u32[]{:S(2)}) collective-permute-start(bf16[2,4,24,576]{3,2,1,0:T(8,128)(2,1)S(1)} %pad_maximum_fusion.refs_0_), channel_id=1, source_target_pairs={{0,8},{4,12},{8,0},{12,4},{16,24},{20,28},{24,16},{28,20},{1,9},{5... | collective-permute-start | bytes 663560 | tf_op jit(solution)/shard_map/ppermute | solution.py:26
  258.1 20.0 %collective-permute-start.56 = (bf16[2,120,768]{2,1,0:T(8,128)(2,1)S(1)}, bf16[2,120,768]{2,1,0:T(8,128)(2,1)}, u32[]{:S(2)}, u32[]{:S(2)}) collective-permute-start(bf16[2,120,768]{2,1,0:T(8,128)(2,1)S(1)} %sum.4.refs_2_.refs_0_), channel_id=1, source_target_pairs={{0,4},{4,0},{8,12},{12,8},{16,20},{20,16},{24,28},{28,24},{1,5},{5... | collective-permute-start | bytes 1105928 | tf_op jit(solution)/shard_map/ppermute | solution.py:26
  260.5 17.5 %collective-permute-start.57 = (bf16[2,120,768]{2,1,0:T(8,128)(2,1)}, bf16[2,120,768]{2,1,0:T(8,128)(2,1)S(1)}, u32[]{:S(2)}, u32[]{:S(2)}) collective-permute-start(bf16[2,120,768]{2,1,0:T(8,128)(2,1)} %gate.22.refs_1_), channel_id=1, source_target_pairs={{0,4},{4,0},{8,12},{12,8},{16,20},{20,16},{24,28},{28,24},{1,5},{5... | collective-permute-start | bytes 1105928 | tf_op jit(solution)/shard_map/ppermute | solution.py:26
  (109 other events, 804.9 us)

commit v4 on v3

--- a/solution.py
+++ b/solution.py
@@ -377,7 +377,7 @@
     size = terms.shape[3]
 
     wo_copies, up_copies, down_copies = weight_copies(place_ref, pieces, wo, up, down, sems)
-    start_all(wo_copies + up_copies[0] + up_copies[1])
+    start_all(wo_copies + sum(up_copies, []) + sum(down_copies, []))
     out_bias, gain1, shift1, down_bias, gain2, shift2 = (vec_ref[i : i + 1, :] for i in range(6))
     residual = in_ref[...] + out_bias
     wait_all(wo_copies)
@@ -388,16 +388,14 @@
     scale_ref[...] = scale1
     first_out = unit1 * gain1 + shift1
     low = first_out.astype(BF16)
+    wait_all(sum(up_copies, []))
+    wait_all(sum(down_copies, []))
+    second_in = first_out + down_bias
     for r in range(4):
-        wait_all(up_copies[r])
-        start_all(up_copies[r + 2] if r < 2 else down_copies[2 * r - 4] + down_copies[2 * r - 3])
         x = nn(low, up[r]) + upb_ref[pl.ds(seq ^ r, 1), :]
         value, rise = gelu_parts(x)
         act[r] = value.astype(BF16)
         slope[r] = rise
-    second_in = first_out + down_bias
-    for r in range(4):
-        wait_all(down_copies[r])
         second_in += nn(act[r], down[r])
     unit2, scale2 = norm_parts(second_in)
     out_ref[...] = (unit2 * gain2 + shift2).astype(BF16)

time: 288 us -> 287 us (level)
  the two profiles are of different devices: /device:TPU:0 before, /device:TPU:4 now
where the time goes in v4:
time: 287 us; the launch traced here: 281 us
  waiting for transfers between devices  94.6 us (33%)
  Pallas kernels  76.8 us (27%)
  starting transfers between devices  64.3 us (22%)
  local copies, waits for them, and re-layouts  25.4 us (9%)
  other arithmetic  18.3 us (6%)
    ppermute x61, waiting for transfers between devices, swap(): lax.ppermute(x, axis, [(i, i ^ by) for i in range(lax.axis_size(axis))])  94.6 us
    ppermute x61, starting transfers between devices, swap(): lax.ppermute(x, axis, [(i, i ^ by) for i in range(lax.axis_size(axis))])  64.3 us
    pallas_call x1, Pallas kernels, forward(): pl.pallas_call(forward_kernel, in_specs=[pl.BlockSpec(memory_space=pltpu....  24 us
    unnamed x161, local copies, waits for them, and re-layouts  21.8 us
    pallas_call x1, Pallas kernels, attend_back(): pl.pallas_call(functools.partial(attend_back_kernel, waits=len(after)), g...  16.1 us
    pallas_call x1, Pallas kernels, attend(): pl.pallas_call(functools.partial(attend_kernel, waits=len(after)), grid=(...  11 us
    pallas_call x3, Pallas kernels, settle(): pl.pallas_call(functools.partial(settle_kernel, order=order, store=store,...  8.74 us
    pallas_call x1, Pallas kernels, backward(): pl.pallas_call(backward_kernel, in_specs=[pl.BlockSpec(memory_space=pltpu...  6.79 us
  transfers between devices with their start and end apart: 61, of which 24 were waited for; matrix products, arithmetic and copies ran while one was open for 8% of the time, Pallas kernels for 17%

profile of v4, /device:TPU:4, one launch (start us, length us, event | category | flops | bytes accessed | tf_op | source)
XLA Modules:
  0.0 281.2 jit_solution(10681168184906804730)
XLA Ops:
  2.6 2.5 pack_heads.1
  8.2 2.9 %pack_halves.1 = (bf16[2,480,768]{2,1,0:T(8,128)(2,1)}, bf16[480,768]{1,0:T(8,128)(2,1)}) custom-call(s32[2]{0:T(128)} %pad_add_fusion.place_ref.seq_ref, bf16[192,768]{1,0:T(8,128)(2,1)} %out_ref.1, bf16[192,3072]{1,0:T(8,128)(2,1)} %up_ref.1), custom_call_target="tpu_custom_call" | custom-call | bytes 4194304 | tf_op jit(solution)/shard_map/pack_halves/pallas_call | solution.py:133
  14.2 2.1 collective-permute-done.2
  22.0 2.6 collective-permute-start.6
  24.6 2.1 collective-permute-done.6
  28.5 2.4 copy.64.refs_0_
  30.9 5.6 %collective-permute-done.14.refs_2_.refs_9_ = bf16[480,768]{1,0:T(8,128)(2,1)S(1)} collective-permute-done((bf16[480,768]{1,0:T(8,128)(2,1)}, bf16[480,768]{1,0:T(8,128)(2,1)S(1)}, u32[]{:S(2)}, u32[]{:S(2)}) %collective-permute-start.14) | collective-permute-done | bytes 737312 | tf_op jit(solution)/shard_map/ppermute | solution.py:26
  38.9 10.3 %collective-permute-done.8.refs_2_.refs_6_ = bf16[3,128,768]{2,1,0:T(8,128)(2,1)} collective-permute-done((bf16[3,128,768]{2,1,0:T(8,128)(2,1)S(1)}, bf16[3,128,768]{2,1,0:T(8,128)(2,1)}, u32[]{:S(2)}, u32[]{:S(2)}) %collective-permute-start.8) | collective-permute-done | bytes 589856 | tf_op jit(solution)/shard_map/ppermute | solution.py:26
  55.2 11.0 %attend.1 = (bf16[3,512,192]{2,1,0:T(8,128)(2,1)}, bf16[3,512,192]{2,1,0:T(8,128)(2,1)}, bf16[3,512,192]{2,1,0:T(8,128)(2,1)}, bf16[3,768,192]{2,1,0:T(8,128)(2,...) custom-call(s32[2]{0:T(128)} %pad_add_fusion.place_ref.seq_ref, ...), custom_call_target="tpu_custom_call" | custom-call | flops 1962934272 | bytes 8388608 | tf_op jit(solution)/shard_map/attend/pallas_call | solution.py:182
  67.6 9.0 %collective-permute-done.13.refs_1_.refs_3_ = bf16[192,384]{1,0:T(8,128)(2,1)S(1)} collective-permute-done((bf16[192,384]{1,0:T(8,128)(2,1)}, bf16[192,384]{1,0:T(8,128)(2,1)S(1)}, u32[]{:S(2)}, u32[]{:S(2)}) %collective-permute-start.13) | collective-permute-done | bytes 147488 | tf_op jit(solution)/shard_map/ppermute | solution.py:26
  84.4 3.0 %collective-permute-done.12.refs_2_ = bf16[192,384]{1,0:T(8,128)(2,1)S(1)} collective-permute-done((bf16[192,384]{1,0:T(8,128)(2,1)S(1)}, bf16[192,384]{1,0:T(8,128)(2,1)S(1)}, u32[]{:S(2)}, u32[]{:S(2)}) %collective-permute-start.12) | collective-permute-done | bytes 147488 | tf_op jit(solution)/shard_map/ppermute | solution.py:26
  88.0 24.0 %forward.1 = (bf16[384,768]{1,0:T(8,128)(2,1)}, f32[384,768]{1,0:T(8,128)}, f32[384,1]{1,0:T(8,128)}, f32[384,768]{1,0:T(8,128)}, f32[3,768]{1,0:T(4,128)}, /*in...) custom-call(s32[2]{0:T(128)} %pad_add_fusion.place_ref.seq_ref, ...), custom_call_target="tpu_custom_call" | custom-call | flops 10871635968 | bytes 27262976 | tf_op jit(solution)/shard_map/forward/pallas_call | solution.py:485
  112.6 6.8 %backward.1 = (f32[384,768]{1,0:T(8,128)}, bf16[192,384]{1,0:T(8,128)(2,1)}, bf16[192,384]{1,0:T(8,128)(2,1)}, bf16[192,384]{1,0:T(8,128)(2,1)}, bf16[192,384]{1...) custom-call(s32[2]{0:T(128)} %pad_add_fusion.place_ref.seq_ref, ...), custom_call_target="tpu_custom_call" | custom-call | flops 905969664 | bytes 6291456 | tf_op jit(solution)/shard_map/backward/pallas_call | solution.py:525
  121.3 5.1 %collective-permute-done.23.refs_3_.refs_2_ = bf16[192,384]{1,0:T(8,128)(2,1)S(1)} collective-permute-done((bf16[192,384]{1,0:T(8,128)(2,1)}, bf16[192,384]{1,0:T(8,128)(2,1)S(1)}, u32[]{:S(2)}, u32[]{:S(2)}) %collective-permute-start.23) | collective-permute-done | bytes 147488 | tf_op jit(solution)/shard_map/ppermute | solution.py:26
  126.4 2.3 collective-permute-done.24.refs_4_.refs_3_
  138.3 16.1 %attend_back.1 = (bf16[2,3,128,768]{3,2,1,0:T(8,128)(2,1)}, bf16[2,3,128,768]{3,2,1,0:T(8,128)(2,1)}, bf16[4,4,24,576]{3,2,1,0:T(8,128)(2,1)}, bf16[4,4,24,576]{3,2,1,0:T(8,128)(2,1)}, f32[2,192]{1,0:T(2,128)}) custom-call(s32[2]{0:T(128)} %pad_add_fusion.place_ref.seq_ref, bf16[192,384]{1,0:T(8,128)(2,1)} %get-tuple-element.97.refs_0_, ...), custom_call_target="tpu_custom_call" | custom-call | flops 4227858432 | bytes 12582912 | tf_op jit(solution)/shard_map/attend_back/pallas_call | solution.py:281
  161.0 15.6 %collective-permute-done.39.refs_3_ = bf16[4,120,768]{2,1,0:T(8,128)(2,1)S(1)} collective-permute-done((bf16[4,120,768]{2,1,0:T(8,128)(2,1)S(1)}, bf16[4,120,768]{2,1,0:T(8,128)(2,1)S(1)}, u32[]{:S(2)}, u32[]{:S(2)}) %collective-permute-start.39) | collective-permute-done | bytes 737312 | tf_op jit(solution)/shard_map/ppermute | solution.py:26
  183.4 2.3 inner.1
  190.8 2.3 collective-permute-done.41.refs_0_
  199.4 2.7 collective-permute-start.43
  202.1 2.1 collective-permute-done.32.refs_1_
  205.6 2.6 collective-permute-start.53
  212.7 7.0 %collective-permute-done.43.refs_1_ = bf16[2,4,24,576]{3,2,1,0:T(8,128)(2,1)S(1)} collective-permute-done((bf16[2,4,24,576]{3,2,1,0:T(8,128)(2,1)S(1)}, bf16[2,4,24,576]{3,2,1,0:T(8,128)(2,1)S(1)}, u32[]{:S(2)}, u32[]{:S(2)}) %collective-permute-start.43) | collective-permute-done | bytes 221216 | tf_op jit(solution)/shard_map/ppermute | solution.py:26
  226.0 6.0 %collective-permute-start.54 = (bf16[2,120,768]{2,1,0:T(8,128)(2,1)S(1)}, bf16[2,120,768]{2,1,0:T(8,128)(2,1)S(1)}, u32[]{:S(2)}, u32[]{:S(2)}) collective-permute-start(bf16[2,120,768]{2,1,0:T(8,128)(2,1)S(1)} %sum.4.refs_2_.refs_0_), channel_id=1, source_target_pairs={{0,8},{4,12},{8,0},{12,4},{16,24},{20,28},{24,16},{28,20},{1,9},{5... | collective-permute-start | bytes 1105928 | tf_op jit(solution)/shard_map/ppermute | solution.py:26
  234.1 4.7 %collective-permute-done.35 = f32[15,768]{1,0:T(8,128)S(1)} collective-permute-done((f32[15,768]{1,0:T(8,128)S(1)}, f32[15,768]{1,0:T(8,128)S(1)}, u32[]{:S(2)}, u32[]{:S(2)}) %collective-permute-start.35) | collective-permute-done | bytes 46112 | tf_op jit(solution)/shard_map/ppermute | solution.py:26
  242.3 6.0 %collective-permute-done.36 = f32[15,768]{1,0:T(8,128)S(1)} collective-permute-done((f32[15,768]{1,0:T(8,128)S(1)}, f32[15,768]{1,0:T(8,128)S(1)}, u32[]{:S(2)}, u32[]{:S(2)}) %collective-permute-start.36) | collective-permute-done | bytes 46112 | tf_op jit(solution)/shard_map/ppermute | solution.py:26
  248.3 7.9 %collective-permute-start.37 = (f32[15,768]{1,0:T(8,128)S(1)}, f32[15,768]{1,0:T(8,128)S(1)}, u32[]{:S(2)}, u32[]{:S(2)}) collective-permute-start(f32[15,768]{1,0:T(8,128)S(1)} %add.127), channel_id=1, source_target_pairs={{0,16},{4,20},{8,24},{12,28},{16,0},{20,4},{24,8},{28,12},{1,17},{... | collective-permute-start | bytes 138248 | tf_op jit(solution)/shard_map/ppermute | solution.py:26
  256.3 2.2 collective-permute-done.37
  266.8 2.8 settle.3
  270.4 3.1 %collective-permute-done.60.refs_3_ = bf16[2,96,768]{2,1,0:T(8,128)(2,1)S(1)} collective-permute-done((bf16[2,96,768]{2,1,0:T(8,128)(2,1)}, bf16[2,96,768]{2,1,0:T(8,128)(2,1)S(1)}, u32[]{:S(2)}, u32[]{:S(2)}) %collective-permute-start.60) | collective-permute-done | bytes 294944 | tf_op jit(solution)/shard_map/ppermute | solution.py:26
  274.2 2.8 settle.5
  277.8 3.2 %settle.4 = (f32[192,3072]{1,0:T(8,128)}, f32[192,768]{1,0:T(8,128)}) custom-call(s32[2]{0:T(128)} %pad_add_fusion.place_ref.seq_ref, bf16[2,120,768]{2,1,0:T(8,128)(2,1)} %copy-done, bf16[2,120,768]{2,1,0:T(8,128)(2,1)} %gate.22.refs_1_, bf16[2,120,768]{2,1,0:T(8,128)(2,1)} %collective-permute-done.56.refs_2_, bf16[2,120,768]{2,1,0:T(8,128)(2,1)} %copy-done.46, ...), custom_call_target="tpu_custom_call" | custom-call | bytes 4194304 | tf_op jit(solution)/shard_map/settle/pallas_call | solution.py:635
  (338 shorter events, 98.6 us)
Async XLA Ops:
  6.4 14.2 %collective-permute-start.4 = (bf16[192,576]{1,0:T(8,128)(2,1)}, bf16[192,576]{1,0:T(8,128)(2,1)S(1)}, u32[]{:S(2)}, u32[]{:S(2)}) collective-permute-start(bf16[192,576]{1,0:T(8,128)(2,1)} %get-tuple-element.83), channel_id=1, source_target_pairs={{0,2},{1,3},{2,0},{3,1},{4,6},{5,7},{6,4},{7,5},{8,10},{9,11},{10,... | collective-permute-start | bytes 663560 | tf_op jit(solution)/shard_map/ppermute | solution.py:26
  8.0 12.6 %collective-permute-start.5 = (bf16[192,576]{1,0:T(8,128)(2,1)}, bf16[192,576]{1,0:T(8,128)(2,1)S(1)}, u32[]{:S(2)}, u32[]{:S(2)}) collective-permute-start(bf16[192,576]{1,0:T(8,128)(2,1)} %get-tuple-element.84), channel_id=1, source_target_pairs={{0,3},{1,2},{2,1},{3,0},{4,7},{5,6},{6,5},{7,4},{8,11},{9,10},{10,... | collective-permute-start | bytes 663560 | tf_op jit(solution)/shard_map/ppermute | solution.py:26
  11.1 25.4 %collective-permute-start.14 = (bf16[480,768]{1,0:T(8,128)(2,1)}, bf16[480,768]{1,0:T(8,128)(2,1)S(1)}, u32[]{:S(2)}, u32[]{:S(2)}) collective-permute-start(bf16[480,768]{1,0:T(8,128)(2,1)} %get-tuple-element.91), channel_id=1, source_target_pairs={{0,2},{1,3},{2,0},{3,1},{4,6},{5,7},{6,4},{7,5},{8,10},{9,11},{10,... | collective-permute-start | bytes 2211848 | tf_op jit(solution)/shard_map/ppermute | solution.py:26
  28.0 21.2 %collective-permute-start.8 = (bf16[3,128,768]{2,1,0:T(8,128)(2,1)S(1)}, bf16[3,128,768]{2,1,0:T(8,128)(2,1)}, u32[]{:S(2)}, u32[]{:S(2)}) collective-permute-start(bf16[3,128,768]{2,1,0:T(8,128)(2,1)S(1)} %add_convert_fusion.refs_0_.refs_1_.refs_4_), channel_id=1, source_target_pairs={{0,2},{1,3},{2,0},{3,1},{4,6},{5,7},{6,4},{7,5},{8,10},{9,11},{10,... | collective-permute-start | bytes 1769480 | tf_op jit(solution)/shard_map/ppermute | solution.py:26
  37.3 39.3 %collective-permute-start.20 = (bf16[768,768]{1,0:T(8,128)(2,1)}, bf16[768,768]{1,0:T(8,128)(2,1)}, u32[]{:S(2)}, u32[]{:S(2)}) collective-permute-start(bf16[768,768]{1,0:T(8,128)(2,1)} %gate.14), channel_id=1, source_target_pairs={{0,2},{1,3},{2,0},{3,1},{4,6},{5,7},{6,4},{7,5},{8,10},{9,11},{10,... | collective-permute-start | bytes 3538952 | tf_op jit(solution)/shard_map/ppermute | solution.py:26
  38.9 14.0 %collective-permute-start.7 = (bf16[3,128,768]{2,1,0:T(8,128)(2,1)}, bf16[3,128,768]{2,1,0:T(8,128)(2,1)S(1)}, u32[]{:S(2)}, u32[]{:S(2)}) collective-permute-start(bf16[3,128,768]{2,1,0:T(8,128)(2,1)} %copy-done.36), channel_id=1, source_target_pairs={{0,1},{1,0},{2,3},{3,2},{4,5},{5,4},{6,7},{7,6},{8,9},{9,8},{10,11... | collective-permute-start | bytes 1769480 | tf_op jit(solution)/shard_map/ppermute | solution.py:26
  49.2 30.3 %collective-permute-start.19 = (bf16[768,768]{1,0:T(8,128)(2,1)}, bf16[768,768]{1,0:T(8,128)(2,1)}, u32[]{:S(2)}, u32[]{:S(2)}) collective-permute-start(bf16[768,768]{1,0:T(8,128)(2,1)} %refs_14_.1), channel_id=1, source_target_pairs={{0,1},{1,0},{2,3},{3,2},{4,5},{5,4},{6,7},{7,6},{8,9},{9,8},{10,11... | collective-permute-start | bytes 3538952 | tf_op jit(solution)/shard_map/ppermute | solution.py:26
  52.7 31.7 %collective-permute-start.16 = (bf16[2,480,768]{2,1,0:T(8,128)(2,1)}, bf16[2,480,768]{2,1,0:T(8,128)(2,1)}, u32[]{:S(2)}, u32[]{:S(2)}) collective-permute-start(bf16[2,480,768]{2,1,0:T(8,128)(2,1)} %get-tuple-element.90.refs_8_), channel_id=1, source_target_pairs={{0,1},{1,0},{2,3},{3,2},{4,5},{5,4},{6,7},{7,6},{8,9},{9,8},{10,11... | collective-permute-start | bytes 4423688 | tf_op jit(solution)/shard_map/ppermute | solution.py:26
  52.9 25.0 %collective-permute-start.15 = (bf16[480,768]{1,0:T(8,128)(2,1)}, bf16[480,768]{1,0:T(8,128)(2,1)S(1)}, u32[]{:S(2)}, u32[]{:S(2)}) collective-permute-start(bf16[480,768]{1,0:T(8,128)(2,1)} %copy-done.34), channel_id=1, source_target_pairs={{0,4},{4,0},{8,12},{12,8},{16,20},{20,16},{24,28},{28,24},{1,5},{5... | collective-permute-start | bytes 2211848 | tf_op jit(solution)/shard_map/ppermute | solution.py:26
  112.0 16.6 %collective-permute-start.27 = (bf16[2,8,96,768]{3,2,1,0:T(8,128)(2,1)}, bf16[2,8,96,768]{3,2,1,0:T(8,128)(2,1)S(1)}, u32[]{:S(2)}, u32[]{:S(2)}) collective-permute-start(bf16[2,8,96,768]{3,2,1,0:T(8,128)(2,1)} %get-tuple-element.114), channel_id=1, source_target_pairs={{0,1},{1,0},{2,3},{3,2},{4,5},{5,4},{6,7},{7,6},{8,9},{9,8},{10,11... | collective-permute-start | bytes 7077896 | tf_op jit(solution)/shard_map/ppermute | solution.py:26
  112.1 18.0 %collective-permute-start.25 = (bf16[2,8,96,768]{3,2,1,0:T(8,128)(2,1)}, bf16[2,8,96,768]{3,2,1,0:T(8,128)(2,1)S(1)}, u32[]{:S(2)}, u32[]{:S(2)}) collective-permute-start(bf16[2,8,96,768]{3,2,1,0:T(8,128)(2,1)} %get-tuple-element.108), channel_id=1, source_target_pairs={{0,1},{1,0},{2,3},{3,2},{4,5},{5,4},{6,7},{7,6},{8,9},{9,8},{10,11... | collective-permute-start | bytes 7077896 | tf_op jit(solution)/shard_map/ppermute | solution.py:26
  133.1 21.3 %collective-permute-start.29 = (bf16[4,120,768]{2,1,0:T(8,128)(2,1)S(1)}, bf16[4,120,768]{2,1,0:T(8,128)(2,1)S(1)}, u32[]{:S(2)}, u32[]{:S(2)}) collective-permute-start(bf16[4,120,768]{2,1,0:T(8,128)(2,1)S(1)} %get-tuple-element.116.refs_17_), channel_id=1, source_target_pairs={{0,2},{1,3},{2,0},{3,1},{4,6},{5,7},{6,4},{7,5},{8,10},{9,11},{10,... | collective-permute-start | bytes 2211848 | tf_op jit(solution)/shard_map/ppermute | solution.py:26
  134.6 19.7 %collective-permute-start.28 = (bf16[4,96,768]{2,1,0:T(8,128)(2,1)S(1)}, bf16[4,96,768]{2,1,0:T(8,128)(2,1)S(1)}, u32[]{:S(2)}, u32[]{:S(2)}) collective-permute-start(bf16[4,96,768]{2,1,0:T(8,128)(2,1)S(1)} %get-tuple-element.115.refs_6_), channel_id=1, source_target_pairs={{0,8},{4,12},{8,0},{12,4},{16,24},{20,28},{24,16},{28,20},{1,9},{5... | collective-permute-start | bytes 1769480 | tf_op jit(solution)/shard_map/ppermute | solution.py:26
  156.9 26.3 %collective-permute-start.30 = (bf16[2,3,128,768]{3,2,1,0:T(8,128)(2,1)}, bf16[2,3,128,768]{3,2,1,0:T(8,128)(2,1)}, u32[]{:S(2)}, u32[]{:S(2)}) collective-permute-start(bf16[2,3,128,768]{3,2,1,0:T(8,128)(2,1)} %gate.16), channel_id=1, source_target_pairs={{0,1},{1,0},{2,3},{3,2},{4,5},{5,4},{6,7},{7,6},{8,9},{9,8},{10,11... | collective-permute-start | bytes 3538952 | tf_op jit(solution)/shard_map/ppermute | solution.py:26
  158.1 18.5 %collective-permute-start.39 = (bf16[4,120,768]{2,1,0:T(8,128)(2,1)S(1)}, bf16[4,120,768]{2,1,0:T(8,128)(2,1)S(1)}, u32[]{:S(2)}, u32[]{:S(2)}) collective-permute-start(bf16[4,120,768]{2,1,0:T(8,128)(2,1)S(1)} %copy-done.26), channel_id=1, source_target_pairs={{0,2},{1,3},{2,0},{3,1},{4,6},{5,7},{6,4},{7,5},{8,10},{9,11},{10,... | collective-permute-start | bytes 2211848 | tf_op jit(solution)/shard_map/ppermute | solution.py:26
  158.5 24.7 %collective-permute-start.31 = (bf16[4,96,768]{2,1,0:T(8,128)(2,1)}, bf16[4,96,768]{2,1,0:T(8,128)(2,1)S(1)}, u32[]{:S(2)}, u32[]{:S(2)}) collective-permute-start(bf16[4,96,768]{2,1,0:T(8,128)(2,1)} %copy-done.28), channel_id=1, source_target_pairs={{0,8},{4,12},{8,0},{12,4},{16,24},{20,28},{24,16},{28,20},{1,9},{5... | collective-permute-start | bytes 1769480 | tf_op jit(solution)/shard_map/ppermute | solution.py:26
  159.0 18.7 %collective-permute-start.38 = (bf16[4,4,24,576]{3,2,1,0:T(8,128)(2,1)}, bf16[4,4,24,576]{3,2,1,0:T(8,128)(2,1)S(1)}, u32[]{:S(2)}, u32[]{:S(2)}) collective-permute-start(bf16[4,4,24,576]{3,2,1,0:T(8,128)(2,1)} %gate.17), channel_id=1, source_target_pairs={{0,4},{4,0},{8,12},{12,8},{16,20},{20,16},{24,28},{28,24},{1,5},{5... | collective-permute-start | bytes 1327112 | tf_op jit(solution)/shard_map/ppermute | solution.py:26
  160.5 22.4 %collective-permute-start.42 = (bf16[2,120,768]{2,1,0:T(8,128)(2,1)S(1)}, bf16[2,120,768]{2,1,0:T(8,128)(2,1)}, u32[]{:S(2)}, u32[]{:S(2)}) collective-permute-start(bf16[2,120,768]{2,1,0:T(8,128)(2,1)S(1)} %copy-done.3), channel_id=1, source_target_pairs={{0,4},{4,0},{8,12},{12,8},{16,20},{20,16},{24,28},{28,24},{1,5},{5... | collective-permute-start | bytes 1105928 | tf_op jit(solution)/shard_map/ppermute | solution.py:26
  176.6 16.6 %collective-permute-start.41 = (bf16[4,96,768]{2,1,0:T(8,128)(2,1)}, bf16[4,96,768]{2,1,0:T(8,128)(2,1)}, u32[]{:S(2)}, u32[]{:S(2)}) collective-permute-start(bf16[4,96,768]{2,1,0:T(8,128)(2,1)} %copy-done.29), channel_id=1, source_target_pairs={{0,2},{1,3},{2,0},{3,1},{4,6},{5,7},{6,4},{7,5},{8,10},{9,11},{10,... | collective-permute-start | bytes 1769480 | tf_op jit(solution)/shard_map/ppermute | solution.py:26
  178.5 25.7 %collective-permute-start.44 = (bf16[2,120,768]{2,1,0:T(8,128)(2,1)S(1)}, bf16[2,120,768]{2,1,0:T(8,128)(2,1)}, u32[]{:S(2)}, u32[]{:S(2)}) collective-permute-start(bf16[2,120,768]{2,1,0:T(8,128)(2,1)S(1)} %get-tuple-element.123.refs_2_), channel_id=1, source_target_pairs={{0,4},{4,0},{8,12},{12,8},{16,20},{20,16},{24,28},{28,24},{1,5},{5... | collective-permute-start | bytes 1105928 | tf_op jit(solution)/shard_map/ppermute | solution.py:26
  182.8 14.8 %collective-permute-start.40 = (bf16[2,4,24,576]{3,2,1,0:T(8,128)(2,1)}, bf16[2,4,24,576]{3,2,1,0:T(8,128)(2,1)S(1)}, u32[]{:S(2)}, u32[]{:S(2)}) collective-permute-start(bf16[2,4,24,576]{3,2,1,0:T(8,128)(2,1)} %get-tuple-element.134.refs_1_), channel_id=1, source_target_pairs={{0,8},{4,12},{8,0},{12,4},{16,24},{20,28},{24,16},{28,20},{1,9},{5... | collective-permute-start | bytes 663560 | tf_op jit(solution)/shard_map/ppermute | solution.py:26
  185.7 18.5 %collective-permute-start.32 = (bf16[3,128,768]{2,1,0:T(8,128)(2,1)}, bf16[3,128,768]{2,1,0:T(8,128)(2,1)}, u32[]{:S(2)}, u32[]{:S(2)}) collective-permute-start(bf16[3,128,768]{2,1,0:T(8,128)(2,1)} %get-tuple-element.126), channel_id=1, source_target_pairs={{0,2},{1,3},{2,0},{3,1},{4,6},{5,7},{6,4},{7,5},{8,10},{9,11},{10,... | collective-permute-start | bytes 1769480 | tf_op jit(solution)/shard_map/ppermute | solution.py:26
  189.4 12.7 %collective-permute-start.45 = (bf16[2,120,768]{2,1,0:T(8,128)(2,1)}, bf16[2,120,768]{2,1,0:T(8,128)(2,1)}, u32[]{:S(2)}, u32[]{:S(2)}) collective-permute-start(bf16[2,120,768]{2,1,0:T(8,128)(2,1)} %get-tuple-element.167), channel_id=1, source_target_pairs={{0,8},{4,12},{8,0},{12,4},{16,24},{20,28},{24,16},{28,20},{1,9},{5... | collective-permute-start | bytes 1105928 | tf_op jit(solution)/shard_map/ppermute | solution.py:26
  196.2 15.3 %collective-permute-start.46 = (bf16[2,96,768]{2,1,0:T(8,128)(2,1)}, bf16[2,96,768]{2,1,0:T(8,128)(2,1)}, u32[]{:S(2)}, u32[]{:S(2)}) collective-permute-start(bf16[2,96,768]{2,1,0:T(8,128)(2,1)} %slice.103), channel_id=1, source_target_pairs={{0,4},{4,0},{8,12},{12,8},{16,20},{20,16},{24,28},{28,24},{1,5},{5... | collective-permute-start | bytes 884744 | tf_op jit(solution)/shard_map/ppermute | solution.py:26
  199.4 20.3 %collective-permute-start.43 = (bf16[2,4,24,576]{3,2,1,0:T(8,128)(2,1)S(1)}, bf16[2,4,24,576]{3,2,1,0:T(8,128)(2,1)S(1)}, u32[]{:S(2)}, u32[]{:S(2)}) collective-permute-start(bf16[2,4,24,576]{3,2,1,0:T(8,128)(2,1)S(1)} %add_convert_fusion.1.refs_0_), channel_id=1, source_target_pairs={{0,16},{4,20},{8,24},{12,28},{16,0},{20,4},{24,8},{28,12},{1,17},{... | collective-permute-start | bytes 663560 | tf_op jit(solution)/shard_map/ppermute | solution.py:26
  205.6 20.3 %collective-permute-start.53 = (bf16[2,120,768]{2,1,0:T(8,128)(2,1)S(1)}, bf16[2,120,768]{2,1,0:T(8,128)(2,1)S(1)}, u32[]{:S(2)}, u32[]{:S(2)}) collective-permute-start(bf16[2,120,768]{2,1,0:T(8,128)(2,1)S(1)} %get-tuple-element.165.refs_0_), channel_id=1, source_target_pairs={{0,16},{4,20},{8,24},{12,28},{16,0},{20,4},{24,8},{28,12},{1,17},{... | collective-permute-start | bytes 1105928 | tf_op jit(solution)/shard_map/ppermute | solution.py:26
  224.3 14.6 %collective-permute-start.55 = (bf16[2,96,768]{2,1,0:T(8,128)(2,1)S(1)}, bf16[2,96,768]{2,1,0:T(8,128)(2,1)S(1)}, u32[]{:S(2)}, u32[]{:S(2)}) collective-permute-start(bf16[2,96,768]{2,1,0:T(8,128)(2,1)S(1)} %get-tuple-element.163.refs_0_), channel_id=1, source_target_pairs={{0,16},{4,20},{8,24},{12,28},{16,0},{20,4},{24,8},{28,12},{1,17},{... | collective-permute-start | bytes 884744 | tf_op jit(solution)/shard_map/ppermute | solution.py:26
  226.0 33.2 %collective-permute-start.54 = (bf16[2,120,768]{2,1,0:T(8,128)(2,1)S(1)}, bf16[2,120,768]{2,1,0:T(8,128)(2,1)S(1)}, u32[]{:S(2)}, u32[]{:S(2)}) collective-permute-start(bf16[2,120,768]{2,1,0:T(8,128)(2,1)S(1)} %sum.4.refs_2_.refs_0_), channel_id=1, source_target_pairs={{0,8},{4,12},{8,0},{12,4},{16,24},{20,28},{24,16},{28,20},{1,9},{5... | collective-permute-start | bytes 1105928 | tf_op jit(solution)/shard_map/ppermute | solution.py:26
  238.9 23.7 %collective-permute-start.58 = (bf16[2,96,768]{2,1,0:T(8,128)(2,1)S(1)}, bf16[2,96,768]{2,1,0:T(8,128)(2,1)S(1)}, u32[]{:S(2)}, u32[]{:S(2)}) collective-permute-start(bf16[2,96,768]{2,1,0:T(8,128)(2,1)S(1)} %sum.5.refs_1_.refs_0_), channel_id=1, source_target_pairs={{0,4},{4,0},{8,12},{12,8},{16,20},{20,16},{24,28},{28,24},{1,5},{5... | collective-permute-start | bytes 884744 | tf_op jit(solution)/shard_map/ppermute | solution.py:26
  240.3 22.3 %collective-permute-start.52 = (bf16[2,4,24,576]{3,2,1,0:T(8,128)(2,1)}, bf16[2,4,24,576]{3,2,1,0:T(8,128)(2,1)}, u32[]{:S(2)}, u32[]{:S(2)}) collective-permute-start(bf16[2,4,24,576]{3,2,1,0:T(8,128)(2,1)} %collective-permute-done.50.refs_1_), channel_id=1, source_target_pairs={{0,8},{4,12},{8,0},{12,4},{16,24},{20,28},{24,16},{28,20},{1,9},{5... | collective-permute-start | bytes 663560 | tf_op jit(solution)/shard_map/ppermute | solution.py:26
  259.1 17.9 %collective-permute-start.56 = (bf16[2,120,768]{2,1,0:T(8,128)(2,1)S(1)}, bf16[2,120,768]{2,1,0:T(8,128)(2,1)}, u32[]{:S(2)}, u32[]{:S(2)}) collective-permute-start(bf16[2,120,768]{2,1,0:T(8,128)(2,1)S(1)} %sum.4.refs_2_.refs_0_), channel_id=1, source_target_pairs={{0,4},{4,0},{8,12},{12,8},{16,20},{20,16},{24,28},{28,24},{1,5},{5... | collective-permute-start | bytes 1105928 | tf_op jit(solution)/shard_map/ppermute | solution.py:26
  259.9 17.1 %collective-permute-start.57 = (bf16[2,120,768]{2,1,0:T(8,128)(2,1)}, bf16[2,120,768]{2,1,0:T(8,128)(2,1)S(1)}, u32[]{:S(2)}, u32[]{:S(2)}) collective-permute-start(bf16[2,120,768]{2,1,0:T(8,128)(2,1)} %gate.22.refs_1_), channel_id=1, source_target_pairs={{0,4},{4,0},{8,12},{12,8},{16,20},{20,16},{24,28},{28,24},{1,5},{5... | collective-permute-start | bytes 1105928 | tf_op jit(solution)/shard_map/ppermute | solution.py:26
  (109 other events, 831.3 us)

commit v5 on v4

--- a/solution.py
+++ b/solution.py
@@ -370,7 +370,7 @@
     pieces, refs = refs[:10], refs[10:]
     out_ref, unit_ref, scale_ref, grad_ref, sums_ref, upsum_ref = refs[:6]
     outs = (refs[6:9], refs[9:12])
-    wo, up, down, act, slope, low_t, spare, terms, sems, out_sems = refs[12:]
+    wo, up, down, act, slope, low_t, spare, terms, out_held, unit_held, sems, out_sems, early_sems = refs[12:]
     seq, dp = place_ref[0], place_ref[1]
     part = wo.shape[1]
     half = part // 2
@@ -384,7 +384,12 @@
     joined = jnp.concatenate([ref[...] for ref in a_refs], axis=0)
     residual += tn(joined, wo[...].reshape(joined.shape[0], -1))
     unit1, scale1 = norm_parts(residual)
-    unit_ref[...] = unit1
+    early = [
+        pltpu.make_async_copy(unit_held, unit_ref, early_sems.at[0]),
+        pltpu.make_async_copy(out_held, out_ref, early_sems.at[1]),
+    ]
+    unit_held[...] = unit1
+    early[0].start()
     scale_ref[...] = scale1
     first_out = unit1 * gain1 + shift1
     low = first_out.astype(BF16)
@@ -398,7 +403,8 @@
         slope[r] = rise
         second_in += nn(act[r], down[r])
     unit2, scale2 = norm_parts(second_in)
-    out_ref[...] = (unit2 * gain2 + shift2).astype(BF16)
+    out_held[...] = (unit2 * gain2 + shift2).astype(BF16)
+    early[1].start()
     incoming = cot_ref[...].astype(F32)
     grad_first = norm_back(incoming, unit2, scale2, gain2)
     grad_down = grad_first.astype(BF16)
@@ -433,7 +439,7 @@
             spot = place(p ^ (dp % NEAR), DOWN_ORDER)
             terms[0, r, spot] = value[p * size : (p + 1) * size].astype(BF16)
         send(0, r).start()
-    wait_all([send(which, r) for which in range(2) for r in range(4)])
+    wait_all(early + [send(which, r) for which in range(2) for r in range(4)])
 
 
 def backward_kernel(place_ref, *refs):
@@ -485,7 +491,7 @@
     return pl.pallas_call(
         forward_kernel,
         in_specs=[pl.BlockSpec(memory_space=pltpu.SMEM)] + [whole_spec()] * 8 + [any_spec()] * 10,
-        out_specs=[whole_spec()] * 6 + [any_spec()] * 6,
+        out_specs=[any_spec()] * 2 + [whole_spec()] * 4 + [any_spec()] * 6,
         out_shape=[
             shaped(rows, features),
             shaped(rows, features, dtype=F32),
@@ -505,8 +511,11 @@
             pltpu.VMEM((features, rows), BF16),
             pltpu.VMEM((features, rows), BF16),
             pltpu.VMEM((2, 4, PIECES, size, features), BF16),
+            pltpu.VMEM((rows, features), BF16),
+            pltpu.VMEM((rows, features), F32),
             pltpu.SemaphoreType.DMA((44,)),
             pltpu.SemaphoreType.DMA((2, 4)),
+            pltpu.SemaphoreType.DMA((2,)),
         ],
         compiler_params=params(56),
         cost_estimate=pl.CostEstimate(

time: 287 us -> 287 us (level)
  the two profiles are of different devices: /device:TPU:4 before, /device:TPU:0 now
where the time goes in v5:
time: 287 us; the launch traced here: 281 us
  waiting for transfers between devices  105 us (37%)
  Pallas kernels  76.9 us (27%)
  starting transfers between devices  53.5 us (19%)
  local copies, waits for them, and re-layouts  25.2 us (9%)
  other arithmetic  18.3 us (6%)
    ppermute x61, waiting for transfers between devices, swap(): lax.ppermute(x, axis, [(i, i ^ by) for i in range(lax.axis_size(axis))])  105 us
    ppermute x61, starting transfers between devices, swap(): lax.ppermute(x, axis, [(i, i ^ by) for i in range(lax.axis_size(axis))])  53.5 us
    pallas_call x1, Pallas kernels, forward(): pl.pallas_call(forward_kernel, in_specs=[pl.BlockSpec(memory_space=pltpu....  24 us
    unnamed x161, local copies, waits for them, and re-layouts  21.6 us
    pallas_call x1, Pallas kernels, attend_back(): pl.pallas_call(functools.partial(attend_back_kernel, waits=len(after)), g...  16.1 us
    pallas_call x1, Pallas kernels, attend(): pl.pallas_call(functools.partial(attend_kernel, waits=len(after)), grid=(...  11 us
    pallas_call x3, Pallas kernels, settle(): pl.pallas_call(functools.partial(settle_kernel, order=order, store=store,...  8.74 us
    pallas_call x1, Pallas kernels, backward(): pl.pallas_call(backward_kernel, in_specs=[pl.BlockSpec(memory_space=pltpu...  6.78 us
  transfers between devices with their start and end apart: 61, of which 25 were waited for; matrix products, arithmetic and copies ran while one was open for 8% of the time, Pallas kernels for 17%

profile of v5, /device:TPU:0, one launch (start us, length us, event | category | flops | bytes accessed | tf_op | source)
XLA Modules:
  0.0 281.0 jit_solution(2239621290659006054)
XLA Ops:
  1.9 3.0 %collective-permute-start = (f32[2,768]{1,0:T(2,128)S(1)}, f32[2,768]{1,0:T(2,128)S(1)}, u32[]{:S(2)}, u32[]{:S(2)}) collective-permute-start(f32[2,768]{1,0:T(2,128)S(1)} %pad_maximum_fusion.1), channel_id=1, source_target_pairs={{0,2},{1,3},{2,0},{3,1},{4,6},{5,7},{6,4},{7,5},{8,10},{9,11},{10,... | collective-permute-start | bytes 18440 | tf_op jit(solution)/shard_map/ppermute | solution.py:26
  5.5 2.5 pack_heads.1
  10.7 2.9 %pack_halves.1 = (bf16[2,480,768]{2,1,0:T(8,128)(2,1)}, bf16[480,768]{1,0:T(8,128)(2,1)}) custom-call(s32[2]{0:T(128)} %pad_add_fusion.place_ref.seq_ref, bf16[192,768]{1,0:T(8,128)(2,1)} %out_ref.1, bf16[192,3072]{1,0:T(8,128)(2,1)} %up_ref.1), custom_call_target="tpu_custom_call" | custom-call | bytes 4194304 | tf_op jit(solution)/shard_map/pack_halves/pallas_call | solution.py:133
  15.6 2.1 collective-permute-done.2
  23.4 2.6 collective-permute-start.6
  26.0 2.1 collective-permute-done.6
  31.0 2.4 copy.64.refs_0_
  33.4 5.6 %collective-permute-done.14.refs_2_.refs_9_ = bf16[480,768]{1,0:T(8,128)(2,1)S(1)} collective-permute-done((bf16[480,768]{1,0:T(8,128)(2,1)}, bf16[480,768]{1,0:T(8,128)(2,1)S(1)}, u32[]{:S(2)}, u32[]{:S(2)}) %collective-permute-start.14) | collective-permute-done | bytes 737312 | tf_op jit(solution)/shard_map/ppermute | solution.py:26
  40.3 11.4 %collective-permute-done.8.refs_2_.refs_6_ = bf16[3,128,768]{2,1,0:T(8,128)(2,1)} collective-permute-done((bf16[3,128,768]{2,1,0:T(8,128)(2,1)S(1)}, bf16[3,128,768]{2,1,0:T(8,128)(2,1)}, u32[]{:S(2)}, u32[]{:S(2)}) %collective-permute-start.8) | collective-permute-done | bytes 589856 | tf_op jit(solution)/shard_map/ppermute | solution.py:26
  57.7 11.0 %attend.1 = (bf16[3,512,192]{2,1,0:T(8,128)(2,1)}, bf16[3,512,192]{2,1,0:T(8,128)(2,1)}, bf16[3,512,192]{2,1,0:T(8,128)(2,1)}, bf16[3,768,192]{2,1,0:T(8,128)(2,...) custom-call(s32[2]{0:T(128)} %pad_add_fusion.place_ref.seq_ref, ...), custom_call_target="tpu_custom_call" | custom-call | flops 1962934272 | bytes 8388608 | tf_op jit(solution)/shard_map/attend/pallas_call | solution.py:182
  69.1 10.0 %collective-permute-done.13.refs_1_.refs_3_ = bf16[192,384]{1,0:T(8,128)(2,1)S(1)} collective-permute-done((bf16[192,384]{1,0:T(8,128)(2,1)}, bf16[192,384]{1,0:T(8,128)(2,1)S(1)}, u32[]{:S(2)}, u32[]{:S(2)}) %collective-permute-start.13) | collective-permute-done | bytes 147488 | tf_op jit(solution)/shard_map/ppermute | solution.py:26
  85.8 4.0 %collective-permute-done.12.refs_2_ = bf16[192,384]{1,0:T(8,128)(2,1)S(1)} collective-permute-done((bf16[192,384]{1,0:T(8,128)(2,1)S(1)}, bf16[192,384]{1,0:T(8,128)(2,1)S(1)}, u32[]{:S(2)}, u32[]{:S(2)}) %collective-permute-start.12) | collective-permute-done | bytes 147488 | tf_op jit(solution)/shard_map/ppermute | solution.py:26
  90.5 24.0 %forward.1 = (bf16[384,768]{1,0:T(8,128)(2,1)}, f32[384,768]{1,0:T(8,128)}, f32[384,1]{1,0:T(8,128)}, f32[384,768]{1,0:T(8,128)}, f32[3,768]{1,0:T(4,128)}, /*in...) custom-call(s32[2]{0:T(128)} %pad_add_fusion.place_ref.seq_ref, ...), custom_call_target="tpu_custom_call" | custom-call | flops 10871635968 | bytes 27262976 | tf_op jit(solution)/shard_map/forward/pallas_call | solution.py:491
  115.1 6.8 %backward.1 = (f32[384,768]{1,0:T(8,128)}, bf16[192,384]{1,0:T(8,128)(2,1)}, bf16[192,384]{1,0:T(8,128)(2,1)}, bf16[192,384]{1,0:T(8,128)(2,1)}, bf16[192,384]{1...) custom-call(s32[2]{0:T(128)} %pad_add_fusion.place_ref.seq_ref, ...), custom_call_target="tpu_custom_call" | custom-call | flops 905969664 | bytes 6291456 | tf_op jit(solution)/shard_map/backward/pallas_call | solution.py:534
  123.8 5.1 %collective-permute-done.23.refs_3_.refs_2_ = bf16[192,384]{1,0:T(8,128)(2,1)S(1)} collective-permute-done((bf16[192,384]{1,0:T(8,128)(2,1)}, bf16[192,384]{1,0:T(8,128)(2,1)S(1)}, u32[]{:S(2)}, u32[]{:S(2)}) %collective-permute-start.23) | collective-permute-done | bytes 147488 | tf_op jit(solution)/shard_map/ppermute | solution.py:26
  128.9 2.2 collective-permute-done.24.refs_4_.refs_3_
  139.8 16.1 %attend_back.1 = (bf16[2,3,128,768]{3,2,1,0:T(8,128)(2,1)}, bf16[2,3,128,768]{3,2,1,0:T(8,128)(2,1)}, bf16[4,4,24,576]{3,2,1,0:T(8,128)(2,1)}, bf16[4,4,24,576]{3,2,1,0:T(8,128)(2,1)}, f32[2,192]{1,0:T(2,128)}) custom-call(s32[2]{0:T(128)} %pad_add_fusion.place_ref.seq_ref, bf16[192,384]{1,0:T(8,128)(2,1)} %get-tuple-element.97.refs_0_, ...), custom_call_target="tpu_custom_call" | custom-call | flops 4227858432 | bytes 12582912 | tf_op jit(solution)/shard_map/attend_back/pallas_call | solution.py:281
  163.5 14.5 %collective-permute-done.39.refs_3_ = bf16[4,120,768]{2,1,0:T(8,128)(2,1)S(1)} collective-permute-done((bf16[4,120,768]{2,1,0:T(8,128)(2,1)S(1)}, bf16[4,120,768]{2,1,0:T(8,128)(2,1)S(1)}, u32[]{:S(2)}, u32[]{:S(2)}) %collective-permute-start.39) | collective-permute-done | bytes 737312 | tf_op jit(solution)/shard_map/ppermute | solution.py:26
  185.9 2.3 inner.1
  192.3 2.3 collective-permute-done.41.refs_0_
  200.9 2.7 collective-permute-start.43
  207.0 2.6 collective-permute-start.53
  214.2 7.0 %collective-permute-done.43.refs_1_ = bf16[2,4,24,576]{3,2,1,0:T(8,128)(2,1)S(1)} collective-permute-done((bf16[2,4,24,576]{3,2,1,0:T(8,128)(2,1)S(1)}, bf16[2,4,24,576]{3,2,1,0:T(8,128)(2,1)S(1)}, u32[]{:S(2)}, u32[]{:S(2)}) %collective-permute-start.43) | collective-permute-done | bytes 221216 | tf_op jit(solution)/shard_map/ppermute | solution.py:26
  230.9 6.6 %collective-permute-done.35 = f32[15,768]{1,0:T(8,128)S(1)} collective-permute-done((f32[15,768]{1,0:T(8,128)S(1)}, f32[15,768]{1,0:T(8,128)S(1)}, u32[]{:S(2)}, u32[]{:S(2)}) %collective-permute-start.35) | collective-permute-done | bytes 46112 | tf_op jit(solution)/shard_map/ppermute | solution.py:26
  237.5 3.8 %collective-permute-done.55.refs_1_ = bf16[2,96,768]{2,1,0:T(8,128)(2,1)S(1)} collective-permute-done((bf16[2,96,768]{2,1,0:T(8,128)(2,1)S(1)}, bf16[2,96,768]{2,1,0:T(8,128)(2,1)S(1)}, u32[]{:S(2)}, u32[]{:S(2)}) %collective-permute-start.55) | collective-permute-done | bytes 294944 | tf_op jit(solution)/shard_map/ppermute | solution.py:26
  243.7 7.0 %collective-permute-done.36 = f32[15,768]{1,0:T(8,128)S(1)} collective-permute-done((f32[15,768]{1,0:T(8,128)S(1)}, f32[15,768]{1,0:T(8,128)S(1)}, u32[]{:S(2)}, u32[]{:S(2)}) %collective-permute-start.36) | collective-permute-done | bytes 46112 | tf_op jit(solution)/shard_map/ppermute | solution.py:26
  252.7 3.5 %collective-permute-done.37 = f32[15,768]{1,0:T(8,128)S(1)} collective-permute-done((f32[15,768]{1,0:T(8,128)S(1)}, f32[15,768]{1,0:T(8,128)S(1)}, u32[]{:S(2)}, u32[]{:S(2)}) %collective-permute-start.37) | collective-permute-done | bytes 46112 | tf_op jit(solution)/shard_map/ppermute | solution.py:26
  264.5 2.8 settle.3
  267.3 3.0 %collective-permute-done.59.refs_2_ = bf16[2,96,768]{2,1,0:T(8,128)(2,1)} collective-permute-done((bf16[2,96,768]{2,1,0:T(8,128)(2,1)}, bf16[2,96,768]{2,1,0:T(8,128)(2,1)}, u32[]{:S(2)}, u32[]{:S(2)}) %collective-permute-start.59) | collective-permute-done | bytes 294944 | tf_op jit(solution)/shard_map/ppermute | solution.py:26
  270.2 3.1 %collective-permute-done.60.refs_3_ = bf16[2,96,768]{2,1,0:T(8,128)(2,1)S(1)} collective-permute-done((bf16[2,96,768]{2,1,0:T(8,128)(2,1)}, bf16[2,96,768]{2,1,0:T(8,128)(2,1)S(1)}, u32[]{:S(2)}, u32[]{:S(2)}) %collective-permute-start.60) | collective-permute-done | bytes 294944 | tf_op jit(solution)/shard_map/ppermute | solution.py:26
  274.0 2.8 settle.5
  277.6 3.2 %settle.4 = (f32[192,3072]{1,0:T(8,128)}, f32[192,768]{1,0:T(8,128)}) custom-call(s32[2]{0:T(128)} %pad_add_fusion.place_ref.seq_ref, bf16[2,120,768]{2,1,0:T(8,128)(2,1)} %copy-done, bf16[2,120,768]{2,1,0:T(8,128)(2,1)} %gate.22.refs_1_, bf16[2,120,768]{2,1,0:T(8,128)(2,1)} %collective-permute-done.56.refs_2_, bf16[2,120,768]{2,1,0:T(8,128)(2,1)} %copy-done.46, ...), custom_call_target="tpu_custom_call" | custom-call | bytes 4194304 | tf_op jit(solution)/shard_map/settle/pallas_call | solution.py:644
  (338 shorter events, 98.3 us)
Async XLA Ops:
  8.8 13.2 %collective-permute-start.4 = (bf16[192,576]{1,0:T(8,128)(2,1)}, bf16[192,576]{1,0:T(8,128)(2,1)S(1)}, u32[]{:S(2)}, u32[]{:S(2)}) collective-permute-start(bf16[192,576]{1,0:T(8,128)(2,1)} %get-tuple-element.83), channel_id=1, source_target_pairs={{0,2},{1,3},{2,0},{3,1},{4,6},{5,7},{6,4},{7,5},{8,10},{9,11},{10,... | collective-permute-start | bytes 663560 | tf_op jit(solution)/shard_map/ppermute | solution.py:26
  13.6 25.4 %collective-permute-start.14 = (bf16[480,768]{1,0:T(8,128)(2,1)}, bf16[480,768]{1,0:T(8,128)(2,1)S(1)}, u32[]{:S(2)}, u32[]{:S(2)}) collective-permute-start(bf16[480,768]{1,0:T(8,128)(2,1)} %get-tuple-element.91), channel_id=1, source_target_pairs={{0,2},{1,3},{2,0},{3,1},{4,6},{5,7},{6,4},{7,5},{8,10},{9,11},{10,... | collective-permute-start | bytes 2211848 | tf_op jit(solution)/shard_map/ppermute | solution.py:26
  29.4 22.3 %collective-permute-start.8 = (bf16[3,128,768]{2,1,0:T(8,128)(2,1)S(1)}, bf16[3,128,768]{2,1,0:T(8,128)(2,1)}, u32[]{:S(2)}, u32[]{:S(2)}) collective-permute-start(bf16[3,128,768]{2,1,0:T(8,128)(2,1)S(1)} %add_convert_fusion.refs_0_.refs_1_.refs_4_), channel_id=1, source_target_pairs={{0,2},{1,3},{2,0},{3,1},{4,6},{5,7},{6,4},{7,5},{8,10},{9,11},{10,... | collective-permute-start | bytes 1769480 | tf_op jit(solution)/shard_map/ppermute | solution.py:26
  39.8 39.3 %collective-permute-start.20 = (bf16[768,768]{1,0:T(8,128)(2,1)}, bf16[768,768]{1,0:T(8,128)(2,1)}, u32[]{:S(2)}, u32[]{:S(2)}) collective-permute-start(bf16[768,768]{1,0:T(8,128)(2,1)} %gate.14), channel_id=1, source_target_pairs={{0,2},{1,3},{2,0},{3,1},{4,6},{5,7},{6,4},{7,5},{8,10},{9,11},{10,... | collective-permute-start | bytes 3538952 | tf_op jit(solution)/shard_map/ppermute | solution.py:26
  40.3 15.0 %collective-permute-start.7 = (bf16[3,128,768]{2,1,0:T(8,128)(2,1)}, bf16[3,128,768]{2,1,0:T(8,128)(2,1)S(1)}, u32[]{:S(2)}, u32[]{:S(2)}) collective-permute-start(bf16[3,128,768]{2,1,0:T(8,128)(2,1)} %copy-done.36), channel_id=1, source_target_pairs={{0,1},{1,0},{2,3},{3,2},{4,5},{5,4},{6,7},{7,6},{8,9},{9,8},{10,11... | collective-permute-start | bytes 1769480 | tf_op jit(solution)/shard_map/ppermute | solution.py:26
  51.7 30.3 %collective-permute-start.19 = (bf16[768,768]{1,0:T(8,128)(2,1)}, bf16[768,768]{1,0:T(8,128)(2,1)}, u32[]{:S(2)}, u32[]{:S(2)}) collective-permute-start(bf16[768,768]{1,0:T(8,128)(2,1)} %refs_14_.1), channel_id=1, source_target_pairs={{0,1},{1,0},{2,3},{3,2},{4,5},{5,4},{6,7},{7,6},{8,9},{9,8},{10,11... | collective-permute-start | bytes 3538952 | tf_op jit(solution)/shard_map/ppermute | solution.py:26
  55.2 30.6 %collective-permute-start.16 = (bf16[2,480,768]{2,1,0:T(8,128)(2,1)}, bf16[2,480,768]{2,1,0:T(8,128)(2,1)}, u32[]{:S(2)}, u32[]{:S(2)}) collective-permute-start(bf16[2,480,768]{2,1,0:T(8,128)(2,1)} %get-tuple-element.90.refs_8_), channel_id=1, source_target_pairs={{0,1},{1,0},{2,3},{3,2},{4,5},{5,4},{6,7},{7,6},{8,9},{9,8},{10,11... | collective-permute-start | bytes 4423688 | tf_op jit(solution)/shard_map/ppermute | solution.py:26
  55.3 25.0 %collective-permute-start.15 = (bf16[480,768]{1,0:T(8,128)(2,1)}, bf16[480,768]{1,0:T(8,128)(2,1)S(1)}, u32[]{:S(2)}, u32[]{:S(2)}) collective-permute-start(bf16[480,768]{1,0:T(8,128)(2,1)} %copy-done.34), channel_id=1, source_target_pairs={{0,4},{4,0},{8,12},{12,8},{16,20},{20,16},{24,28},{28,24},{1,5},{5... | collective-permute-start | bytes 2211848 | tf_op jit(solution)/shard_map/ppermute | solution.py:26
  114.5 16.6 %collective-permute-start.27 = (bf16[2,8,96,768]{3,2,1,0:T(8,128)(2,1)}, bf16[2,8,96,768]{3,2,1,0:T(8,128)(2,1)S(1)}, u32[]{:S(2)}, u32[]{:S(2)}) collective-permute-start(bf16[2,8,96,768]{3,2,1,0:T(8,128)(2,1)} %get-tuple-element.114), channel_id=1, source_target_pairs={{0,1},{1,0},{2,3},{3,2},{4,5},{5,4},{6,7},{7,6},{8,9},{9,8},{10,11... | collective-permute-start | bytes 7077896 | tf_op jit(solution)/shard_map/ppermute | solution.py:26
  114.6 18.0 %collective-permute-start.25 = (bf16[2,8,96,768]{3,2,1,0:T(8,128)(2,1)}, bf16[2,8,96,768]{3,2,1,0:T(8,128)(2,1)S(1)}, u32[]{:S(2)}, u32[]{:S(2)}) collective-permute-start(bf16[2,8,96,768]{3,2,1,0:T(8,128)(2,1)} %get-tuple-element.108), channel_id=1, source_target_pairs={{0,1},{1,0},{2,3},{3,2},{4,5},{5,4},{6,7},{7,6},{8,9},{9,8},{10,11... | collective-permute-start | bytes 7077896 | tf_op jit(solution)/shard_map/ppermute | solution.py:26
  135.6 20.3 %collective-permute-start.29 = (bf16[4,120,768]{2,1,0:T(8,128)(2,1)S(1)}, bf16[4,120,768]{2,1,0:T(8,128)(2,1)S(1)}, u32[]{:S(2)}, u32[]{:S(2)}) collective-permute-start(bf16[4,120,768]{2,1,0:T(8,128)(2,1)S(1)} %get-tuple-element.116.refs_17_), channel_id=1, source_target_pairs={{0,2},{1,3},{2,0},{3,1},{4,6},{5,7},{6,4},{7,5},{8,10},{9,11},{10,... | collective-permute-start | bytes 2211848 | tf_op jit(solution)/shard_map/ppermute | solution.py:26
  136.1 19.7 %collective-permute-start.28 = (bf16[4,96,768]{2,1,0:T(8,128)(2,1)S(1)}, bf16[4,96,768]{2,1,0:T(8,128)(2,1)S(1)}, u32[]{:S(2)}, u32[]{:S(2)}) collective-permute-start(bf16[4,96,768]{2,1,0:T(8,128)(2,1)S(1)} %get-tuple-element.115.refs_6_), channel_id=1, source_target_pairs={{0,8},{4,12},{8,0},{12,4},{16,24},{20,28},{24,16},{28,20},{1,9},{5... | collective-permute-start | bytes 1769480 | tf_op jit(solution)/shard_map/ppermute | solution.py:26
  158.4 27.4 %collective-permute-start.30 = (bf16[2,3,128,768]{3,2,1,0:T(8,128)(2,1)}, bf16[2,3,128,768]{3,2,1,0:T(8,128)(2,1)}, u32[]{:S(2)}, u32[]{:S(2)}) collective-permute-start(bf16[2,3,128,768]{3,2,1,0:T(8,128)(2,1)} %gate.16), channel_id=1, source_target_pairs={{0,1},{1,0},{2,3},{3,2},{4,5},{5,4},{6,7},{7,6},{8,9},{9,8},{10,11... | collective-permute-start | bytes 3538952 | tf_op jit(solution)/shard_map/ppermute | solution.py:26
  159.5 18.5 %collective-permute-start.39 = (bf16[4,120,768]{2,1,0:T(8,128)(2,1)S(1)}, bf16[4,120,768]{2,1,0:T(8,128)(2,1)S(1)}, u32[]{:S(2)}, u32[]{:S(2)}) collective-permute-start(bf16[4,120,768]{2,1,0:T(8,128)(2,1)S(1)} %copy-done.26), channel_id=1, source_target_pairs={{0,2},{1,3},{2,0},{3,1},{4,6},{5,7},{6,4},{7,5},{8,10},{9,11},{10,... | collective-permute-start | bytes 2211848 | tf_op jit(solution)/shard_map/ppermute | solution.py:26
  161.1 24.7 %collective-permute-start.31 = (bf16[4,96,768]{2,1,0:T(8,128)(2,1)}, bf16[4,96,768]{2,1,0:T(8,128)(2,1)S(1)}, u32[]{:S(2)}, u32[]{:S(2)}) collective-permute-start(bf16[4,96,768]{2,1,0:T(8,128)(2,1)} %copy-done.28), channel_id=1, source_target_pairs={{0,8},{4,12},{8,0},{12,4},{16,24},{20,28},{24,16},{28,20},{1,9},{5... | collective-permute-start | bytes 1769480 | tf_op jit(solution)/shard_map/ppermute | solution.py:26
  161.5 18.7 %collective-permute-start.38 = (bf16[4,4,24,576]{3,2,1,0:T(8,128)(2,1)}, bf16[4,4,24,576]{3,2,1,0:T(8,128)(2,1)S(1)}, u32[]{:S(2)}, u32[]{:S(2)}) collective-permute-start(bf16[4,4,24,576]{3,2,1,0:T(8,128)(2,1)} %gate.17), channel_id=1, source_target_pairs={{0,4},{4,0},{8,12},{12,8},{16,20},{20,16},{24,28},{28,24},{1,5},{5... | collective-permute-start | bytes 1327112 | tf_op jit(solution)/shard_map/ppermute | solution.py:26
  163.0 22.4 %collective-permute-start.42 = (bf16[2,120,768]{2,1,0:T(8,128)(2,1)S(1)}, bf16[2,120,768]{2,1,0:T(8,128)(2,1)}, u32[]{:S(2)}, u32[]{:S(2)}) collective-permute-start(bf16[2,120,768]{2,1,0:T(8,128)(2,1)S(1)} %copy-done.3), channel_id=1, source_target_pairs={{0,4},{4,0},{8,12},{12,8},{16,20},{20,16},{24,28},{28,24},{1,5},{5... | collective-permute-start | bytes 1105928 | tf_op jit(solution)/shard_map/ppermute | solution.py:26
  178.1 16.6 %collective-permute-start.41 = (bf16[4,96,768]{2,1,0:T(8,128)(2,1)}, bf16[4,96,768]{2,1,0:T(8,128)(2,1)}, u32[]{:S(2)}, u32[]{:S(2)}) collective-permute-start(bf16[4,96,768]{2,1,0:T(8,128)(2,1)} %copy-done.29), channel_id=1, source_target_pairs={{0,2},{1,3},{2,0},{3,1},{4,6},{5,7},{6,4},{7,5},{8,10},{9,11},{10,... | collective-permute-start | bytes 1769480 | tf_op jit(solution)/shard_map/ppermute | solution.py:26
  181.0 24.7 %collective-permute-start.44 = (bf16[2,120,768]{2,1,0:T(8,128)(2,1)S(1)}, bf16[2,120,768]{2,1,0:T(8,128)(2,1)}, u32[]{:S(2)}, u32[]{:S(2)}) collective-permute-start(bf16[2,120,768]{2,1,0:T(8,128)(2,1)S(1)} %get-tuple-element.123.refs_2_), channel_id=1, source_target_pairs={{0,4},{4,0},{8,12},{12,8},{16,20},{20,16},{24,28},{28,24},{1,5},{5... | collective-permute-start | bytes 1105928 | tf_op jit(solution)/shard_map/ppermute | solution.py:26
  185.3 13.8 %collective-permute-start.40 = (bf16[2,4,24,576]{3,2,1,0:T(8,128)(2,1)}, bf16[2,4,24,576]{3,2,1,0:T(8,128)(2,1)S(1)}, u32[]{:S(2)}, u32[]{:S(2)}) collective-permute-start(bf16[2,4,24,576]{3,2,1,0:T(8,128)(2,1)} %get-tuple-element.134.refs_1_), channel_id=1, source_target_pairs={{0,8},{4,12},{8,0},{12,4},{16,24},{20,28},{24,16},{28,20},{1,9},{5... | collective-permute-start | bytes 663560 | tf_op jit(solution)/shard_map/ppermute | solution.py:26
  188.2 17.5 %collective-permute-start.32 = (bf16[3,128,768]{2,1,0:T(8,128)(2,1)}, bf16[3,128,768]{2,1,0:T(8,128)(2,1)}, u32[]{:S(2)}, u32[]{:S(2)}) collective-permute-start(bf16[3,128,768]{2,1,0:T(8,128)(2,1)} %get-tuple-element.126), channel_id=1, source_target_pairs={{0,2},{1,3},{2,0},{3,1},{4,6},{5,7},{6,4},{7,5},{8,10},{9,11},{10,... | collective-permute-start | bytes 1769480 | tf_op jit(solution)/shard_map/ppermute | solution.py:26
  197.7 15.3 %collective-permute-start.46 = (bf16[2,96,768]{2,1,0:T(8,128)(2,1)}, bf16[2,96,768]{2,1,0:T(8,128)(2,1)}, u32[]{:S(2)}, u32[]{:S(2)}) collective-permute-start(bf16[2,96,768]{2,1,0:T(8,128)(2,1)} %slice.103), channel_id=1, source_target_pairs={{0,4},{4,0},{8,12},{12,8},{16,20},{20,16},{24,28},{28,24},{1,5},{5... | collective-permute-start | bytes 884744 | tf_op jit(solution)/shard_map/ppermute | solution.py:26
  200.9 20.3 %collective-permute-start.43 = (bf16[2,4,24,576]{3,2,1,0:T(8,128)(2,1)S(1)}, bf16[2,4,24,576]{3,2,1,0:T(8,128)(2,1)S(1)}, u32[]{:S(2)}, u32[]{:S(2)}) collective-permute-start(bf16[2,4,24,576]{3,2,1,0:T(8,128)(2,1)S(1)} %add_convert_fusion.1.refs_0_), channel_id=1, source_target_pairs={{0,16},{4,20},{8,24},{12,28},{16,0},{20,4},{24,8},{28,12},{1,17},{... | collective-permute-start | bytes 663560 | tf_op jit(solution)/shard_map/ppermute | solution.py:26
  207.0 20.3 %collective-permute-start.53 = (bf16[2,120,768]{2,1,0:T(8,128)(2,1)S(1)}, bf16[2,120,768]{2,1,0:T(8,128)(2,1)S(1)}, u32[]{:S(2)}, u32[]{:S(2)}) collective-permute-start(bf16[2,120,768]{2,1,0:T(8,128)(2,1)S(1)} %get-tuple-element.165.refs_0_), channel_id=1, source_target_pairs={{0,16},{4,20},{8,24},{12,28},{16,0},{20,4},{24,8},{28,12},{1,17},{... | collective-permute-start | bytes 1105928 | tf_op jit(solution)/shard_map/ppermute | solution.py:26
  225.4 15.9 %collective-permute-start.55 = (bf16[2,96,768]{2,1,0:T(8,128)(2,1)S(1)}, bf16[2,96,768]{2,1,0:T(8,128)(2,1)S(1)}, u32[]{:S(2)}, u32[]{:S(2)}) collective-permute-start(bf16[2,96,768]{2,1,0:T(8,128)(2,1)S(1)} %get-tuple-element.163.refs_0_), channel_id=1, source_target_pairs={{0,16},{4,20},{8,24},{12,28},{16,0},{20,4},{24,8},{28,12},{1,17},{... | collective-permute-start | bytes 884744 | tf_op jit(solution)/shard_map/ppermute | solution.py:26
  227.5 31.1 %collective-permute-start.54 = (bf16[2,120,768]{2,1,0:T(8,128)(2,1)S(1)}, bf16[2,120,768]{2,1,0:T(8,128)(2,1)S(1)}, u32[]{:S(2)}, u32[]{:S(2)}) collective-permute-start(bf16[2,120,768]{2,1,0:T(8,128)(2,1)S(1)} %sum.4.refs_2_.refs_0_), channel_id=1, source_target_pairs={{0,8},{4,12},{8,0},{12,4},{16,24},{20,28},{24,16},{28,20},{1,9},{5... | collective-permute-start | bytes 1105928 | tf_op jit(solution)/shard_map/ppermute | solution.py:26
  228.8 12.9 %collective-permute-start.50 = (bf16[2,4,24,576]{3,2,1,0:T(8,128)(2,1)S(1)}, bf16[2,4,24,576]{3,2,1,0:T(8,128)(2,1)}, u32[]{:S(2)}, u32[]{:S(2)}) collective-permute-start(bf16[2,4,24,576]{3,2,1,0:T(8,128)(2,1)S(1)} %pad_maximum_fusion.refs_0_), channel_id=1, source_target_pairs={{0,4},{4,0},{8,12},{12,8},{16,20},{20,16},{24,28},{28,24},{1,5},{5... | collective-permute-start | bytes 663560 | tf_op jit(solution)/shard_map/ppermute | solution.py:26
  241.5 19.1 %collective-permute-start.58 = (bf16[2,96,768]{2,1,0:T(8,128)(2,1)S(1)}, bf16[2,96,768]{2,1,0:T(8,128)(2,1)S(1)}, u32[]{:S(2)}, u32[]{:S(2)}) collective-permute-start(bf16[2,96,768]{2,1,0:T(8,128)(2,1)S(1)} %sum.5.refs_1_.refs_0_), channel_id=1, source_target_pairs={{0,4},{4,0},{8,12},{12,8},{16,20},{20,16},{24,28},{28,24},{1,5},{5... | collective-permute-start | bytes 884744 | tf_op jit(solution)/shard_map/ppermute | solution.py:26
  241.7 18.6 %collective-permute-start.52 = (bf16[2,4,24,576]{3,2,1,0:T(8,128)(2,1)}, bf16[2,4,24,576]{3,2,1,0:T(8,128)(2,1)}, u32[]{:S(2)}, u32[]{:S(2)}) collective-permute-start(bf16[2,4,24,576]{3,2,1,0:T(8,128)(2,1)} %collective-permute-done.50.refs_1_), channel_id=1, source_target_pairs={{0,8},{4,12},{8,0},{12,4},{16,24},{20,28},{24,16},{28,20},{1,9},{5... | collective-permute-start | bytes 663560 | tf_op jit(solution)/shard_map/ppermute | solution.py:26
  251.0 13.5 %collective-permute-start.51 = (bf16[2,4,24,576]{3,2,1,0:T(8,128)(2,1)S(1)}, bf16[2,4,24,576]{3,2,1,0:T(8,128)(2,1)}, u32[]{:S(2)}, u32[]{:S(2)}) collective-permute-start(bf16[2,4,24,576]{3,2,1,0:T(8,128)(2,1)S(1)} %pad_maximum_fusion.refs_0_), channel_id=1, source_target_pairs={{0,8},{4,12},{8,0},{12,4},{16,24},{20,28},{24,16},{28,20},{1,9},{5... | collective-permute-start | bytes 663560 | tf_op jit(solution)/shard_map/ppermute | solution.py:26
  256.8 20.0 %collective-permute-start.56 = (bf16[2,120,768]{2,1,0:T(8,128)(2,1)S(1)}, bf16[2,120,768]{2,1,0:T(8,128)(2,1)}, u32[]{:S(2)}, u32[]{:S(2)}) collective-permute-start(bf16[2,120,768]{2,1,0:T(8,128)(2,1)S(1)} %sum.4.refs_2_.refs_0_), channel_id=1, source_target_pairs={{0,4},{4,0},{8,12},{12,8},{16,20},{20,16},{24,28},{28,24},{1,5},{5... | collective-permute-start | bytes 1105928 | tf_op jit(solution)/shard_map/ppermute | solution.py:26
  259.3 17.5 %collective-permute-start.57 = (bf16[2,120,768]{2,1,0:T(8,128)(2,1)}, bf16[2,120,768]{2,1,0:T(8,128)(2,1)S(1)}, u32[]{:S(2)}, u32[]{:S(2)}) collective-permute-start(bf16[2,120,768]{2,1,0:T(8,128)(2,1)} %gate.22.refs_1_), channel_id=1, source_target_pairs={{0,4},{4,0},{8,12},{12,8},{16,20},{20,16},{24,28},{28,24},{1,5},{5... | collective-permute-start | bytes 1105928 | tf_op jit(solution)/shard_map/ppermute | solution.py:26
  (109 other events, 804.8 us)
